TPU v7x, 32 devices: a whole 2x2x4 slice. The times are simulated.
32 devices in a mesh: gx: 8 (over y, x, core), gz: 4 (over z).
Axes of the slice: x: 2, y: 2, z: 4, core: 2. Of those that a mesh axis runs over, the one named last changes fastest.
Arguments:
- field: bfloat16 [512, 16, 512], P('gx', None, 'gz'), may hold values from -6 to 6
- even_vectors: bfloat16 [256, 256], P('gx', 'gz'), may hold values from -0.375 to 0.375
- odd_vectors: bfloat16 [256, 256], P('gx', 'gz'), may hold values from -0.375 to 0.375
Outputs:
- even_modes: float32 [256, 16, 512], P('gx', None, 'gz')
- odd_modes: float32 [256, 16, 512], P('gx', None, 'gz')
All inputs are finite; a program needn't handle non-finite values.
Results may differ from a plain program's by a relative error of at most 0.0031.
Values may be sent and summed in bfloat16 or wider, within the bound.
No kernel may reach another device: no remote copies, remote signals or barrier semaphores. Data moves between devices by JAX's collectives and lax.ppermute only.
A program may use at most 64 MiB of HBM per device.

v0:
```python
import jax
import jax.numpy as jnp
from jax import lax
from jax.sharding import PartitionSpec as P


def local(field, even_vectors, odd_vectors):
    count = lax.axis_size("gx")
    width = field.shape[0]
    half_rows = width // 2
    planes = field.shape[1]
    depth = field.shape[2]
    order = count * half_rows
    even_block, odd_block = (
        lax.all_gather(even_vectors, "gz", axis=1, tiled=True),
        lax.all_gather(odd_vectors, "gz", axis=1, tiled=True),
    )
    flat = field.reshape(width, planes * depth)
    lines = lax.all_to_all(flat, "gx", split_axis=1, concat_axis=0, tiled=True)
    lower = lines[:order].astype(jnp.float32)
    upper = lines[order:][::-1].astype(jnp.float32)
    both_parts = jnp.stack(
        ((lower + upper).astype(jnp.bfloat16), (lower - upper).astype(jnp.bfloat16))
    )
    stacked = jnp.stack((even_block, odd_block))
    all_modes = jnp.einsum(
        "prj,pjc->prc",
        lax.all_gather(stacked, "gx", axis=1, tiled=True),
        both_parts,
        preferred_element_type=jnp.float32,
    )
    returned = lax.all_to_all(all_modes, "gx", split_axis=1, concat_axis=2, tiled=True)
    even_modes = returned[0]
    odd_modes = returned[1]
    return (
        even_modes.reshape(even_block.shape[0], planes, depth),
        odd_modes.reshape(odd_block.shape[0], planes, depth),
    )


def solution(mesh):
    placed = (P("gx", None, "gz"), P("gx", "gz"), P("gx", "gz"))
    return jax.shard_map(
        local,
        mesh=mesh,
        in_specs=placed,
        out_specs=(P("gx", None, "gz"), P("gx", None, "gz")),
        check_vma=False,
    )
```

profile of v0, /device:TPU:0, one launch (start us, length us, event | category | flops | bytes accessed | tf_op | source)
XLA Modules:
  0.0 60.4 jit_solution(8286460301267492028)
XLA Ops:
  0.6 1.0 %all_to_all.23 = bf16[64,8,256]{2,1,0:T(8,128)(2,1)S(1)} reshape(bf16[64,16,128]{2,1,0:T(8,128)(2,1)} %param.3) | data formatting | bytes 524288 | tf_op jit(solution)/shard_map/all_to_all | solution.py:19
  1.7 0.8 %copy.12 = bf16[64,8,256]{2,0,1:T(8,128)(2,1)} copy(bf16[64,8,256]{2,1,0:T(8,128)(2,1)S(1)} %all_to_all.23) | data formatting | bytes 524288 | tf_op jit(solution)/shard_map/all_to_all | solution.py:19
  2.4 0.0 copy-start
  2.4 5.3 %all-to-all-start = ((bf16[64,8,256]{2,0,1:T(8,128)(2,1)}), bf16[64,8,256]{2,0,1:T(8,128)(2,1)S(1)}, u32[]{:S(2)}, u32[]{:S(2)}) async-start(bf16[64,8,256]{2,0,1:T(8,128)(2,1)} %copy.12), calls=%async_computation | async-start | bytes 524288 | tf_op jit(solution)/shard_map/all_to_all | solution.py:19
  7.7 0.0 copy-done
  7.7 13.4 %all-gather = bf16[4,64,32]{1,2,0:T(8,128)(2,1)S(1)} all-gather(bf16[1,64,32]{1,2,0:T(8,128)(2,1)S(1)} %bitcast.39), channel_id=1, replica_groups=mesh['gx'=8,'gz'=4] {'gz'}, dimensions={0}, use_global_device_ids=true | all-gather | bytes 20480 | tf_op jit(solution)/shard_map/all_gather | solution.py:15
  21.1 0.0 copy-start.1
  21.1 0.1 reshape.19
  21.2 0.6 copy-done.1
  21.8 13.1 %all-gather.1 = bf16[4,64,32]{1,2,0:T(8,128)(2,1)S(1)} all-gather(bf16[1,64,32]{1,2,0:T(8,128)(2,1)S(1)} %bitcast.40), channel_id=1, replica_groups=mesh['gx'=8,'gz'=4] {'gz'}, dimensions={0}, use_global_device_ids=true | all-gather | bytes 20480 | tf_op jit(solution)/shard_map/all_gather | solution.py:16
  35.0 0.1 reshape.21
  35.1 9.8 %all_gather.11 = bf16[2,256,256]{2,1,0:T(8,128)(2,1)S(1)} all-gather(bf16[2,32,256]{2,1,0:T(8,128)(2,1)S(1)} %pad_maximum_fusion), channel_id=1, replica_groups=mesh['gx'=8,'gz'=4] {'gx'}, dimensions={1}, use_global_device_ids=true | all-gather | bytes 294912 | tf_op jit(solution)/shard_map/all_gather | solution.py:28
  44.9 0.0 all-to-all-done
  44.9 0.2 rev.3
  45.1 0.1 fusion.7
  45.2 0.2 fusion.2
  45.4 0.4 copy.13
  45.8 12.3 %all_to_all.31 = f32[2,256,256]{2,0,1:T(2,128)S(1)} all-to-all(f32[2,256,256]{2,0,1:T(2,128)S(1)} %copy.13), channel_id=1, replica_groups=mesh['gx'=8,'gz'=4] {'gx'}, dimensions={1} | all-to-all | bytes 1048576 | tf_op jit(solution)/shard_map/all_to_all | solution.py:32
  58.1 0.5 fusion.9
  58.6 0.2 copy.15
  58.8 0.7 %reshape_squeeze.7 = f32[32,16,128]{2,1,0:T(8,128)} reshape(f32[1,32,8,256]{3,2,1,0:T(8,128)S(1)} %copy.15) | data formatting | bytes 524288 | tf_op jit(solution)/shard_map/reshape;squeeze | solution.py:37
  59.5 0.2 copy.14
  59.6 0.7 %reshape_squeeze.6 = f32[32,16,128]{2,1,0:T(8,128)} reshape(f32[1,32,8,256]{3,2,1,0:T(8,128)S(1)} %copy.14) | data formatting | bytes 524288 | tf_op jit(solution)/shard_map/reshape;squeeze | solution.py:36
  (4 shorter events, 0.1 us)
Async XLA Ops:
  2.4 5.3 %copy-start = (bf16[32,64]{1,0:T(8,128)(2,1)S(1)}, bf16[32,64]{1,0:T(8,128)(2,1)}, u32[]{:S(2)}) copy-start(bf16[32,64]{1,0:T(8,128)(2,1)} %param.4) | copy-start | bytes 12292
  2.4 42.4 %all-to-all-start = ((bf16[64,8,256]{2,0,1:T(8,128)(2,1)}), bf16[64,8,256]{2,0,1:T(8,128)(2,1)S(1)}, u32[]{:S(2)}, u32[]{:S(2)}) async-start(bf16[64,8,256]{2,0,1:T(8,128)(2,1)} %copy.12), calls=%async_computation | async-start | bytes 524288 | tf_op jit(solution)/shard_map/all_to_all | solution.py:19
  21.1 0.7 %copy-start.1 = (bf16[32,64]{1,0:T(8,128)(2,1)S(1)}, bf16[32,64]{1,0:T(8,128)(2,1)}, u32[]{:S(2)}) copy-start(bf16[32,64]{1,0:T(8,128)(2,1)} %param.5) | copy-start | bytes 12292
where the time goes:
time: 60.8 us; the launch traced here: 60.4 us
  blocking collectives  48.6 us (80%)
  local copies, waits for them, and re-layouts  5.49 us (9%)
  starting transfers between devices  5.3 us (9%)
  between operations  0.7 us (1%)
    all_gather x1, blocking collectives, local(): lax.all_gather(even_vectors, 'gz', axis=1, tiled=True)  13.4 us
    all_gather x1, blocking collectives, local(): lax.all_gather(odd_vectors, 'gz', axis=1, tiled=True)  13.1 us
    all_to_all x1, blocking collectives, local(): lax.all_to_all(all_modes, 'gx', split_axis=1, concat_axis=2, tiled=True)  12.3 us
    all_gather x1, blocking collectives, local(): lax.all_gather(stacked, 'gx', axis=1, tiled=True)  9.8 us
    all_to_all x1, starting transfers between devices, local(): lines = lax.all_to_all(flat, 'gx', split_axis=1, concat_axis=0, tiled=True)  5.3 us
    all_to_all x2, local copies, waits for them, and re-layouts, local(): lines = lax.all_to_all(flat, 'gx', split_axis=1, concat_axis=0, tiled=True)  1.79 us
  transfers between devices with their start and end apart: 1, of which 0 were waited for; matrix products, arithmetic and copies ran while one was open for 0% of the time, Pallas kernels for 0%

commit v1 on v0

v1 whole, which is shorter than its diff:
```python
import functools

import jax
import jax.numpy as jnp
from jax import lax
from jax.experimental import pallas as pl
from jax.experimental.pallas import tpu as pltpu
from jax.sharding import PartitionSpec as P


def pair_sums(first, second, upper, even_lines, odd_lines, rows, planes, depth, at):
    def spread(even_ref, odd_ref):
        for j in range(rows):
            here = pl.ds(j * planes, planes)
            there = pl.ds((rows - 1 - j) * planes, planes)
            low = jnp.where(upper, second[here, :], first[here, :]).astype(jnp.float32)
            high = jnp.where(upper, first[there, :], second[there, :]).astype(
                jnp.float32
            )
            even_ref[here, :] = low + high
            odd_ref[here, :] = low - high
        for y in range(planes):
            line = pl.ds(y, rows, stride=planes)
            columns = pl.ds(y * depth, depth)
            even_lines[at, columns] = even_ref[line, :].astype(jnp.bfloat16)
            odd_lines[at, columns] = odd_ref[line, :].astype(jnp.bfloat16)

    pl.run_scoped(
        spread,
        pltpu.VMEM((rows * planes, depth), jnp.float32),
        pltpu.VMEM((rows * planes, depth), jnp.float32),
    )


def transform_kernel(pairs, rows, planes, depth, has_sum, places, vectors, *refs):
    blocks = refs[: 2 * pairs]
    refs = refs[2 * pairs :]
    if has_sum:
        sum_own, sum_other = refs[:2]
        refs = refs[2:]
    own, other, even_lines, odd_lines = refs
    core = places[0]
    for p in range(pairs):
        pair_sums(
            blocks[2 * p],
            blocks[2 * p + 1],
            places[1 + 2 * p] > 0,
            even_lines,
            odd_lines,
            rows,
            planes,
            depth,
            pl.ds(p * rows, rows),
        )
    for result, before, which in (
        (own, sum_own if has_sum else None, core),
        (other, sum_other if has_sum else None, 1 - core),
    ):
        for parity, lines in enumerate((even_lines, odd_lines)):
            total = before[parity] if has_sum else None
            for p in range(pairs):
                block = vectors[places[2 + 2 * p], which, parity]
                part = jnp.dot(
                    block,
                    lines[pl.ds(p * rows, rows), :],
                    preferred_element_type=jnp.float32,
                )
                total = part if total is None else total + part
            result[parity] = total


def transform(places, vectors, blocks, sums, planes):
    pairs = len(blocks) // 2
    lines, depth = blocks[0].shape
    rows = lines // planes
    modes = vectors.shape[3]
    shape = jax.ShapeDtypeStruct((2, modes, planes * depth), jnp.float32)
    vmem = pl.BlockSpec(memory_space=pltpu.VMEM)
    return pl.pallas_call(
        functools.partial(
            transform_kernel, pairs, rows, planes, depth, bool(sums)
        ),
        out_shape=(shape, shape),
        in_specs=[pl.BlockSpec(memory_space=pltpu.SMEM)]
        + [vmem] * (1 + len(blocks) + len(sums)),
        out_specs=(vmem, vmem),
        scratch_shapes=[
            pltpu.VMEM((pairs * rows, planes * depth), jnp.bfloat16),
            pltpu.VMEM((pairs * rows, planes * depth), jnp.bfloat16),
        ],
        compiler_params=pltpu.CompilerParams(vmem_limit_bytes=48 * 1024 * 1024),
        name="transform",
    )(places, vectors, *blocks, *sums)


def finish_kernel(planes, depth, own, received, even_out, odd_out):
    modes = own.shape[1]
    for parity, out in enumerate((even_out, odd_out)):
        for y in range(planes):
            columns = pl.ds(y * depth, depth)
            out[pl.ds(y, modes, stride=planes), :] = (
                own[parity, :, columns] + received[parity, :, columns]
            )


def finish(own, received, planes, depth):
    modes = own.shape[1]
    shape = jax.ShapeDtypeStruct((modes * planes, depth), jnp.float32)
    vmem = pl.BlockSpec(memory_space=pltpu.VMEM)
    return pl.pallas_call(
        functools.partial(finish_kernel, planes, depth),
        out_shape=(shape, shape),
        in_specs=[vmem, vmem],
        out_specs=(vmem, vmem),
        compiler_params=pltpu.CompilerParams(vmem_limit_bytes=48 * 1024 * 1024),
        name="finish",
    )(own, received)


def local(field, even_vectors, odd_vectors):
    count = lax.axis_size("gx")
    slices = lax.axis_size("gz")
    me = lax.axis_index("gx")
    z = lax.axis_index("gz")
    rows, planes, depth = field.shape
    modes = even_vectors.shape[0]
    top = count // 2
    masks = [1 << b for b in range(1, count.bit_length() - 2)] + [top | 1]

    def in_first(g):
        return (g & 1) == (g // top)

    def swap(value, mask):
        return lax.ppermute(value, "gx", [(g, g ^ mask) for g in range(count)])

    def swap_two(value, first, second):
        return lax.ppermute(
            value,
            "gx",
            [(g, g ^ (first if in_first(g) else second)) for g in range(count)],
        )

    held = [field]
    for a, b in zip(masks, reversed(masks)):
        held = held + [swap_two(block, a, b) for block in held]
    packed = jnp.stack((even_vectors, odd_vectors))[None]
    step = 1
    while step < slices:
        moved = lax.ppermute(packed, "gz", [(i, i ^ step) for i in range(slices)])
        packed = jnp.concatenate((packed, moved))
        step *= 2
    partner = swap(packed, 1)
    core = me & 1
    vectors = jnp.where(
        core == 0, jnp.stack((packed, partner), 1), jnp.stack((partner, packed), 1)
    )

    flat = [block.reshape(rows * planes, depth) for block in held]
    first_set = (me & 1) == (me // top)

    def places(ks):
        out = [core]
        for k in ks:
            first = second = 0
            for s, (a, b) in enumerate(zip(masks, reversed(masks))):
                if k >> s & 1:
                    first, second = first ^ a, second ^ b
            at = me ^ jnp.where(first_set, first, second)
            upper = at >= top
            block = jnp.where(upper, count - 1 - at, at)
            out += [upper.astype(jnp.int32), z ^ block]
        return jnp.stack(out).astype(jnp.int32)

    last = len(held) - 1
    early = range(1, len(held) // 2)
    sums = transform(
        places(early),
        vectors,
        [flat[i] for k in early for i in (k, last - k)],
        (),
        planes,
    )
    own, other = transform(places([0]), vectors, [flat[0], flat[last]], sums, planes)
    received = swap(other, 1)
    even, odd = finish(own, received, planes, depth)
    return even.reshape(modes, planes, depth), odd.reshape(modes, planes, depth)


def solution(mesh):
    placed = (P("gx", None, "gz"), P("gx", "gz"), P("gx", "gz"))
    return jax.shard_map(
        local,
        mesh=mesh,
        in_specs=placed,
        out_specs=(P("gx", None, "gz"), P("gx", None, "gz")),
        check_vma=False,
    )
```

time: 60.8 us -> 21.3 us (0.35)
  blocking collectives: 48.6 us -> 0 us
  waiting for transfers between devices: 0.01 us -> 7.88 us
  local copies, waits for them, and re-layouts: 5.49 us -> 0.01 us
  Pallas kernels: 0 us -> 3.63 us
  starting transfers between devices: 5.3 us -> 7.85 us
  other arithmetic: 0.07 us -> 0.95 us
    all_gather x3 -> x0, blocking collectives: 36.3 us -> none  [the longest x1 13.4 us: local(): lax.all_gather(even_vectors, 'gz', axis=1, tiled=True)]
    all_to_all x1 -> x0, blocking collectives: 12.3 us -> none  [local(): lax.all_to_all(all_modes, 'gx', split_axis=1, concat_axis=2, tiled=True)]
    ppermute x0 -> x7, waiting for transfers between devices: none -> 7.88 us  [the longest x2 3.88 us: local(): moved = lax.ppermute(packed, 'gz', [(i, i ^ step) for i in range(slices)])]
    ppermute x0 -> x7, starting transfers between devices: none -> 7.85 us  [the longest x2 4.28 us: local(): moved = lax.ppermute(packed, 'gz', [(i, i ^ step) for i in range(slices)])]
    all_to_all x1 -> x0, starting transfers between devices: 5.3 us -> none  [local(): lines = lax.all_to_all(flat, 'gx', split_axis=1, concat_axis=0, tiled=True)]
    pallas_call x0 -> x3, Pallas kernels: none -> 3.63 us  [the longest x2 2.62 us: transform(): pl.pallas_call(functools.partial(transform_kernel, pairs, rows, planes, d...]
    all_to_all x2 -> x0, local copies, waits for them, and re-layouts: 1.79 us -> none  [local(): lines = lax.all_to_all(flat, 'gx', split_axis=1, concat_axis=0, tiled=True)]
    another operation x2 -> x0, local copies, waits for them, and re-layouts: 1.44 us -> none  [the longest x1 0.72 us: local(): odd_modes.reshape(odd_block.shape[0], planes, depth)]
  transfers between devices with their start and end apart: 1 -> 7, of which waited for: 0 -> 5; matrix products, arithmetic and copies ran while one was open for 0% -> 5% of each run, Pallas kernels for 0% -> 6%
where the time goes in v1:
time: 21.3 us; the launch traced here: 21 us
  waiting for transfers between devices  7.88 us (37%)
  starting transfers between devices  7.85 us (37%)
  Pallas kernels  3.63 us (17%)
  other arithmetic  0.95 us (4%)
  between operations  0.7 us (3%)
    ppermute x2, starting transfers between devices, local(): moved = lax.ppermute(packed, 'gz', [(i, i ^ step) for i in range(slices)])  4.28 us
    ppermute x2, waiting for transfers between devices, local(): moved = lax.ppermute(packed, 'gz', [(i, i ^ step) for i in range(slices)])  3.88 us
    ppermute x3, starting transfers between devices, swap_two(): lax.ppermute(value, 'gx', [(g, g ^ (first if in_first(g) else second)) fo...  3.43 us
    ppermute x2, waiting for transfers between devices, swap(): return lax.ppermute(value, 'gx', [(g, g ^ mask) for g in range(count)])  3.06 us
    pallas_call x2, Pallas kernels, transform(): pl.pallas_call(functools.partial(transform_kernel, pairs, rows, planes, d...  2.62 us
    pallas_call x1, Pallas kernels, finish(): pl.pallas_call(functools.partial(finish_kernel, planes, depth), out_shape...  1.01 us
    ppermute x3, waiting for transfers between devices, swap_two(): lax.ppermute(value, 'gx', [(g, g ^ (first if in_first(g) else second)) fo...  0.94 us
    broadcast_in_dim x1, other arithmetic, local(): packed = jnp.stack((even_vectors, odd_vectors))[None]  0.72 us
  transfers between devices with their start and end apart: 7, of which 5 were waited for; matrix products, arithmetic and copies ran while one was open for 5% of the time, Pallas kernels for 6%

profile of v1, /device:TPU:0, one launch (start us, length us, event | category | flops | bytes accessed | tf_op | source)
XLA Modules:
  0.0 21.0 jit_solution(11695757834019749010)
XLA Ops:
  0.6 3.0 %collective-permute-start.3 = (bf16[64,16,128]{2,1,0:T(8,128)(2,1)}, bf16[64,16,128]{2,1,0:T(8,128)(2,1)S(1)}, u32[]{:S(2)}, u32[]{:S(2)}) collective-permute-start(bf16[64,16,128]{2,1,0:T(8,128)(2,1)} %param.3), channel_id=1, source_target_pairs={{0,8},{4,16},{8,0},{12,24},{16,4},{20,28},{24,12},{28,20},{1,9},{5... | collective-permute-start | bytes 786440 | tf_op jit(solution)/shard_map/ppermute | solution.py:137
  3.6 0.7 %maximum_bitcast_fusion = bf16[1,2,32,64]{3,2,1,0:T(8,128)(2,1)S(1)} fusion(bf16[1,32,64]{2,1,0:T(8,128)(2,1)} %bitcast.23, bf16[1,32,64]{2,1,0:T(8,128)(2,1)} %bitcast.24), kind=kLoop, calls=%fused_computation.3 | loop fusion | flops 4096 | bytes 16384 | tf_op jit(solution)/shard_map/broadcast_in_dim | solution.py:146
  4.4 1.6 %collective-permute-start = (bf16[1,2,32,64]{3,2,1,0:T(8,128)(2,1)S(1)}, bf16[1,2,32,64]{3,2,1,0:T(8,128)(2,1)S(1)}, u32[]{:S(2)}, u32[]{:S(2)}) collective-permute-start(bf16[1,2,32,64]{3,2,1,0:T(8,128)(2,1)S(1)} %maximum_bitcast_fusion), channel_id=1, source_target_pairs={{0,1},{1,0},{2,3},{3,2},{4,5},{5,4},{6,7},{7,6},{8,9},{9,8},{10,11... | collective-permute-start | bytes 24584 | tf_op jit(solution)/shard_map/ppermute | solution.py:149
  6.0 0.4 %collective-permute-start.5 = (bf16[64,16,128]{2,1,0:T(8,128)(2,1)}, bf16[64,16,128]{2,1,0:T(8,128)(2,1)S(1)}, u32[]{:S(2)}, u32[]{:S(2)}) collective-permute-start(bf16[64,16,128]{2,1,0:T(8,128)(2,1)} %param.3), channel_id=1, source_target_pairs={{0,20},{4,12},{8,28},{12,4},{16,24},{20,0},{24,16},{28,8},{1,21},{... | collective-permute-start | bytes 786440 | tf_op jit(solution)/shard_map/ppermute | solution.py:137
  6.4 1.8 %collective-permute-done = bf16[1,2,32,64]{3,2,1,0:T(8,128)(2,1)S(1)} collective-permute-done((bf16[1,2,32,64]{3,2,1,0:T(8,128)(2,1)S(1)}, bf16[1,2,32,64]{3,2,1,0:T(8,128)(2,1)S(1)}, u32[]{:S(2)}, u32[]{:S(2)}) %collective-permute-start) | collective-permute-done | bytes 8224 | tf_op jit(solution)/shard_map/ppermute | solution.py:149
  8.2 2.7 %collective-permute-start.1 = (bf16[2,2,32,64]{3,2,1,0:T(8,128)(2,1)S(1)}, bf16[2,2,32,64]{3,2,1,0:T(8,128)(2,1)S(1)}, u32[]{:S(2)}, u32[]{:S(2)}) collective-permute-start(bf16[2,2,32,64]{3,2,1,0:T(8,128)(2,1)S(1)} %pad_maximum_fusion.1), channel_id=1, source_target_pairs={{0,2},{1,3},{2,0},{3,1},{4,6},{5,7},{6,4},{7,5},{8,10},{9,11},{10,... | collective-permute-start | bytes 49160 | tf_op jit(solution)/shard_map/ppermute | solution.py:149
  10.8 0.1 pad_add_fusion.1.places
  10.9 0.0 collective-permute-done.3
  10.9 0.0 collective-permute-start.4
  10.9 2.1 %collective-permute-done.1 = bf16[2,2,32,64]{3,2,1,0:T(8,128)(2,1)S(1)} collective-permute-done((bf16[2,2,32,64]{3,2,1,0:T(8,128)(2,1)S(1)}, bf16[2,2,32,64]{3,2,1,0:T(8,128)(2,1)S(1)}, u32[]{:S(2)}, u32[]{:S(2)}) %collective-permute-start.1) | collective-permute-done | bytes 16416 | tf_op jit(solution)/shard_map/ppermute | solution.py:149
  13.1 0.1 collective-permute-start.2
  13.1 0.1 pad_add_fusion.places
  13.2 1.2 %collective-permute-done.2 = bf16[4,2,32,64]{3,2,1,0:T(8,128)(2,1)S(1)} collective-permute-done((bf16[4,2,32,64]{3,2,1,0:T(8,128)(2,1)S(1)}, bf16[4,2,32,64]{3,2,1,0:T(8,128)(2,1)S(1)}, u32[]{:S(2)}, u32[]{:S(2)}) %collective-permute-start.2) | collective-permute-done | bytes 32800 | tf_op jit(solution)/shard_map/ppermute | solution.py:134
  14.4 0.0 collective-permute-done.5
  14.4 0.0 copy-start
  14.5 1.3 %transform.2 = (f32[2,32,2048]{2,1,0:T(8,128)S(1)}, f32[2,32,2048]{2,1,0:T(8,128)S(1)}) custom-call(s32[3]{0:T(128)S(1)} %pad_add_fusion.1.places, bf16[4,2,2,32,64]{4,3,2,1,0:T(8,128)(2,1)S(1)} %maximum_select_fusion.vectors, bf16[1024,128]{1,0:T(8,128)(2,1)S(1)} %bitcast.20, bf16[1024,128]{1,0:T(8,128)(2,1)S(1)} %bitcast.21), custom_call_target="tpu_custom_call" | custom-call | tf_op jit(solution)/shard_map/transform/pallas_call | solution.py:79
  15.8 0.9 %collective-permute-done.4 = bf16[64,16,128]{2,1,0:T(8,128)(2,1)S(1)} collective-permute-done((bf16[64,16,128]{2,1,0:T(8,128)(2,1)S(1)}, bf16[64,16,128]{2,1,0:T(8,128)(2,1)S(1)}, u32[]{:S(2)}, u32[]{:S(2)}) %collective-permute-start.4) | collective-permute-done | bytes 262176 | tf_op jit(solution)/shard_map/ppermute | solution.py:137
  16.7 0.0 copy-done
  16.7 1.3 %transform.3 = (f32[2,32,2048]{2,1,0:T(8,128)S(1)}, f32[2,32,2048]{2,1,0:T(8,128)S(1)}) custom-call(s32[3]{0:T(128)S(1)} %pad_add_fusion.places, bf16[4,2,2,32,64]{4,3,2,1,0:T(8,128)(2,1)S(1)} %maximum_select_fusion.vectors, bf16[1024,128]{1,0:T(8,128)(2,1)S(1)} %bitcast.18, bf16[1024,128]{1,0:T(8,128)(2,1)S(1)} %bitcast.19, ...), custom_call_target="tpu_custom_call" | custom-call | tf_op jit(solution)/shard_map/transform/pallas_call | solution.py:79
  18.0 0.1 collective-permute-start.6
  18.1 1.9 %collective-permute-done.6.received = f32[2,32,2048]{2,1,0:T(8,128)S(1)} collective-permute-done((f32[2,32,2048]{2,1,0:T(8,128)S(1)}, f32[2,32,2048]{2,1,0:T(8,128)S(1)}, u32[]{:S(2)}, u32[]{:S(2)}) %collective-permute-start.6) | collective-permute-done | bytes 524320 | tf_op jit(solution)/shard_map/ppermute | solution.py:134
  20.0 1.0 %finish.1 = (f32[512,128]{1,0:T(8,128)}, f32[512,128]{1,0:T(8,128)}) custom-call(f32[2,32,2048]{2,1,0:T(8,128)S(1)} %get-tuple-element.10.own, f32[2,32,2048]{2,1,0:T(8,128)S(1)} %collective-permute-done.6.received), custom_call_target="tpu_custom_call" | custom-call | tf_op jit(solution)/shard_map/finish/pallas_call | solution.py:110
  (3 shorter events, 0.1 us)
Async XLA Ops:
  0.6 10.3 %collective-permute-start.3 = (bf16[64,16,128]{2,1,0:T(8,128)(2,1)}, bf16[64,16,128]{2,1,0:T(8,128)(2,1)S(1)}, u32[]{:S(2)}, u32[]{:S(2)}) collective-permute-start(bf16[64,16,128]{2,1,0:T(8,128)(2,1)} %param.3), channel_id=1, source_target_pairs={{0,8},{4,16},{8,0},{12,24},{16,4},{20,28},{24,12},{28,20},{1,9},{5... | collective-permute-start | bytes 786440 | tf_op jit(solution)/shard_map/ppermute | solution.py:137
  4.4 3.8 %collective-permute-start = (bf16[1,2,32,64]{3,2,1,0:T(8,128)(2,1)S(1)}, bf16[1,2,32,64]{3,2,1,0:T(8,128)(2,1)S(1)}, u32[]{:S(2)}, u32[]{:S(2)}) collective-permute-start(bf16[1,2,32,64]{3,2,1,0:T(8,128)(2,1)S(1)} %maximum_bitcast_fusion), channel_id=1, source_target_pairs={{0,1},{1,0},{2,3},{3,2},{4,5},{5,4},{6,7},{7,6},{8,9},{9,8},{10,11... | collective-permute-start | bytes 24584 | tf_op jit(solution)/shard_map/ppermute | solution.py:149
  6.0 8.4 %collective-permute-start.5 = (bf16[64,16,128]{2,1,0:T(8,128)(2,1)}, bf16[64,16,128]{2,1,0:T(8,128)(2,1)S(1)}, u32[]{:S(2)}, u32[]{:S(2)}) collective-permute-start(bf16[64,16,128]{2,1,0:T(8,128)(2,1)} %param.3), channel_id=1, source_target_pairs={{0,20},{4,12},{8,28},{12,4},{16,24},{20,0},{24,16},{28,8},{1,21},{... | collective-permute-start | bytes 786440 | tf_op jit(solution)/shard_map/ppermute | solution.py:137
  8.2 4.9 %collective-permute-start.1 = (bf16[2,2,32,64]{3,2,1,0:T(8,128)(2,1)S(1)}, bf16[2,2,32,64]{3,2,1,0:T(8,128)(2,1)S(1)}, u32[]{:S(2)}, u32[]{:S(2)}) collective-permute-start(bf16[2,2,32,64]{3,2,1,0:T(8,128)(2,1)S(1)} %pad_maximum_fusion.1), channel_id=1, source_target_pairs={{0,2},{1,3},{2,0},{3,1},{4,6},{5,7},{6,4},{7,5},{8,10},{9,11},{10,... | collective-permute-start | bytes 49160 | tf_op jit(solution)/shard_map/ppermute | solution.py:149
  10.9 5.8 %collective-permute-start.4 = (bf16[64,16,128]{2,1,0:T(8,128)(2,1)S(1)}, bf16[64,16,128]{2,1,0:T(8,128)(2,1)S(1)}, u32[]{:S(2)}, u32[]{:S(2)}) collective-permute-start(bf16[64,16,128]{2,1,0:T(8,128)(2,1)S(1)} %collective-permute-done.3), channel_id=1, source_target_pairs={{0,20},{4,12},{8,28},{12,4},{16,24},{20,0},{24,16},{28,8},{1,21},{... | collective-permute-start | bytes 786440 | tf_op jit(solution)/shard_map/ppermute | solution.py:137
  13.1 1.3 %collective-permute-start.2 = (bf16[4,2,32,64]{3,2,1,0:T(8,128)(2,1)S(1)}, bf16[4,2,32,64]{3,2,1,0:T(8,128)(2,1)S(1)}, u32[]{:S(2)}, u32[]{:S(2)}) collective-permute-start(bf16[4,2,32,64]{3,2,1,0:T(8,128)(2,1)S(1)} %get-tuple-element.15), channel_id=1, source_target_pairs={{0,4},{4,0},{8,12},{12,8},{16,20},{20,16},{24,28},{28,24},{1,5},{5... | collective-permute-start | bytes 98312 | tf_op jit(solution)/shard_map/ppermute | solution.py:134
  14.4 2.3 %copy-start = (bf16[64,16,128]{2,1,0:T(8,128)(2,1)S(1)}, bf16[64,16,128]{2,1,0:T(8,128)(2,1)}, u32[]{:S(2)}) copy-start(bf16[64,16,128]{2,1,0:T(8,128)(2,1)} %param.3) | copy-start | bytes 786436
  18.0 2.0 %collective-permute-start.6 = (f32[2,32,2048]{2,1,0:T(8,128)S(1)}, f32[2,32,2048]{2,1,0:T(8,128)S(1)}, u32[]{:S(2)}, u32[]{:S(2)}) collective-permute-start(f32[2,32,2048]{2,1,0:T(8,128)S(1)} %get-tuple-element.11), channel_id=1, source_target_pairs={{0,4},{4,0},{8,12},{12,8},{16,20},{20,16},{24,28},{28,24},{1,5},{5... | collective-permute-start | bytes 1572872 | tf_op jit(solution)/shard_map/ppermute | solution.py:134

commit v2 on v0

v2 whole, which is shorter than its diff:
```python
import functools

import jax
import jax.numpy as jnp
from jax import lax
from jax.experimental import pallas as pl
from jax.experimental.pallas import tpu as pltpu
from jax.sharding import PartitionSpec as P

PARAMS = pltpu.CompilerParams(vmem_limit_bytes=48 * 1024 * 1024)
CHUNK = 16


class Block:
    def __init__(self, value, even, odd):
        self.value, self.even, self.odd = value, even, odd

    def place(self, count):
        me = lax.axis_index("gx")
        at = me ^ jnp.where((me & 1) == 0, self.even, self.odd)
        upper = (at >= count // 2).astype(jnp.int32)
        block = jnp.where(upper == 1, count - 1 - at, at)
        return upper, lax.axis_index("gz") ^ block


def send(block, even, odd, count):
    pairs = [(g, g ^ (odd if g & 1 else even)) for g in range(count)]
    if even & 1:
        offsets = odd ^ block.odd, even ^ block.even
    else:
        offsets = even ^ block.even, odd ^ block.odd
    return Block(lax.ppermute(block.value, "gx", pairs), *offsets)


def parity_lines(first, second, upper, planes, even, odd, start):
    lines, depth = first.shape
    rows = lines // planes

    def spread(low, high):
        for j in range(0, rows, CHUNK):
            evens, odds = [], []
            for i in range(j, j + CHUNK):
                a = low[pl.ds(i * planes, planes), :].astype(jnp.float32)
                b = high[pl.ds((rows - 1 - i) * planes, planes), :].astype(jnp.float32)
                evens.append((a + b).astype(jnp.bfloat16))
                odds.append((a - b).astype(jnp.bfloat16))
            for part, ref in ((evens, even), (odds, odd)):
                part = jnp.swapaxes(jnp.stack(part), 0, 1)
                for y in range(planes):
                    ref[pl.ds(start + j, CHUNK), pl.ds(y * depth, depth)] = part[y]

    @pl.when(upper == 0)
    def _():
        spread(first, second)

    @pl.when(upper != 0)
    def _():
        spread(second, first)


def prepare_kernel(place, planes, first, second, even, odd):
    parity_lines(first, second, place()[0], planes, even, odd, 0)


def prepare(pair, count, planes):
    lines, depth = pair[0].value.shape
    shape = jax.ShapeDtypeStruct((lines // planes, planes * depth), jnp.bfloat16)
    vmem = pl.BlockSpec(memory_space=pltpu.VMEM)
    return pl.pallas_call(
        functools.partial(
            prepare_kernel, functools.partial(pair[0].place, count), planes
        ),
        out_shape=(shape, shape),
        in_specs=[vmem, vmem],
        out_specs=(vmem, vmem),
        compiler_params=PARAMS,
        name="prepare",
    )(pair[0].value, pair[1].value)


def finish_kernel(places, planes, vectors, first, second, *refs):
    even_out, odd_out, even_last, odd_last = refs[-4:]
    earlier = refs[:-4]
    depth = first.shape[1]
    modes = vectors.shape[2]
    spots = [place() for place in places]
    parity_lines(first, second, spots[-1][0], planes, even_last, odd_last, 0)
    for parity, (out, last) in enumerate(((even_out, even_last), (odd_out, odd_last))):
        matrix = jnp.concatenate([vectors[at, parity] for _, at in spots], axis=1)
        lines = jnp.concatenate(
            [ref[...] for ref in earlier[parity::2]] + [last[...]], axis=0
        )
        result = jnp.dot(matrix, lines, preferred_element_type=jnp.float32)
        for y in range(planes):
            out[pl.ds(y, modes, stride=planes), :] = result[
                :, y * depth : (y + 1) * depth
            ]


def finish(pairs, count, planes, vectors, earlier):
    lines, depth = pairs[-1][0].value.shape
    rows = lines // planes
    modes = vectors.shape[2]
    shape = jax.ShapeDtypeStruct((modes * planes, depth), jnp.float32)
    vmem = pl.BlockSpec(memory_space=pltpu.VMEM)
    places = [functools.partial(first.place, count) for first, _ in pairs]
    return pl.pallas_call(
        functools.partial(finish_kernel, places, planes),
        out_shape=(shape, shape),
        in_specs=[vmem] * (3 + len(earlier)),
        out_specs=(vmem, vmem),
        scratch_shapes=[pltpu.VMEM((rows, planes * depth), jnp.bfloat16)] * 2,
        compiler_params=PARAMS,
        name="finish",
    )(vectors, pairs[-1][0].value, pairs[-1][1].value, *earlier)


def local(field, even_vectors, odd_vectors):
    count = lax.axis_size("gx")
    slices = lax.axis_size("gz")
    rows, planes, depth = field.shape
    modes = even_vectors.shape[0]
    masks = [1 << b | 1 for b in range(1, count.bit_length() - 1)]

    def widen(vectors, step):
        pairs = [(i, i ^ step) for i in range(slices)]
        return jnp.concatenate((vectors, lax.ppermute(vectors, "gz", pairs)))

    vectors = jnp.stack((even_vectors, odd_vectors))[None]
    steps = [1 << b for b in range(slices.bit_length() - 1)]
    held = [Block(field.reshape(rows * planes, depth), 0, 0)]
    while masks:
        a, b = (masks + masks)[:2]
        crossed = len(masks) > 1
        near = [send(block, a, b, count) for block in held]
        far = [send(block, b, a, count) for block in held] if crossed else []
        if steps:
            vectors = widen(vectors, steps.pop(0))
            vectors, near[0].value = lax.optimization_barrier((vectors, near[0].value))
        across = [send(block, a, b, count) for block in near] if crossed else []
        held += near + far + across
        masks = masks[2:]
    for step in steps:
        vectors = widen(vectors, step)
    held[-1].value, vectors = lax.optimization_barrier((held[-1].value, vectors))
    both = held + [send(block, 1, 1, count) for block in held]

    pairs, left = [], list(range(len(both)))
    while left:
        i = left.pop(0)
        j = next(
            j
            for j in left
            if both[j].even == both[i].even ^ (count - 1)
            and both[j].odd == both[i].odd ^ (count - 1)
        )
        left.remove(j)
        pairs.append((j, i))
    pairs = [(both[i], both[j]) for j, i in sorted(pairs)]
    early = []
    for pair in pairs[:-1]:
        early += prepare(pair, count, planes)
    even, odd = finish(pairs, count, planes, vectors, early)
    return even.reshape(modes, planes, depth), odd.reshape(modes, planes, depth)


def solution(mesh):
    placed = (P("gx", None, "gz"), P("gx", "gz"), P("gx", "gz"))
    return jax.shard_map(
        local,
        mesh=mesh,
        in_specs=placed,
        out_specs=(P("gx", None, "gz"), P("gx", None, "gz")),
        check_vma=False,
    )
```

time: 60.8 us -> 18.3 us (0.30)
  the two profiles are of different devices: /device:TPU:0 before, /device:TPU:29 now
where the time goes in v2:
time: 18.3 us; the launch traced here: 18.1 us
  waiting for transfers between devices  6.99 us (38%)
  starting transfers between devices  6.96 us (38%)
  Pallas kernels  2.31 us (13%)
  other arithmetic  0.75 us (4%)
  between operations  0.69 us (4%)
  local copies, waits for them, and re-layouts  0.37 us (2%)
    ppermute x7, starting transfers between devices, send(): return Block(lax.ppermute(block.value, 'gx', pairs), *offsets)  6.69 us
    ppermute x7, waiting for transfers between devices, send(): return Block(lax.ppermute(block.value, 'gx', pairs), *offsets)  4.73 us
    ppermute x2, waiting for transfers between devices, widen(): return jnp.concatenate((vectors, lax.ppermute(vectors, 'gz', pairs)))  2.26 us
    pallas_call x1, Pallas kernels, finish(): pl.pallas_call(functools.partial(finish_kernel, places, planes), out_shap...  1.49 us
    pallas_call x3, Pallas kernels, prepare(): pl.pallas_call(functools.partial(prepare_kernel, functools.partial(pair[0...  0.82 us
    broadcast_in_dim x1, other arithmetic, local(): vectors = jnp.stack((even_vectors, odd_vectors))[None]  0.72 us
    unnamed x2, local copies, waits for them, and re-layouts  0.37 us
  transfers between devices with their start and end apart: 9, of which 5 were waited for; matrix products, arithmetic and copies ran while one was open for 4% of the time, Pallas kernels for 5%

profile of v2, /device:TPU:29, one launch (start us, length us, event | category | flops | bytes accessed | tf_op | source)
XLA Modules:
  0.0 18.1 jit_solution(3855509712212481625)
XLA Ops:
  0.6 0.8 %collective-permute-start.1 = (bf16[1024,128]{1,0:T(8,128)(2,1)}, bf16[1024,128]{1,0:T(8,128)(2,1)S(1)}, u32[]{:S(2)}, u32[]{:S(2)}) collective-permute-start(bf16[1024,128]{1,0:T(8,128)(2,1)} %bitcast.7), channel_id=1, source_target_pairs={{0,12},{4,16},{8,4},{12,24},{16,28},{20,0},{24,20},{28,8},{1,13},{... | collective-permute-start | bytes 786440 | tf_op jit(solution)/shard_map/ppermute | solution.py:32
  1.5 0.7 %maximum_bitcast_fusion = bf16[1,2,32,64]{3,2,1,0:T(8,128)(2,1)S(1)} fusion(bf16[1,32,64]{2,1,0:T(8,128)(2,1)} %bitcast.11, bf16[1,32,64]{2,1,0:T(8,128)(2,1)} %bitcast.12), kind=kLoop, calls=%fused_computation.2 | loop fusion | flops 4096 | bytes 16384 | tf_op jit(solution)/shard_map/broadcast_in_dim | solution.py:129
  2.2 0.2 %collective-permute-start = (bf16[1,2,32,64]{3,2,1,0:T(8,128)(2,1)S(1)}, bf16[1,2,32,64]{3,2,1,0:T(8,128)(2,1)S(1)}, u32[]{:S(2)}, u32[]{:S(2)}) collective-permute-start(bf16[1,2,32,64]{3,2,1,0:T(8,128)(2,1)S(1)} %maximum_bitcast_fusion), channel_id=1, source_target_pairs={{0,1},{1,0},{2,3},{3,2},{4,5},{5,4},{6,7},{7,6},{8,9},{9,8},{10,11... | collective-permute-start | bytes 24584 | tf_op jit(solution)/shard_map/ppermute | solution.py:127
  2.4 1.3 %collective-permute-start.7 = (bf16[1024,128]{1,0:T(8,128)(2,1)}, bf16[1024,128]{1,0:T(8,128)(2,1)S(1)}, u32[]{:S(2)}, u32[]{:S(2)}) collective-permute-start(bf16[1024,128]{1,0:T(8,128)(2,1)} %bitcast.8), channel_id=1, source_target_pairs={{0,20},{4,8},{8,28},{12,0},{16,4},{20,24},{24,12},{28,16},{1,21},{... | collective-permute-start | bytes 786440 | tf_op jit(solution)/shard_map/ppermute | solution.py:32
  3.7 1.4 %collective-permute-done = bf16[1,2,32,64]{3,2,1,0:T(8,128)(2,1)S(1)} collective-permute-done((bf16[1,2,32,64]{3,2,1,0:T(8,128)(2,1)S(1)}, bf16[1,2,32,64]{3,2,1,0:T(8,128)(2,1)S(1)}, u32[]{:S(2)}, u32[]{:S(2)}) %collective-permute-start) | collective-permute-done | bytes 8224 | tf_op jit(solution)/shard_map/ppermute | solution.py:127
  5.1 2.5 %collective-permute-done.1.first = bf16[1024,128]{1,0:T(8,128)(2,1)S(1)} collective-permute-done((bf16[1024,128]{1,0:T(8,128)(2,1)}, bf16[1024,128]{1,0:T(8,128)(2,1)S(1)}, u32[]{:S(2)}, u32[]{:S(2)}) %collective-permute-start.1) | collective-permute-done | bytes 262176 | tf_op jit(solution)/shard_map/ppermute | solution.py:32
  7.7 0.5 %collective-permute-start.2 = (bf16[1024,128]{1,0:T(8,128)(2,1)S(1)}, bf16[1024,128]{1,0:T(8,128)(2,1)S(1)}, u32[]{:S(2)}, u32[]{:S(2)}) collective-permute-start(bf16[1024,128]{1,0:T(8,128)(2,1)S(1)} %collective-permute-done.1.first), channel_id=1, source_target_pairs={{0,12},{4,16},{8,4},{12,24},{16,28},{20,0},{24,20},{28,8},{1,13},{... | collective-permute-start | bytes 786440 | tf_op jit(solution)/shard_map/ppermute | solution.py:32
  8.2 0.1 collective-permute-start.3
  8.2 2.3 %collective-permute-start.5 = (bf16[1024,128]{1,0:T(8,128)(2,1)}, bf16[1024,128]{1,0:T(8,128)(2,1)S(1)}, u32[]{:S(2)}, u32[]{:S(2)}) collective-permute-start(bf16[1024,128]{1,0:T(8,128)(2,1)} %bitcast.9), channel_id=1, source_target_pairs={{0,4},{4,0},{8,12},{12,8},{16,20},{20,16},{24,28},{28,24},{1,5},{5... | collective-permute-start | bytes 786440 | tf_op jit(solution)/shard_map/ppermute | solution.py:32
  10.5 0.0 collective-permute-start.6
  10.5 0.0 collective-permute-done.7.first
  10.5 0.5 %collective-permute-start.8 = (bf16[1024,128]{1,0:T(8,128)(2,1)S(1)}, bf16[1024,128]{1,0:T(8,128)(2,1)S(1)}, u32[]{:S(2)}, u32[]{:S(2)}) collective-permute-start(bf16[1024,128]{1,0:T(8,128)(2,1)S(1)} %collective-permute-done.7.first), channel_id=1, source_target_pairs={{0,4},{4,0},{8,12},{12,8},{16,20},{20,16},{24,28},{28,24},{1,5},{5... | collective-permute-start | bytes 786440 | tf_op jit(solution)/shard_map/ppermute | solution.py:32
  11.0 0.8 %collective-permute-done.3 = bf16[2,2,32,64]{3,2,1,0:T(8,128)(2,1)S(1)} collective-permute-done((bf16[2,2,32,64]{3,2,1,0:T(8,128)(2,1)S(1)}, bf16[2,2,32,64]{3,2,1,0:T(8,128)(2,1)S(1)}, u32[]{:S(2)}, u32[]{:S(2)}) %collective-permute-start.3) | collective-permute-done | bytes 16416 | tf_op jit(solution)/shard_map/ppermute | solution.py:127
  11.8 1.9 %collective-permute-done.2.first = bf16[1024,128]{1,0:T(8,128)(2,1)S(1)} collective-permute-done((bf16[1024,128]{1,0:T(8,128)(2,1)S(1)}, bf16[1024,128]{1,0:T(8,128)(2,1)S(1)}, u32[]{:S(2)}, u32[]{:S(2)}) %collective-permute-start.2) | collective-permute-done | bytes 262176 | tf_op jit(solution)/shard_map/ppermute | solution.py:32
  13.8 1.3 %collective-permute-start.4 = (bf16[1024,128]{1,0:T(8,128)(2,1)S(1)}, bf16[1024,128]{1,0:T(8,128)(2,1)S(1)}, u32[]{:S(2)}, u32[]{:S(2)}) collective-permute-start(bf16[1024,128]{1,0:T(8,128)(2,1)S(1)} %collective-permute-done.2.first), channel_id=1, source_target_pairs={{0,4},{4,0},{8,12},{12,8},{16,20},{20,16},{24,28},{28,24},{1,5},{5... | collective-permute-start | bytes 786440 | tf_op jit(solution)/shard_map/ppermute | solution.py:32
  15.1 0.0 collective-permute-done.8.second
  15.1 0.3 %prepare.5 = (bf16[64,2048]{1,0:T(8,128)(2,1)S(1)}, bf16[64,2048]{1,0:T(8,128)(2,1)S(1)}) custom-call(bf16[1024,128]{1,0:T(8,128)(2,1)S(1)} %collective-permute-done.7.first, bf16[1024,128]{1,0:T(8,128)(2,1)S(1)} %collective-permute-done.8.second), custom_call_target="tpu_custom_call" | custom-call | tf_op jit(solution)/shard_map/prepare/pallas_call | solution.py:69
  15.3 0.0 collective-permute-done.6.second
  15.3 0.3 %prepare.4 = (bf16[64,2048]{1,0:T(8,128)(2,1)S(1)}, bf16[64,2048]{1,0:T(8,128)(2,1)S(1)}) custom-call(bf16[1024,128]{1,0:T(8,128)(2,1)S(1)} %collective-permute-done.1.first, bf16[1024,128]{1,0:T(8,128)(2,1)S(1)} %collective-permute-done.6.second), custom_call_target="tpu_custom_call" | custom-call | tf_op jit(solution)/shard_map/prepare/pallas_call | solution.py:69
  15.6 0.0 copy-start
  15.6 0.0 collective-permute-done.5.second
  15.7 0.3 %prepare.3 = (bf16[64,2048]{1,0:T(8,128)(2,1)S(1)}, bf16[64,2048]{1,0:T(8,128)(2,1)S(1)}) custom-call(bf16[1024,128]{1,0:T(8,128)(2,1)S(1)} %collective-permute-done.2.first, bf16[1024,128]{1,0:T(8,128)(2,1)S(1)} %collective-permute-done.5.second), custom_call_target="tpu_custom_call" | custom-call | tf_op jit(solution)/shard_map/prepare/pallas_call | solution.py:69
  15.9 0.3 %collective-permute-done.4.second = bf16[1024,128]{1,0:T(8,128)(2,1)S(1)} collective-permute-done((bf16[1024,128]{1,0:T(8,128)(2,1)S(1)}, bf16[1024,128]{1,0:T(8,128)(2,1)S(1)}, u32[]{:S(2)}, u32[]{:S(2)}) %collective-permute-start.4) | collective-permute-done | bytes 262176 | tf_op jit(solution)/shard_map/ppermute | solution.py:32
  16.2 0.4 %copy-done = bf16[64,16,128]{2,1,0:T(8,128)(2,1)S(1)} copy-done((bf16[64,16,128]{2,1,0:T(8,128)(2,1)S(1)}, bf16[64,16,128]{2,1,0:T(8,128)(2,1)}, u32[]{:S(2)}) %copy-start) | copy-done | bytes 262168
  16.6 1.5 %finish.1 = (f32[512,128]{1,0:T(8,128)}, f32[512,128]{1,0:T(8,128)}) custom-call(bf16[4,2,32,64]{3,2,1,0:T(8,128)(2,1)S(1)} %pad_maximum_fusion.vectors, bf16[1024,128]{1,0:T(8,128)(2,1)S(1)} %bitcast.10, bf16[1024,128]{1,0:T(8,128)(2,1)S(1)} %collective-permute-done.4.second, bf16[64,2048]{1,0:T(8,128)(2,1)S(1)} %get-tuple-element.18.refs_0_, ...), custom_call_target="tpu_custom_call" | custom-call | tf_op jit(solution)/shard_map/finish/pallas_call | solution.py:107
  (2 shorter events, 0.0 us)
Async XLA Ops:
  0.6 7.0 %collective-permute-start.1 = (bf16[1024,128]{1,0:T(8,128)(2,1)}, bf16[1024,128]{1,0:T(8,128)(2,1)S(1)}, u32[]{:S(2)}, u32[]{:S(2)}) collective-permute-start(bf16[1024,128]{1,0:T(8,128)(2,1)} %bitcast.7), channel_id=1, source_target_pairs={{0,12},{4,16},{8,4},{12,24},{16,28},{20,0},{24,20},{28,8},{1,13},{... | collective-permute-start | bytes 786440 | tf_op jit(solution)/shard_map/ppermute | solution.py:32
  2.2 2.9 %collective-permute-start = (bf16[1,2,32,64]{3,2,1,0:T(8,128)(2,1)S(1)}, bf16[1,2,32,64]{3,2,1,0:T(8,128)(2,1)S(1)}, u32[]{:S(2)}, u32[]{:S(2)}) collective-permute-start(bf16[1,2,32,64]{3,2,1,0:T(8,128)(2,1)S(1)} %maximum_bitcast_fusion), channel_id=1, source_target_pairs={{0,1},{1,0},{2,3},{3,2},{4,5},{5,4},{6,7},{7,6},{8,9},{9,8},{10,11... | collective-permute-start | bytes 24584 | tf_op jit(solution)/shard_map/ppermute | solution.py:127
  2.4 8.1 %collective-permute-start.7 = (bf16[1024,128]{1,0:T(8,128)(2,1)}, bf16[1024,128]{1,0:T(8,128)(2,1)S(1)}, u32[]{:S(2)}, u32[]{:S(2)}) collective-permute-start(bf16[1024,128]{1,0:T(8,128)(2,1)} %bitcast.8), channel_id=1, source_target_pairs={{0,20},{4,8},{8,28},{12,0},{16,4},{20,24},{24,12},{28,16},{1,21},{... | collective-permute-start | bytes 786440 | tf_op jit(solution)/shard_map/ppermute | solution.py:32
  7.7 6.1 %collective-permute-start.2 = (bf16[1024,128]{1,0:T(8,128)(2,1)S(1)}, bf16[1024,128]{1,0:T(8,128)(2,1)S(1)}, u32[]{:S(2)}, u32[]{:S(2)}) collective-permute-start(bf16[1024,128]{1,0:T(8,128)(2,1)S(1)} %collective-permute-done.1.first), channel_id=1, source_target_pairs={{0,12},{4,16},{8,4},{12,24},{16,28},{20,0},{24,20},{28,8},{1,13},{... | collective-permute-start | bytes 786440 | tf_op jit(solution)/shard_map/ppermute | solution.py:32
  8.2 3.7 %collective-permute-start.3 = (bf16[2,2,32,64]{3,2,1,0:T(8,128)(2,1)S(1)}, bf16[2,2,32,64]{3,2,1,0:T(8,128)(2,1)S(1)}, u32[]{:S(2)}, u32[]{:S(2)}) collective-permute-start(bf16[2,2,32,64]{3,2,1,0:T(8,128)(2,1)S(1)} %pad_maximum_fusion.1), channel_id=1, source_target_pairs={{0,2},{1,3},{2,0},{3,1},{4,6},{5,7},{6,4},{7,5},{8,10},{9,11},{10,... | collective-permute-start | bytes 49160 | tf_op jit(solution)/shard_map/ppermute | solution.py:127
  8.2 7.4 %collective-permute-start.5 = (bf16[1024,128]{1,0:T(8,128)(2,1)}, bf16[1024,128]{1,0:T(8,128)(2,1)S(1)}, u32[]{:S(2)}, u32[]{:S(2)}) collective-permute-start(bf16[1024,128]{1,0:T(8,128)(2,1)} %bitcast.9), channel_id=1, source_target_pairs={{0,4},{4,0},{8,12},{12,8},{16,20},{20,16},{24,28},{28,24},{1,5},{5... | collective-permute-start | bytes 786440 | tf_op jit(solution)/shard_map/ppermute | solution.py:32
  10.5 4.9 %collective-permute-start.6 = (bf16[1024,128]{1,0:T(8,128)(2,1)S(1)}, bf16[1024,128]{1,0:T(8,128)(2,1)S(1)}, u32[]{:S(2)}, u32[]{:S(2)}) collective-permute-start(bf16[1024,128]{1,0:T(8,128)(2,1)S(1)} %collective-permute-done.1.first), channel_id=1, source_target_pairs={{0,4},{4,0},{8,12},{12,8},{16,20},{20,16},{24,28},{28,24},{1,5},{5... | collective-permute-start | bytes 786440 | tf_op jit(solution)/shard_map/ppermute | solution.py:32
  10.5 4.6 %collective-permute-start.8 = (bf16[1024,128]{1,0:T(8,128)(2,1)S(1)}, bf16[1024,128]{1,0:T(8,128)(2,1)S(1)}, u32[]{:S(2)}, u32[]{:S(2)}) collective-permute-start(bf16[1024,128]{1,0:T(8,128)(2,1)S(1)} %collective-permute-done.7.first), channel_id=1, source_target_pairs={{0,4},{4,0},{8,12},{12,8},{16,20},{20,16},{24,28},{28,24},{1,5},{5... | collective-permute-start | bytes 786440 | tf_op jit(solution)/shard_map/ppermute | solution.py:32
  13.8 2.4 %collective-permute-start.4 = (bf16[1024,128]{1,0:T(8,128)(2,1)S(1)}, bf16[1024,128]{1,0:T(8,128)(2,1)S(1)}, u32[]{:S(2)}, u32[]{:S(2)}) collective-permute-start(bf16[1024,128]{1,0:T(8,128)(2,1)S(1)} %collective-permute-done.2.first), channel_id=1, source_target_pairs={{0,4},{4,0},{8,12},{12,8},{16,20},{20,16},{24,28},{28,24},{1,5},{5... | collective-permute-start | bytes 786440 | tf_op jit(solution)/shard_map/ppermute | solution.py:32
  15.6 1.0 %copy-start = (bf16[64,16,128]{2,1,0:T(8,128)(2,1)S(1)}, bf16[64,16,128]{2,1,0:T(8,128)(2,1)}, u32[]{:S(2)}) copy-start(bf16[64,16,128]{2,1,0:T(8,128)(2,1)} %param.3) | copy-start | bytes 786436

commit v3 on v2

--- a/solution.py
+++ b/solution.py
@@ -78,41 +78,56 @@
     )(pair[0].value, pair[1].value)
 
 
-def finish_kernel(places, planes, vectors, first, second, *refs):
-    even_out, odd_out, even_last, odd_last = refs[-4:]
-    earlier = refs[:-4]
+def combine_kernel(places, planes, last, vectors, first, second, *refs):
+    ready = 2 * (len(places) - 1)
+    lines, sums, (*outs, even, odd) = refs[:ready], refs[ready], refs[ready + last :]
     depth = first.shape[1]
     modes = vectors.shape[2]
     spots = [place() for place in places]
-    parity_lines(first, second, spots[-1][0], planes, even_last, odd_last, 0)
-    for parity, (out, last) in enumerate(((even_out, even_last), (odd_out, odd_last))):
+    parity_lines(first, second, spots[-1][0], planes, even, odd, 0)
+    for parity, fresh in enumerate((even, odd)):
         matrix = jnp.concatenate([vectors[at, parity] for _, at in spots], axis=1)
-        lines = jnp.concatenate(
-            [ref[...] for ref in earlier[parity::2]] + [last[...]], axis=0
+        parts = jnp.concatenate(
+            [ref[...] for ref in lines[parity::2]] + [fresh[...]], axis=0
         )
-        result = jnp.dot(matrix, lines, preferred_element_type=jnp.float32)
+        result = jnp.dot(matrix, parts, preferred_element_type=jnp.float32)
+        if not last:
+            outs[0][parity] = result
+            continue
+        result = result + sums[parity]
         for y in range(planes):
-            out[pl.ds(y, modes, stride=planes), :] = result[
+            outs[parity][pl.ds(y, modes, stride=planes), :] = result[
                 :, y * depth : (y + 1) * depth
             ]
 
 
-def finish(pairs, count, planes, vectors, earlier):
-    lines, depth = pairs[-1][0].value.shape
+def combine(vectors, pair, count, planes, ready=(), sums=None):
+    last = sums is not None
+    first, second = (block.value for block in pair)
+    lines, depth = first.shape
     rows = lines // planes
     modes = vectors.shape[2]
-    shape = jax.ShapeDtypeStruct((modes * planes, depth), jnp.float32)
+    if last:
+        shape = [jax.ShapeDtypeStruct((modes * planes, depth), jnp.float32)] * 2
+    else:
+        shape = [jax.ShapeDtypeStruct((2, modes, planes * depth), jnp.float32)]
+    operands = [vectors, first, second]
+    for _, parts in ready:
+        operands += parts
+    if last:
+        operands.append(sums)
+    places = [functools.partial(block.place, count) for block, _ in ready]
+    places.append(functools.partial(pair[0].place, count))
     vmem = pl.BlockSpec(memory_space=pltpu.VMEM)
-    places = [functools.partial(first.place, count) for first, _ in pairs]
     return pl.pallas_call(
-        functools.partial(finish_kernel, places, planes),
-        out_shape=(shape, shape),
-        in_specs=[vmem] * (3 + len(earlier)),
-        out_specs=(vmem, vmem),
+        functools.partial(combine_kernel, places, planes, last),
+        out_shape=shape,
+        in_specs=[vmem] * len(operands),
+        out_specs=[vmem] * len(shape),
         scratch_shapes=[pltpu.VMEM((rows, planes * depth), jnp.bfloat16)] * 2,
         compiler_params=PARAMS,
-        name="finish",
-    )(vectors, pairs[-1][0].value, pairs[-1][1].value, *earlier)
+        name="finish" if last else "combine",
+    )(*operands)
 
 
 def local(field, even_vectors, odd_vectors):
@@ -126,6 +141,10 @@
         pairs = [(i, i ^ step) for i in range(slices)]
         return jnp.concatenate((vectors, lax.ppermute(vectors, "gz", pairs)))
 
+    def after(block, *values):
+        value = lax.optimization_barrier((block.value, *values))[0]
+        return Block(value, block.even, block.odd)
+
     vectors = jnp.stack((even_vectors, odd_vectors))[None]
     steps = [1 << b for b in range(slices.bit_length() - 1)]
     held = [Block(field.reshape(rows * planes, depth), 0, 0)]
@@ -136,15 +155,19 @@
         far = [send(block, b, a, count) for block in held] if crossed else []
         if steps:
             vectors = widen(vectors, steps.pop(0))
-            vectors, near[0].value = lax.optimization_barrier((vectors, near[0].value))
+            near[0] = after(near[0], vectors)
         across = [send(block, a, b, count) for block in near] if crossed else []
         held += near + far + across
         masks = masks[2:]
     for step in steps:
         vectors = widen(vectors, step)
-    held[-1].value, vectors = lax.optimization_barrier((held[-1].value, vectors))
-    both = held + [send(block, 1, 1, count) for block in held]
+    others = []
+    for block in held[:-1]:
+        block = after(block, *(other.value for other in others[:1]))
+        others.append(send(block, 1, 1, count))
+    others.append(send(after(held[-1], vectors), 1, 1, count))
 
+    both = held[:-1] + others[:-1] + [held[-1], others[-1]]
     pairs, left = [], list(range(len(both)))
     while left:
         i = left.pop(0)
@@ -157,10 +180,9 @@
         left.remove(j)
         pairs.append((j, i))
     pairs = [(both[i], both[j]) for j, i in sorted(pairs)]
-    early = []
-    for pair in pairs[:-1]:
-        early += prepare(pair, count, planes)
-    even, odd = finish(pairs, count, planes, vectors, early)
+    ready = [(pair[0], prepare(pair, count, planes)) for pair in pairs[:-2]]
+    (sums,) = combine(vectors, pairs[-2], count, planes, ready)
+    even, odd = combine(vectors, pairs[-1], count, planes, sums=sums)
     return even.reshape(modes, planes, depth), odd.reshape(modes, planes, depth)
 
 

time: 18.3 us -> 18 us (0.984)
  the two profiles are of different devices: /device:TPU:29 before, /device:TPU:0 now
where the time goes in v3:
time: 18 us; the launch traced here: 17.7 us
  starting transfers between devices  11.2 us (62%)
  Pallas kernels  2.52 us (14%)
  waiting for transfers between devices  2.51 us (14%)
  other arithmetic  0.75 us (4%)
  between operations  0.69 us (4%)
    ppermute x7, starting transfers between devices, send(): return Block(lax.ppermute(block.value, 'gx', pairs), *offsets)  7.03 us
    ppermute x2, starting transfers between devices, widen(): return jnp.concatenate((vectors, lax.ppermute(vectors, 'gz', pairs)))  4.22 us
    pallas_call x2, Pallas kernels, combine(): pl.pallas_call(functools.partial(combine_kernel, places, planes, last), o...  1.97 us
    ppermute x7, waiting for transfers between devices, send(): return Block(lax.ppermute(block.value, 'gx', pairs), *offsets)  1.47 us
    ppermute x2, waiting for transfers between devices, widen(): return jnp.concatenate((vectors, lax.ppermute(vectors, 'gz', pairs)))  1.04 us
    broadcast_in_dim x1, other arithmetic, local(): vectors = jnp.stack((even_vectors, odd_vectors))[None]  0.72 us
    pallas_call x2, Pallas kernels, prepare(): pl.pallas_call(functools.partial(prepare_kernel, functools.partial(pair[0...  0.55 us
  transfers between devices with their start and end apart: 9, of which 5 were waited for; matrix products, arithmetic and copies ran while one was open for 4% of the time, Pallas kernels for 7%

profile of v3, /device:TPU:0, one launch (start us, length us, event | category | flops | bytes accessed | tf_op | source)
XLA Modules:
  0.0 17.7 jit_solution(16948601809389500533)
XLA Ops:
  0.6 2.4 %collective-permute-start.2 = (bf16[1024,128]{1,0:T(8,128)(2,1)}, bf16[1024,128]{1,0:T(8,128)(2,1)S(1)}, u32[]{:S(2)}, u32[]{:S(2)}) collective-permute-start(bf16[1024,128]{1,0:T(8,128)(2,1)} %bitcast.7), channel_id=1, source_target_pairs={{0,12},{4,16},{8,4},{12,24},{16,28},{20,0},{24,20},{28,8},{1,13},{... | collective-permute-start | bytes 786440 | tf_op jit(solution)/shard_map/ppermute | solution.py:32
  3.1 0.7 %maximum_bitcast_fusion = bf16[1,2,32,64]{3,2,1,0:T(8,128)(2,1)S(1)} fusion(bf16[1,32,64]{2,1,0:T(8,128)(2,1)} %bitcast.11, bf16[1,32,64]{2,1,0:T(8,128)(2,1)} %bitcast.12), kind=kLoop, calls=%fused_computation.2 | loop fusion | flops 4096 | bytes 16384 | tf_op jit(solution)/shard_map/broadcast_in_dim | solution.py:148
  3.8 1.6 %collective-permute-start = (bf16[1,2,32,64]{3,2,1,0:T(8,128)(2,1)S(1)}, bf16[1,2,32,64]{3,2,1,0:T(8,128)(2,1)S(1)}, u32[]{:S(2)}, u32[]{:S(2)}) collective-permute-start(bf16[1,2,32,64]{3,2,1,0:T(8,128)(2,1)S(1)} %maximum_bitcast_fusion), channel_id=1, source_target_pairs={{0,1},{1,0},{2,3},{3,2},{4,5},{5,4},{6,7},{7,6},{8,9},{9,8},{10,11... | collective-permute-start | bytes 24584 | tf_op jit(solution)/shard_map/ppermute | solution.py:142
  5.4 0.4 %collective-permute-start.5 = (bf16[1024,128]{1,0:T(8,128)(2,1)}, bf16[1024,128]{1,0:T(8,128)(2,1)S(1)}, u32[]{:S(2)}, u32[]{:S(2)}) collective-permute-start(bf16[1024,128]{1,0:T(8,128)(2,1)} %bitcast.8), channel_id=1, source_target_pairs={{0,4},{4,0},{8,12},{12,8},{16,20},{20,16},{24,28},{28,24},{1,5},{5... | collective-permute-start | bytes 786440 | tf_op jit(solution)/shard_map/ppermute | solution.py:32
  5.8 1.2 %collective-permute-start.7 = (bf16[1024,128]{1,0:T(8,128)(2,1)}, bf16[1024,128]{1,0:T(8,128)(2,1)S(1)}, u32[]{:S(2)}, u32[]{:S(2)}) collective-permute-start(bf16[1024,128]{1,0:T(8,128)(2,1)} %bitcast.9), channel_id=1, source_target_pairs={{0,20},{4,8},{8,28},{12,0},{16,4},{20,24},{24,12},{28,16},{1,21},{... | collective-permute-start | bytes 786440 | tf_op jit(solution)/shard_map/ppermute | solution.py:32
  7.0 0.5 %collective-permute-done = bf16[1,2,32,64]{3,2,1,0:T(8,128)(2,1)S(1)} collective-permute-done((bf16[1,2,32,64]{3,2,1,0:T(8,128)(2,1)S(1)}, bf16[1,2,32,64]{3,2,1,0:T(8,128)(2,1)S(1)}, u32[]{:S(2)}, u32[]{:S(2)}) %collective-permute-start) | collective-permute-done | bytes 8224 | tf_op jit(solution)/shard_map/ppermute | solution.py:142
  7.6 0.0 collective-permute-done.2.first
  7.6 1.8 %collective-permute-start.3 = (bf16[1024,128]{1,0:T(8,128)(2,1)S(1)}, bf16[1024,128]{1,0:T(8,128)(2,1)S(1)}, u32[]{:S(2)}, u32[]{:S(2)}) collective-permute-start(bf16[1024,128]{1,0:T(8,128)(2,1)S(1)} %collective-permute-done.2.first), channel_id=1, source_target_pairs={{0,12},{4,16},{8,4},{12,24},{16,28},{20,0},{24,20},{28,8},{1,13},{... | collective-permute-start | bytes 786440 | tf_op jit(solution)/shard_map/ppermute | solution.py:32
  9.3 2.6 %collective-permute-start.1 = (bf16[2,2,32,64]{3,2,1,0:T(8,128)(2,1)S(1)}, bf16[2,2,32,64]{3,2,1,0:T(8,128)(2,1)S(1)}, u32[]{:S(2)}, u32[]{:S(2)}) collective-permute-start(bf16[2,2,32,64]{3,2,1,0:T(8,128)(2,1)S(1)} %pad_maximum_fusion.1), channel_id=1, source_target_pairs={{0,2},{1,3},{2,0},{3,1},{4,6},{5,7},{6,4},{7,5},{8,10},{9,11},{10,... | collective-permute-start | bytes 49160 | tf_op jit(solution)/shard_map/ppermute | solution.py:142
  11.9 0.0 collective-permute-done.5.first
  11.9 0.5 %collective-permute-done.7.first = bf16[1024,128]{1,0:T(8,128)(2,1)S(1)} collective-permute-done((bf16[1024,128]{1,0:T(8,128)(2,1)}, bf16[1024,128]{1,0:T(8,128)(2,1)S(1)}, u32[]{:S(2)}, u32[]{:S(2)}) %collective-permute-start.7) | collective-permute-done | bytes 262176 | tf_op jit(solution)/shard_map/ppermute | solution.py:32
  12.4 1.2 %collective-permute-start.8 = (bf16[1024,128]{1,0:T(8,128)(2,1)S(1)}, bf16[1024,128]{1,0:T(8,128)(2,1)S(1)}, u32[]{:S(2)}, u32[]{:S(2)}) collective-permute-start(bf16[1024,128]{1,0:T(8,128)(2,1)S(1)} %collective-permute-done.7.first), channel_id=1, source_target_pairs={{0,4},{4,0},{8,12},{12,8},{16,20},{20,16},{24,28},{28,24},{1,5},{5... | collective-permute-start | bytes 786440 | tf_op jit(solution)/shard_map/ppermute | solution.py:32
  13.7 0.0 collective-permute-start.6
  13.7 0.5 %collective-permute-done.1 = bf16[2,2,32,64]{3,2,1,0:T(8,128)(2,1)S(1)} collective-permute-done((bf16[2,2,32,64]{3,2,1,0:T(8,128)(2,1)S(1)}, bf16[2,2,32,64]{3,2,1,0:T(8,128)(2,1)S(1)}, u32[]{:S(2)}, u32[]{:S(2)}) %collective-permute-start.1) | collective-permute-done | bytes 16416 | tf_op jit(solution)/shard_map/ppermute | solution.py:142
  14.2 0.7 %collective-permute-done.3.second = bf16[1024,128]{1,0:T(8,128)(2,1)S(1)} collective-permute-done((bf16[1024,128]{1,0:T(8,128)(2,1)S(1)}, bf16[1024,128]{1,0:T(8,128)(2,1)S(1)}, u32[]{:S(2)}, u32[]{:S(2)}) %collective-permute-start.3) | collective-permute-done | bytes 262176 | tf_op jit(solution)/shard_map/ppermute | solution.py:32
  14.9 0.0 collective-permute-start.4
  14.9 0.0 collective-permute-done.8.second
  14.9 0.3 %prepare.3 = (bf16[64,2048]{1,0:T(8,128)(2,1)S(1)}, bf16[64,2048]{1,0:T(8,128)(2,1)S(1)}) custom-call(bf16[1024,128]{1,0:T(8,128)(2,1)S(1)} %collective-permute-done.7.first, bf16[1024,128]{1,0:T(8,128)(2,1)S(1)} %collective-permute-done.8.second), custom_call_target="tpu_custom_call" | custom-call | tf_op jit(solution)/shard_map/prepare/pallas_call | solution.py:69
  15.2 0.0 collective-permute-done.6.second
  15.2 0.3 %prepare.2 = (bf16[64,2048]{1,0:T(8,128)(2,1)S(1)}, bf16[64,2048]{1,0:T(8,128)(2,1)S(1)}) custom-call(bf16[1024,128]{1,0:T(8,128)(2,1)S(1)} %collective-permute-done.2.first, bf16[1024,128]{1,0:T(8,128)(2,1)S(1)} %collective-permute-done.6.second), custom_call_target="tpu_custom_call" | custom-call | tf_op jit(solution)/shard_map/prepare/pallas_call | solution.py:69
  15.5 0.0 copy-start
  15.5 0.7 %combine.1.refs_0_ = f32[2,32,2048]{2,1,0:T(8,128)S(1)} custom-call(bf16[4,2,32,64]{3,2,1,0:T(8,128)(2,1)S(1)} %pad_maximum_fusion.vectors, bf16[1024,128]{1,0:T(8,128)(2,1)S(1)} %collective-permute-done.5.first, bf16[1024,128]{1,0:T(8,128)(2,1)S(1)} %collective-permute-done.3.second, bf16[64,2048]{1,0:T(8,128)(2,1)S(1)} %get-tuple-element.15.refs_0_, ...), custom_call_target="tpu_custom_call" | custom-call | tf_op jit(solution)/shard_map/combine/pallas_call | solution.py:122
  16.2 0.2 %collective-permute-done.4.second = bf16[1024,128]{1,0:T(8,128)(2,1)S(1)} collective-permute-done((bf16[1024,128]{1,0:T(8,128)(2,1)S(1)}, bf16[1024,128]{1,0:T(8,128)(2,1)S(1)}, u32[]{:S(2)}, u32[]{:S(2)}) %collective-permute-start.4) | collective-permute-done | bytes 262176 | tf_op jit(solution)/shard_map/ppermute | solution.py:32
  16.5 0.0 copy-done
  16.5 1.3 %finish.1 = (f32[512,128]{1,0:T(8,128)}, f32[512,128]{1,0:T(8,128)}) custom-call(bf16[4,2,32,64]{3,2,1,0:T(8,128)(2,1)S(1)} %pad_maximum_fusion.vectors, bf16[1024,128]{1,0:T(8,128)(2,1)S(1)} %bitcast.10, bf16[1024,128]{1,0:T(8,128)(2,1)S(1)} %collective-permute-done.4.second, f32[2,32,2048]{2,1,0:T(8,128)S(1)} %combine.1.refs_0_), custom_call_target="tpu_custom_call" | custom-call | tf_op jit(solution)/shard_map/finish/pallas_call | solution.py:122
  (2 shorter events, 0.0 us)
Async XLA Ops:
  0.6 7.0 %collective-permute-start.2 = (bf16[1024,128]{1,0:T(8,128)(2,1)}, bf16[1024,128]{1,0:T(8,128)(2,1)S(1)}, u32[]{:S(2)}, u32[]{:S(2)}) collective-permute-start(bf16[1024,128]{1,0:T(8,128)(2,1)} %bitcast.7), channel_id=1, source_target_pairs={{0,12},{4,16},{8,4},{12,24},{16,28},{20,0},{24,20},{28,8},{1,13},{... | collective-permute-start | bytes 786440 | tf_op jit(solution)/shard_map/ppermute | solution.py:32
  3.8 3.8 %collective-permute-start = (bf16[1,2,32,64]{3,2,1,0:T(8,128)(2,1)S(1)}, bf16[1,2,32,64]{3,2,1,0:T(8,128)(2,1)S(1)}, u32[]{:S(2)}, u32[]{:S(2)}) collective-permute-start(bf16[1,2,32,64]{3,2,1,0:T(8,128)(2,1)S(1)} %maximum_bitcast_fusion), channel_id=1, source_target_pairs={{0,1},{1,0},{2,3},{3,2},{4,5},{5,4},{6,7},{7,6},{8,9},{9,8},{10,11... | collective-permute-start | bytes 24584 | tf_op jit(solution)/shard_map/ppermute | solution.py:142
  5.4 6.5 %collective-permute-start.5 = (bf16[1024,128]{1,0:T(8,128)(2,1)}, bf16[1024,128]{1,0:T(8,128)(2,1)S(1)}, u32[]{:S(2)}, u32[]{:S(2)}) collective-permute-start(bf16[1024,128]{1,0:T(8,128)(2,1)} %bitcast.8), channel_id=1, source_target_pairs={{0,4},{4,0},{8,12},{12,8},{16,20},{20,16},{24,28},{28,24},{1,5},{5... | collective-permute-start | bytes 786440 | tf_op jit(solution)/shard_map/ppermute | solution.py:32
  5.8 6.6 %collective-permute-start.7 = (bf16[1024,128]{1,0:T(8,128)(2,1)}, bf16[1024,128]{1,0:T(8,128)(2,1)S(1)}, u32[]{:S(2)}, u32[]{:S(2)}) collective-permute-start(bf16[1024,128]{1,0:T(8,128)(2,1)} %bitcast.9), channel_id=1, source_target_pairs={{0,20},{4,8},{8,28},{12,0},{16,4},{20,24},{24,12},{28,16},{1,21},{... | collective-permute-start | bytes 786440 | tf_op jit(solution)/shard_map/ppermute | solution.py:32
  7.6 7.3 %collective-permute-start.3 = (bf16[1024,128]{1,0:T(8,128)(2,1)S(1)}, bf16[1024,128]{1,0:T(8,128)(2,1)S(1)}, u32[]{:S(2)}, u32[]{:S(2)}) collective-permute-start(bf16[1024,128]{1,0:T(8,128)(2,1)S(1)} %collective-permute-done.2.first), channel_id=1, source_target_pairs={{0,12},{4,16},{8,4},{12,24},{16,28},{20,0},{24,20},{28,8},{1,13},{... | collective-permute-start | bytes 786440 | tf_op jit(solution)/shard_map/ppermute | solution.py:32
  9.3 4.8 %collective-permute-start.1 = (bf16[2,2,32,64]{3,2,1,0:T(8,128)(2,1)S(1)}, bf16[2,2,32,64]{3,2,1,0:T(8,128)(2,1)S(1)}, u32[]{:S(2)}, u32[]{:S(2)}) collective-permute-start(bf16[2,2,32,64]{3,2,1,0:T(8,128)(2,1)S(1)} %pad_maximum_fusion.1), channel_id=1, source_target_pairs={{0,2},{1,3},{2,0},{3,1},{4,6},{5,7},{6,4},{7,5},{8,10},{9,11},{10,... | collective-permute-start | bytes 49160 | tf_op jit(solution)/shard_map/ppermute | solution.py:142
  12.4 2.5 %collective-permute-start.8 = (bf16[1024,128]{1,0:T(8,128)(2,1)S(1)}, bf16[1024,128]{1,0:T(8,128)(2,1)S(1)}, u32[]{:S(2)}, u32[]{:S(2)}) collective-permute-start(bf16[1024,128]{1,0:T(8,128)(2,1)S(1)} %collective-permute-done.7.first), channel_id=1, source_target_pairs={{0,4},{4,0},{8,12},{12,8},{16,20},{20,16},{24,28},{28,24},{1,5},{5... | collective-permute-start | bytes 786440 | tf_op jit(solution)/shard_map/ppermute | solution.py:32
  13.7 1.5 %collective-permute-start.6 = (bf16[1024,128]{1,0:T(8,128)(2,1)S(1)}, bf16[1024,128]{1,0:T(8,128)(2,1)S(1)}, u32[]{:S(2)}, u32[]{:S(2)}) collective-permute-start(bf16[1024,128]{1,0:T(8,128)(2,1)S(1)} %collective-permute-done.2.first), channel_id=1, source_target_pairs={{0,4},{4,0},{8,12},{12,8},{16,20},{20,16},{24,28},{28,24},{1,5},{5... | collective-permute-start | bytes 786440 | tf_op jit(solution)/shard_map/ppermute | solution.py:32
  14.9 1.5 %collective-permute-start.4 = (bf16[1024,128]{1,0:T(8,128)(2,1)S(1)}, bf16[1024,128]{1,0:T(8,128)(2,1)S(1)}, u32[]{:S(2)}, u32[]{:S(2)}) collective-permute-start(bf16[1024,128]{1,0:T(8,128)(2,1)S(1)} %collective-permute-done.3.second), channel_id=1, source_target_pairs={{0,4},{4,0},{8,12},{12,8},{16,20},{20,16},{24,28},{28,24},{1,5},{5... | collective-permute-start | bytes 786440 | tf_op jit(solution)/shard_map/ppermute | solution.py:32
  15.5 1.0 %copy-start = (bf16[64,16,128]{2,1,0:T(8,128)(2,1)S(1)}, bf16[64,16,128]{2,1,0:T(8,128)(2,1)}, u32[]{:S(2)}) copy-start(bf16[64,16,128]{2,1,0:T(8,128)(2,1)} %param.3) | copy-start | bytes 786436

commit v4 on v3

--- a/solution.py
+++ b/solution.py
@@ -17,16 +17,17 @@
 
     def place(self, count):
         me = lax.axis_index("gx")
-        at = me ^ jnp.where((me & 1) == 0, self.even, self.odd)
+        bits = sum((me >> b) & 1 for b in range(count.bit_length() - 1))
+        at = me ^ jnp.where((bits & 1) == 0, self.even, self.odd)
         upper = (at >= count // 2).astype(jnp.int32)
         block = jnp.where(upper == 1, count - 1 - at, at)
         return upper, lax.axis_index("gz") ^ block
 
 
 def send(block, even, odd, count):
-    pairs = [(g, g ^ (odd if g & 1 else even)) for g in range(count)]
-    if even & 1:
-        offsets = odd ^ block.odd, even ^ block.even
+    pairs = [(g, g ^ (odd if g.bit_count() & 1 else even)) for g in range(count)]
+    if even.bit_count() & 1:
+        offsets = even ^ block.odd, odd ^ block.even
     else:
         offsets = even ^ block.even, odd ^ block.odd
     return Block(lax.ppermute(block.value, "gx", pairs), *offsets)
@@ -156,7 +157,7 @@
         if steps:
             vectors = widen(vectors, steps.pop(0))
             near[0] = after(near[0], vectors)
-        across = [send(block, a, b, count) for block in near] if crossed else []
+        across = [send(block, b, a, count) for block in near] if crossed else []
         held += near + far + across
         masks = masks[2:]
     for step in steps:

time: 18 us -> 17.8 us (0.989)
  starting transfers between devices: 11.2 us -> 10.6 us
  waiting for transfers between devices: 2.51 us -> 2.9 us
    ppermute x2, waiting for transfers between devices: 1.04 us -> 2.34 us  [widen(): return jnp.concatenate((vectors, lax.ppermute(vectors, 'gz', pairs)))]
    ppermute x7, waiting for transfers between devices: 1.47 us -> 0.55 us  [send(): return Block(lax.ppermute(block.value, 'gx', pairs), *offsets)]
    ppermute x7, starting transfers between devices: 7.03 us -> 6.37 us  [send(): return Block(lax.ppermute(block.value, 'gx', pairs), *offsets)]
  transfers between devices with their start and end apart: 9 -> 9, of which waited for: 5 -> 4; matrix products, arithmetic and copies ran while one was open for 4% -> 4% of each run, Pallas kernels for 7% -> 7%
where the time goes in v4:
time: 17.8 us; the launch traced here: 17.6 us
  starting transfers between devices  10.6 us (60%)
  waiting for transfers between devices  2.9 us (16%)
  Pallas kernels  2.52 us (14%)
  other arithmetic  0.75 us (4%)
  between operations  0.68 us (4%)
    ppermute x7, starting transfers between devices, send(): return Block(lax.ppermute(block.value, 'gx', pairs), *offsets)  6.37 us
    ppermute x2, starting transfers between devices, widen(): return jnp.concatenate((vectors, lax.ppermute(vectors, 'gz', pairs)))  4.23 us
    ppermute x2, waiting for transfers between devices, widen(): return jnp.concatenate((vectors, lax.ppermute(vectors, 'gz', pairs)))  2.34 us
    pallas_call x2, Pallas kernels, combine(): pl.pallas_call(functools.partial(combine_kernel, places, planes, last), o...  1.97 us
    broadcast_in_dim x1, other arithmetic, local(): vectors = jnp.stack((even_vectors, odd_vectors))[None]  0.72 us
    ppermute x7, waiting for transfers between devices, send(): return Block(lax.ppermute(block.value, 'gx', pairs), *offsets)  0.55 us
    pallas_call x2, Pallas kernels, prepare(): pl.pallas_call(functools.partial(prepare_kernel, functools.partial(pair[0...  0.54 us
  transfers between devices with their start and end apart: 9, of which 4 were waited for; matrix products, arithmetic and copies ran while one was open for 4% of the time, Pallas kernels for 7%

profile of v4, /device:TPU:0, one launch (start us, length us, event | category | flops | bytes accessed | tf_op | source)
XLA Modules:
  0.0 17.6 jit_solution(498845304984816842)
XLA Ops:
  0.6 2.4 %collective-permute-start.2 = (bf16[1024,128]{1,0:T(8,128)(2,1)}, bf16[1024,128]{1,0:T(8,128)(2,1)S(1)}, u32[]{:S(2)}, u32[]{:S(2)}) collective-permute-start(bf16[1024,128]{1,0:T(8,128)(2,1)} %bitcast.7), channel_id=1, source_target_pairs={{0,12},{4,16},{8,28},{12,0},{16,4},{20,24},{24,20},{28,8},{1,13},{... | collective-permute-start | bytes 786440 | tf_op jit(solution)/shard_map/ppermute | solution.py:33
  3.1 0.7 %maximum_bitcast_fusion = bf16[1,2,32,64]{3,2,1,0:T(8,128)(2,1)S(1)} fusion(bf16[1,32,64]{2,1,0:T(8,128)(2,1)} %bitcast.11, bf16[1,32,64]{2,1,0:T(8,128)(2,1)} %bitcast.12), kind=kLoop, calls=%fused_computation.2 | loop fusion | flops 4096 | bytes 16384 | tf_op jit(solution)/shard_map/broadcast_in_dim | solution.py:149
  3.8 1.6 %collective-permute-start = (bf16[1,2,32,64]{3,2,1,0:T(8,128)(2,1)S(1)}, bf16[1,2,32,64]{3,2,1,0:T(8,128)(2,1)S(1)}, u32[]{:S(2)}, u32[]{:S(2)}) collective-permute-start(bf16[1,2,32,64]{3,2,1,0:T(8,128)(2,1)S(1)} %maximum_bitcast_fusion), channel_id=1, source_target_pairs={{0,1},{1,0},{2,3},{3,2},{4,5},{5,4},{6,7},{7,6},{8,9},{9,8},{10,11... | collective-permute-start | bytes 24584 | tf_op jit(solution)/shard_map/ppermute | solution.py:143
  5.4 0.4 %collective-permute-start.5 = (bf16[1024,128]{1,0:T(8,128)(2,1)}, bf16[1024,128]{1,0:T(8,128)(2,1)S(1)}, u32[]{:S(2)}, u32[]{:S(2)}) collective-permute-start(bf16[1024,128]{1,0:T(8,128)(2,1)} %bitcast.8), channel_id=1, source_target_pairs={{0,4},{4,0},{8,12},{12,8},{16,20},{20,16},{24,28},{28,24},{1,5},{5... | collective-permute-start | bytes 786440 | tf_op jit(solution)/shard_map/ppermute | solution.py:33
  5.8 1.1 %collective-permute-start.7 = (bf16[1024,128]{1,0:T(8,128)(2,1)}, bf16[1024,128]{1,0:T(8,128)(2,1)S(1)}, u32[]{:S(2)}, u32[]{:S(2)}) collective-permute-start(bf16[1024,128]{1,0:T(8,128)(2,1)} %bitcast.9), channel_id=1, source_target_pairs={{0,20},{4,8},{8,4},{12,24},{16,28},{20,0},{24,12},{28,16},{1,21},{... | collective-permute-start | bytes 786440 | tf_op jit(solution)/shard_map/ppermute | solution.py:33
  6.9 0.6 %collective-permute-done = bf16[1,2,32,64]{3,2,1,0:T(8,128)(2,1)S(1)} collective-permute-done((bf16[1,2,32,64]{3,2,1,0:T(8,128)(2,1)S(1)}, bf16[1,2,32,64]{3,2,1,0:T(8,128)(2,1)S(1)}, u32[]{:S(2)}, u32[]{:S(2)}) %collective-permute-start) | collective-permute-done | bytes 8224 | tf_op jit(solution)/shard_map/ppermute | solution.py:143
  7.6 0.0 collective-permute-done.2.first
  7.6 1.8 %collective-permute-start.3 = (bf16[1024,128]{1,0:T(8,128)(2,1)S(1)}, bf16[1024,128]{1,0:T(8,128)(2,1)S(1)}, u32[]{:S(2)}, u32[]{:S(2)}) collective-permute-start(bf16[1024,128]{1,0:T(8,128)(2,1)S(1)} %collective-permute-done.2.first), channel_id=1, source_target_pairs={{0,20},{4,8},{8,4},{12,24},{16,28},{20,0},{24,12},{28,16},{1,21},{... | collective-permute-start | bytes 786440 | tf_op jit(solution)/shard_map/ppermute | solution.py:33
  9.4 2.6 %collective-permute-start.1 = (bf16[2,2,32,64]{3,2,1,0:T(8,128)(2,1)S(1)}, bf16[2,2,32,64]{3,2,1,0:T(8,128)(2,1)S(1)}, u32[]{:S(2)}, u32[]{:S(2)}) collective-permute-start(bf16[2,2,32,64]{3,2,1,0:T(8,128)(2,1)S(1)} %pad_maximum_fusion.1), channel_id=1, source_target_pairs={{0,2},{1,3},{2,0},{3,1},{4,6},{5,7},{6,4},{7,5},{8,10},{9,11},{10,... | collective-permute-start | bytes 49160 | tf_op jit(solution)/shard_map/ppermute | solution.py:143
  12.0 0.0 collective-permute-done.5.first
  12.0 0.0 collective-permute-done.7.first
  12.0 0.2 %collective-permute-start.8 = (bf16[1024,128]{1,0:T(8,128)(2,1)S(1)}, bf16[1024,128]{1,0:T(8,128)(2,1)S(1)}, u32[]{:S(2)}, u32[]{:S(2)}) collective-permute-start(bf16[1024,128]{1,0:T(8,128)(2,1)S(1)} %collective-permute-done.7.first), channel_id=1, source_target_pairs={{0,4},{4,0},{8,12},{12,8},{16,20},{20,16},{24,28},{28,24},{1,5},{5... | collective-permute-start | bytes 786440 | tf_op jit(solution)/shard_map/ppermute | solution.py:33
  12.2 0.3 %collective-permute-start.6 = (bf16[1024,128]{1,0:T(8,128)(2,1)S(1)}, bf16[1024,128]{1,0:T(8,128)(2,1)S(1)}, u32[]{:S(2)}, u32[]{:S(2)}) collective-permute-start(bf16[1024,128]{1,0:T(8,128)(2,1)S(1)} %collective-permute-done.2.first), channel_id=1, source_target_pairs={{0,4},{4,0},{8,12},{12,8},{16,20},{20,16},{24,28},{28,24},{1,5},{5... | collective-permute-start | bytes 786440 | tf_op jit(solution)/shard_map/ppermute | solution.py:33
  12.5 1.7 %collective-permute-done.1 = bf16[2,2,32,64]{3,2,1,0:T(8,128)(2,1)S(1)} collective-permute-done((bf16[2,2,32,64]{3,2,1,0:T(8,128)(2,1)S(1)}, bf16[2,2,32,64]{3,2,1,0:T(8,128)(2,1)S(1)}, u32[]{:S(2)}, u32[]{:S(2)}) %collective-permute-start.1) | collective-permute-done | bytes 16416 | tf_op jit(solution)/shard_map/ppermute | solution.py:143
  14.2 0.4 %collective-permute-done.3.second = bf16[1024,128]{1,0:T(8,128)(2,1)S(1)} collective-permute-done((bf16[1024,128]{1,0:T(8,128)(2,1)S(1)}, bf16[1024,128]{1,0:T(8,128)(2,1)S(1)}, u32[]{:S(2)}, u32[]{:S(2)}) %collective-permute-start.3) | collective-permute-done | bytes 262176 | tf_op jit(solution)/shard_map/ppermute | solution.py:33
  14.7 0.1 collective-permute-start.4
  14.8 0.0 collective-permute-done.8.second
  14.8 0.3 %prepare.3 = (bf16[64,2048]{1,0:T(8,128)(2,1)S(1)}, bf16[64,2048]{1,0:T(8,128)(2,1)S(1)}) custom-call(bf16[1024,128]{1,0:T(8,128)(2,1)S(1)} %collective-permute-done.7.first, bf16[1024,128]{1,0:T(8,128)(2,1)S(1)} %collective-permute-done.8.second), custom_call_target="tpu_custom_call" | custom-call | tf_op jit(solution)/shard_map/prepare/pallas_call | solution.py:70
  15.0 0.0 collective-permute-done.6.second
  15.1 0.3 %prepare.2 = (bf16[64,2048]{1,0:T(8,128)(2,1)S(1)}, bf16[64,2048]{1,0:T(8,128)(2,1)S(1)}) custom-call(bf16[1024,128]{1,0:T(8,128)(2,1)S(1)} %collective-permute-done.2.first, bf16[1024,128]{1,0:T(8,128)(2,1)S(1)} %collective-permute-done.6.second), custom_call_target="tpu_custom_call" | custom-call | tf_op jit(solution)/shard_map/prepare/pallas_call | solution.py:70
  15.4 0.0 copy-start
  15.4 0.7 %combine.1.refs_0_ = f32[2,32,2048]{2,1,0:T(8,128)S(1)} custom-call(bf16[4,2,32,64]{3,2,1,0:T(8,128)(2,1)S(1)} %pad_maximum_fusion.vectors, bf16[1024,128]{1,0:T(8,128)(2,1)S(1)} %collective-permute-done.5.first, bf16[1024,128]{1,0:T(8,128)(2,1)S(1)} %collective-permute-done.3.second, bf16[64,2048]{1,0:T(8,128)(2,1)S(1)} %get-tuple-element.15.refs_0_, ...), custom_call_target="tpu_custom_call" | custom-call | tf_op jit(solution)/shard_map/combine/pallas_call | solution.py:123
  16.1 0.1 collective-permute-done.4.second
  16.2 0.1 copy-done
  16.3 1.3 %finish.1 = (f32[512,128]{1,0:T(8,128)}, f32[512,128]{1,0:T(8,128)}) custom-call(bf16[4,2,32,64]{3,2,1,0:T(8,128)(2,1)S(1)} %pad_maximum_fusion.vectors, bf16[1024,128]{1,0:T(8,128)(2,1)S(1)} %bitcast.10, bf16[1024,128]{1,0:T(8,128)(2,1)S(1)} %collective-permute-done.4.second, f32[2,32,2048]{2,1,0:T(8,128)S(1)} %combine.1.refs_0_), custom_call_target="tpu_custom_call" | custom-call | tf_op jit(solution)/shard_map/finish/pallas_call | solution.py:123
  (2 shorter events, 0.0 us)
Async XLA Ops:
  0.6 7.0 %collective-permute-start.2 = (bf16[1024,128]{1,0:T(8,128)(2,1)}, bf16[1024,128]{1,0:T(8,128)(2,1)S(1)}, u32[]{:S(2)}, u32[]{:S(2)}) collective-permute-start(bf16[1024,128]{1,0:T(8,128)(2,1)} %bitcast.7), channel_id=1, source_target_pairs={{0,12},{4,16},{8,28},{12,0},{16,4},{20,24},{24,20},{28,8},{1,13},{... | collective-permute-start | bytes 786440 | tf_op jit(solution)/shard_map/ppermute | solution.py:33
  3.8 3.8 %collective-permute-start = (bf16[1,2,32,64]{3,2,1,0:T(8,128)(2,1)S(1)}, bf16[1,2,32,64]{3,2,1,0:T(8,128)(2,1)S(1)}, u32[]{:S(2)}, u32[]{:S(2)}) collective-permute-start(bf16[1,2,32,64]{3,2,1,0:T(8,128)(2,1)S(1)} %maximum_bitcast_fusion), channel_id=1, source_target_pairs={{0,1},{1,0},{2,3},{3,2},{4,5},{5,4},{6,7},{7,6},{8,9},{9,8},{10,11... | collective-permute-start | bytes 24584 | tf_op jit(solution)/shard_map/ppermute | solution.py:143
  5.4 6.6 %collective-permute-start.5 = (bf16[1024,128]{1,0:T(8,128)(2,1)}, bf16[1024,128]{1,0:T(8,128)(2,1)S(1)}, u32[]{:S(2)}, u32[]{:S(2)}) collective-permute-start(bf16[1024,128]{1,0:T(8,128)(2,1)} %bitcast.8), channel_id=1, source_target_pairs={{0,4},{4,0},{8,12},{12,8},{16,20},{20,16},{24,28},{28,24},{1,5},{5... | collective-permute-start | bytes 786440 | tf_op jit(solution)/shard_map/ppermute | solution.py:33
  5.8 6.2 %collective-permute-start.7 = (bf16[1024,128]{1,0:T(8,128)(2,1)}, bf16[1024,128]{1,0:T(8,128)(2,1)S(1)}, u32[]{:S(2)}, u32[]{:S(2)}) collective-permute-start(bf16[1024,128]{1,0:T(8,128)(2,1)} %bitcast.9), channel_id=1, source_target_pairs={{0,20},{4,8},{8,4},{12,24},{16,28},{20,0},{24,12},{28,16},{1,21},{... | collective-permute-start | bytes 786440 | tf_op jit(solution)/shard_map/ppermute | solution.py:33
  7.6 7.1 %collective-permute-start.3 = (bf16[1024,128]{1,0:T(8,128)(2,1)S(1)}, bf16[1024,128]{1,0:T(8,128)(2,1)S(1)}, u32[]{:S(2)}, u32[]{:S(2)}) collective-permute-start(bf16[1024,128]{1,0:T(8,128)(2,1)S(1)} %collective-permute-done.2.first), channel_id=1, source_target_pairs={{0,20},{4,8},{8,4},{12,24},{16,28},{20,0},{24,12},{28,16},{1,21},{... | collective-permute-start | bytes 786440 | tf_op jit(solution)/shard_map/ppermute | solution.py:33
  9.4 4.8 %collective-permute-start.1 = (bf16[2,2,32,64]{3,2,1,0:T(8,128)(2,1)S(1)}, bf16[2,2,32,64]{3,2,1,0:T(8,128)(2,1)S(1)}, u32[]{:S(2)}, u32[]{:S(2)}) collective-permute-start(bf16[2,2,32,64]{3,2,1,0:T(8,128)(2,1)S(1)} %pad_maximum_fusion.1), channel_id=1, source_target_pairs={{0,2},{1,3},{2,0},{3,1},{4,6},{5,7},{6,4},{7,5},{8,10},{9,11},{10,... | collective-permute-start | bytes 49160 | tf_op jit(solution)/shard_map/ppermute | solution.py:143
  12.0 2.8 %collective-permute-start.8 = (bf16[1024,128]{1,0:T(8,128)(2,1)S(1)}, bf16[1024,128]{1,0:T(8,128)(2,1)S(1)}, u32[]{:S(2)}, u32[]{:S(2)}) collective-permute-start(bf16[1024,128]{1,0:T(8,128)(2,1)S(1)} %collective-permute-done.7.first), channel_id=1, source_target_pairs={{0,4},{4,0},{8,12},{12,8},{16,20},{20,16},{24,28},{28,24},{1,5},{5... | collective-permute-start | bytes 786440 | tf_op jit(solution)/shard_map/ppermute | solution.py:33
  12.2 2.8 %collective-permute-start.6 = (bf16[1024,128]{1,0:T(8,128)(2,1)S(1)}, bf16[1024,128]{1,0:T(8,128)(2,1)S(1)}, u32[]{:S(2)}, u32[]{:S(2)}) collective-permute-start(bf16[1024,128]{1,0:T(8,128)(2,1)S(1)} %collective-permute-done.2.first), channel_id=1, source_target_pairs={{0,4},{4,0},{8,12},{12,8},{16,20},{20,16},{24,28},{28,24},{1,5},{5... | collective-permute-start | bytes 786440 | tf_op jit(solution)/shard_map/ppermute | solution.py:33
  14.7 1.5 %collective-permute-start.4 = (bf16[1024,128]{1,0:T(8,128)(2,1)S(1)}, bf16[1024,128]{1,0:T(8,128)(2,1)S(1)}, u32[]{:S(2)}, u32[]{:S(2)}) collective-permute-start(bf16[1024,128]{1,0:T(8,128)(2,1)S(1)} %collective-permute-done.3.second), channel_id=1, source_target_pairs={{0,4},{4,0},{8,12},{12,8},{16,20},{20,16},{24,28},{28,24},{1,5},{5... | collective-permute-start | bytes 786440 | tf_op jit(solution)/shard_map/ppermute | solution.py:33
  15.4 1.0 %copy-start = (bf16[64,16,128]{2,1,0:T(8,128)(2,1)S(1)}, bf16[64,16,128]{2,1,0:T(8,128)(2,1)}, u32[]{:S(2)}) copy-start(bf16[64,16,128]{2,1,0:T(8,128)(2,1)} %param.3) | copy-start | bytes 786436

commit v5 on v4

--- a/solution.py
+++ b/solution.py
@@ -41,10 +41,10 @@
         for j in range(0, rows, CHUNK):
             evens, odds = [], []
             for i in range(j, j + CHUNK):
-                a = low[pl.ds(i * planes, planes), :].astype(jnp.float32)
-                b = high[pl.ds((rows - 1 - i) * planes, planes), :].astype(jnp.float32)
-                evens.append((a + b).astype(jnp.bfloat16))
-                odds.append((a - b).astype(jnp.bfloat16))
+                a = low[pl.ds(i * planes, planes), :]
+                b = high[pl.ds((rows - 1 - i) * planes, planes), :]
+                evens.append(a + b)
+                odds.append(a - b)
             for part, ref in ((evens, even), (odds, odd)):
                 part = jnp.swapaxes(jnp.stack(part), 0, 1)
                 for y in range(planes):

time: 17.8 us -> 17.7 us (level)
  Pallas kernels: 2.52 us -> 2.31 us
  transfers between devices with their start and end apart: 9 -> 9, of which waited for: 4 -> 4; matrix products, arithmetic and copies ran while one was open for 4% -> 4% of each run, Pallas kernels for 7% -> 6%
where the time goes in v5:
time: 17.7 us; the launch traced here: 17.4 us
  starting transfers between devices  10.6 us (60%)
  waiting for transfers between devices  3.05 us (17%)
  Pallas kernels  2.31 us (13%)
  other arithmetic  0.75 us (4%)
  between operations  0.68 us (4%)
    ppermute x7, starting transfers between devices, send(): return Block(lax.ppermute(block.value, 'gx', pairs), *offsets)  6.37 us
    ppermute x2, starting transfers between devices, widen(): return jnp.concatenate((vectors, lax.ppermute(vectors, 'gz', pairs)))  4.23 us
    ppermute x2, waiting for transfers between devices, widen(): return jnp.concatenate((vectors, lax.ppermute(vectors, 'gz', pairs)))  2.34 us
    pallas_call x2, Pallas kernels, combine(): pl.pallas_call(functools.partial(combine_kernel, places, planes, last), o...  1.87 us
    broadcast_in_dim x1, other arithmetic, local(): vectors = jnp.stack((even_vectors, odd_vectors))[None]  0.72 us
    ppermute x7, waiting for transfers between devices, send(): return Block(lax.ppermute(block.value, 'gx', pairs), *offsets)  0.71 us
    pallas_call x2, Pallas kernels, prepare(): pl.pallas_call(functools.partial(prepare_kernel, functools.partial(pair[0...  0.44 us
  transfers between devices with their start and end apart: 9, of which 4 were waited for; matrix products, arithmetic and copies ran while one was open for 4% of the time, Pallas kernels for 6%

profile of v5, /device:TPU:0, one launch (start us, length us, event | category | flops | bytes accessed | tf_op | source)
XLA Modules:
  0.0 17.4 jit_solution(13306319168950737825)
XLA Ops:
  0.6 2.4 %collective-permute-start.2 = (bf16[1024,128]{1,0:T(8,128)(2,1)}, bf16[1024,128]{1,0:T(8,128)(2,1)S(1)}, u32[]{:S(2)}, u32[]{:S(2)}) collective-permute-start(bf16[1024,128]{1,0:T(8,128)(2,1)} %bitcast.7), channel_id=1, source_target_pairs={{0,12},{4,16},{8,28},{12,0},{16,4},{20,24},{24,20},{28,8},{1,13},{... | collective-permute-start | bytes 786440 | tf_op jit(solution)/shard_map/ppermute | solution.py:33
  3.1 0.7 %maximum_bitcast_fusion = bf16[1,2,32,64]{3,2,1,0:T(8,128)(2,1)S(1)} fusion(bf16[1,32,64]{2,1,0:T(8,128)(2,1)} %bitcast.11, bf16[1,32,64]{2,1,0:T(8,128)(2,1)} %bitcast.12), kind=kLoop, calls=%fused_computation.2 | loop fusion | flops 4096 | bytes 16384 | tf_op jit(solution)/shard_map/broadcast_in_dim | solution.py:149
  3.8 1.6 %collective-permute-start = (bf16[1,2,32,64]{3,2,1,0:T(8,128)(2,1)S(1)}, bf16[1,2,32,64]{3,2,1,0:T(8,128)(2,1)S(1)}, u32[]{:S(2)}, u32[]{:S(2)}) collective-permute-start(bf16[1,2,32,64]{3,2,1,0:T(8,128)(2,1)S(1)} %maximum_bitcast_fusion), channel_id=1, source_target_pairs={{0,1},{1,0},{2,3},{3,2},{4,5},{5,4},{6,7},{7,6},{8,9},{9,8},{10,11... | collective-permute-start | bytes 24584 | tf_op jit(solution)/shard_map/ppermute | solution.py:143
  5.4 0.4 %collective-permute-start.5 = (bf16[1024,128]{1,0:T(8,128)(2,1)}, bf16[1024,128]{1,0:T(8,128)(2,1)S(1)}, u32[]{:S(2)}, u32[]{:S(2)}) collective-permute-start(bf16[1024,128]{1,0:T(8,128)(2,1)} %bitcast.8), channel_id=1, source_target_pairs={{0,4},{4,0},{8,12},{12,8},{16,20},{20,16},{24,28},{28,24},{1,5},{5... | collective-permute-start | bytes 786440 | tf_op jit(solution)/shard_map/ppermute | solution.py:33
  5.8 1.1 %collective-permute-start.7 = (bf16[1024,128]{1,0:T(8,128)(2,1)}, bf16[1024,128]{1,0:T(8,128)(2,1)S(1)}, u32[]{:S(2)}, u32[]{:S(2)}) collective-permute-start(bf16[1024,128]{1,0:T(8,128)(2,1)} %bitcast.9), channel_id=1, source_target_pairs={{0,20},{4,8},{8,4},{12,24},{16,28},{20,0},{24,12},{28,16},{1,21},{... | collective-permute-start | bytes 786440 | tf_op jit(solution)/shard_map/ppermute | solution.py:33
  6.9 0.6 %collective-permute-done = bf16[1,2,32,64]{3,2,1,0:T(8,128)(2,1)S(1)} collective-permute-done((bf16[1,2,32,64]{3,2,1,0:T(8,128)(2,1)S(1)}, bf16[1,2,32,64]{3,2,1,0:T(8,128)(2,1)S(1)}, u32[]{:S(2)}, u32[]{:S(2)}) %collective-permute-start) | collective-permute-done | bytes 8224 | tf_op jit(solution)/shard_map/ppermute | solution.py:143
  7.6 0.0 collective-permute-done.2.first
  7.6 1.8 %collective-permute-start.3 = (bf16[1024,128]{1,0:T(8,128)(2,1)S(1)}, bf16[1024,128]{1,0:T(8,128)(2,1)S(1)}, u32[]{:S(2)}, u32[]{:S(2)}) collective-permute-start(bf16[1024,128]{1,0:T(8,128)(2,1)S(1)} %collective-permute-done.2.first), channel_id=1, source_target_pairs={{0,20},{4,8},{8,4},{12,24},{16,28},{20,0},{24,12},{28,16},{1,21},{... | collective-permute-start | bytes 786440 | tf_op jit(solution)/shard_map/ppermute | solution.py:33
  9.4 2.6 %collective-permute-start.1 = (bf16[2,2,32,64]{3,2,1,0:T(8,128)(2,1)S(1)}, bf16[2,2,32,64]{3,2,1,0:T(8,128)(2,1)S(1)}, u32[]{:S(2)}, u32[]{:S(2)}) collective-permute-start(bf16[2,2,32,64]{3,2,1,0:T(8,128)(2,1)S(1)} %pad_maximum_fusion.1), channel_id=1, source_target_pairs={{0,2},{1,3},{2,0},{3,1},{4,6},{5,7},{6,4},{7,5},{8,10},{9,11},{10,... | collective-permute-start | bytes 49160 | tf_op jit(solution)/shard_map/ppermute | solution.py:143
  12.0 0.0 collective-permute-done.5.first
  12.0 0.0 collective-permute-done.7.first
  12.0 0.2 %collective-permute-start.8 = (bf16[1024,128]{1,0:T(8,128)(2,1)S(1)}, bf16[1024,128]{1,0:T(8,128)(2,1)S(1)}, u32[]{:S(2)}, u32[]{:S(2)}) collective-permute-start(bf16[1024,128]{1,0:T(8,128)(2,1)S(1)} %collective-permute-done.7.first), channel_id=1, source_target_pairs={{0,4},{4,0},{8,12},{12,8},{16,20},{20,16},{24,28},{28,24},{1,5},{5... | collective-permute-start | bytes 786440 | tf_op jit(solution)/shard_map/ppermute | solution.py:33
  12.2 0.3 %collective-permute-start.6 = (bf16[1024,128]{1,0:T(8,128)(2,1)S(1)}, bf16[1024,128]{1,0:T(8,128)(2,1)S(1)}, u32[]{:S(2)}, u32[]{:S(2)}) collective-permute-start(bf16[1024,128]{1,0:T(8,128)(2,1)S(1)} %collective-permute-done.2.first), channel_id=1, source_target_pairs={{0,4},{4,0},{8,12},{12,8},{16,20},{20,16},{24,28},{28,24},{1,5},{5... | collective-permute-start | bytes 786440 | tf_op jit(solution)/shard_map/ppermute | solution.py:33
  12.5 1.7 %collective-permute-done.1 = bf16[2,2,32,64]{3,2,1,0:T(8,128)(2,1)S(1)} collective-permute-done((bf16[2,2,32,64]{3,2,1,0:T(8,128)(2,1)S(1)}, bf16[2,2,32,64]{3,2,1,0:T(8,128)(2,1)S(1)}, u32[]{:S(2)}, u32[]{:S(2)}) %collective-permute-start.1) | collective-permute-done | bytes 16416 | tf_op jit(solution)/shard_map/ppermute | solution.py:143
  14.2 0.4 %collective-permute-done.3.second = bf16[1024,128]{1,0:T(8,128)(2,1)S(1)} collective-permute-done((bf16[1024,128]{1,0:T(8,128)(2,1)S(1)}, bf16[1024,128]{1,0:T(8,128)(2,1)S(1)}, u32[]{:S(2)}, u32[]{:S(2)}) %collective-permute-start.3) | collective-permute-done | bytes 262176 | tf_op jit(solution)/shard_map/ppermute | solution.py:33
  14.7 0.1 collective-permute-start.4
  14.8 0.0 collective-permute-done.8.second
  14.8 0.2 %prepare.3 = (bf16[64,2048]{1,0:T(8,128)(2,1)S(1)}, bf16[64,2048]{1,0:T(8,128)(2,1)S(1)}) custom-call(bf16[1024,128]{1,0:T(8,128)(2,1)S(1)} %collective-permute-done.7.first, bf16[1024,128]{1,0:T(8,128)(2,1)S(1)} %collective-permute-done.8.second), custom_call_target="tpu_custom_call" | custom-call | tf_op jit(solution)/shard_map/prepare/pallas_call | solution.py:70
  15.0 0.0 collective-permute-done.6.second
  15.0 0.2 %prepare.2 = (bf16[64,2048]{1,0:T(8,128)(2,1)S(1)}, bf16[64,2048]{1,0:T(8,128)(2,1)S(1)}) custom-call(bf16[1024,128]{1,0:T(8,128)(2,1)S(1)} %collective-permute-done.2.first, bf16[1024,128]{1,0:T(8,128)(2,1)S(1)} %collective-permute-done.6.second), custom_call_target="tpu_custom_call" | custom-call | tf_op jit(solution)/shard_map/prepare/pallas_call | solution.py:70
  15.3 0.0 copy-start
  15.3 0.7 %combine.1.refs_0_ = f32[2,32,2048]{2,1,0:T(8,128)S(1)} custom-call(bf16[4,2,32,64]{3,2,1,0:T(8,128)(2,1)S(1)} %pad_maximum_fusion.vectors, bf16[1024,128]{1,0:T(8,128)(2,1)S(1)} %collective-permute-done.5.first, bf16[1024,128]{1,0:T(8,128)(2,1)S(1)} %collective-permute-done.3.second, bf16[64,2048]{1,0:T(8,128)(2,1)S(1)} %get-tuple-element.15.refs_0_, ...), custom_call_target="tpu_custom_call" | custom-call | tf_op jit(solution)/shard_map/combine/pallas_call | solution.py:123
  15.9 0.3 %collective-permute-done.4.second = bf16[1024,128]{1,0:T(8,128)(2,1)S(1)} collective-permute-done((bf16[1024,128]{1,0:T(8,128)(2,1)S(1)}, bf16[1024,128]{1,0:T(8,128)(2,1)S(1)}, u32[]{:S(2)}, u32[]{:S(2)}) %collective-permute-start.4) | collective-permute-done | bytes 262176 | tf_op jit(solution)/shard_map/ppermute | solution.py:33
  16.2 0.0 copy-done
  16.2 1.2 %finish.1 = (f32[512,128]{1,0:T(8,128)}, f32[512,128]{1,0:T(8,128)}) custom-call(bf16[4,2,32,64]{3,2,1,0:T(8,128)(2,1)S(1)} %pad_maximum_fusion.vectors, bf16[1024,128]{1,0:T(8,128)(2,1)S(1)} %bitcast.10, bf16[1024,128]{1,0:T(8,128)(2,1)S(1)} %collective-permute-done.4.second, f32[2,32,2048]{2,1,0:T(8,128)S(1)} %combine.1.refs_0_), custom_call_target="tpu_custom_call" | custom-call | tf_op jit(solution)/shard_map/finish/pallas_call | solution.py:123
  (2 shorter events, 0.0 us)
Async XLA Ops:
  0.6 7.0 %collective-permute-start.2 = (bf16[1024,128]{1,0:T(8,128)(2,1)}, bf16[1024,128]{1,0:T(8,128)(2,1)S(1)}, u32[]{:S(2)}, u32[]{:S(2)}) collective-permute-start(bf16[1024,128]{1,0:T(8,128)(2,1)} %bitcast.7), channel_id=1, source_target_pairs={{0,12},{4,16},{8,28},{12,0},{16,4},{20,24},{24,20},{28,8},{1,13},{... | collective-permute-start | bytes 786440 | tf_op jit(solution)/shard_map/ppermute | solution.py:33
  3.8 3.8 %collective-permute-start = (bf16[1,2,32,64]{3,2,1,0:T(8,128)(2,1)S(1)}, bf16[1,2,32,64]{3,2,1,0:T(8,128)(2,1)S(1)}, u32[]{:S(2)}, u32[]{:S(2)}) collective-permute-start(bf16[1,2,32,64]{3,2,1,0:T(8,128)(2,1)S(1)} %maximum_bitcast_fusion), channel_id=1, source_target_pairs={{0,1},{1,0},{2,3},{3,2},{4,5},{5,4},{6,7},{7,6},{8,9},{9,8},{10,11... | collective-permute-start | bytes 24584 | tf_op jit(solution)/shard_map/ppermute | solution.py:143
  5.4 6.6 %collective-permute-start.5 = (bf16[1024,128]{1,0:T(8,128)(2,1)}, bf16[1024,128]{1,0:T(8,128)(2,1)S(1)}, u32[]{:S(2)}, u32[]{:S(2)}) collective-permute-start(bf16[1024,128]{1,0:T(8,128)(2,1)} %bitcast.8), channel_id=1, source_target_pairs={{0,4},{4,0},{8,12},{12,8},{16,20},{20,16},{24,28},{28,24},{1,5},{5... | collective-permute-start | bytes 786440 | tf_op jit(solution)/shard_map/ppermute | solution.py:33
  5.8 6.2 %collective-permute-start.7 = (bf16[1024,128]{1,0:T(8,128)(2,1)}, bf16[1024,128]{1,0:T(8,128)(2,1)S(1)}, u32[]{:S(2)}, u32[]{:S(2)}) collective-permute-start(bf16[1024,128]{1,0:T(8,128)(2,1)} %bitcast.9), channel_id=1, source_target_pairs={{0,20},{4,8},{8,4},{12,24},{16,28},{20,0},{24,12},{28,16},{1,21},{... | collective-permute-start | bytes 786440 | tf_op jit(solution)/shard_map/ppermute | solution.py:33
  7.6 7.1 %collective-permute-start.3 = (bf16[1024,128]{1,0:T(8,128)(2,1)S(1)}, bf16[1024,128]{1,0:T(8,128)(2,1)S(1)}, u32[]{:S(2)}, u32[]{:S(2)}) collective-permute-start(bf16[1024,128]{1,0:T(8,128)(2,1)S(1)} %collective-permute-done.2.first), channel_id=1, source_target_pairs={{0,20},{4,8},{8,4},{12,24},{16,28},{20,0},{24,12},{28,16},{1,21},{... | collective-permute-start | bytes 786440 | tf_op jit(solution)/shard_map/ppermute | solution.py:33
  9.4 4.8 %collective-permute-start.1 = (bf16[2,2,32,64]{3,2,1,0:T(8,128)(2,1)S(1)}, bf16[2,2,32,64]{3,2,1,0:T(8,128)(2,1)S(1)}, u32[]{:S(2)}, u32[]{:S(2)}) collective-permute-start(bf16[2,2,32,64]{3,2,1,0:T(8,128)(2,1)S(1)} %pad_maximum_fusion.1), channel_id=1, source_target_pairs={{0,2},{1,3},{2,0},{3,1},{4,6},{5,7},{6,4},{7,5},{8,10},{9,11},{10,... | collective-permute-start | bytes 49160 | tf_op jit(solution)/shard_map/ppermute | solution.py:143
  12.0 2.8 %collective-permute-start.8 = (bf16[1024,128]{1,0:T(8,128)(2,1)S(1)}, bf16[1024,128]{1,0:T(8,128)(2,1)S(1)}, u32[]{:S(2)}, u32[]{:S(2)}) collective-permute-start(bf16[1024,128]{1,0:T(8,128)(2,1)S(1)} %collective-permute-done.7.first), channel_id=1, source_target_pairs={{0,4},{4,0},{8,12},{12,8},{16,20},{20,16},{24,28},{28,24},{1,5},{5... | collective-permute-start | bytes 786440 | tf_op jit(solution)/shard_map/ppermute | solution.py:33
  12.2 2.8 %collective-permute-start.6 = (bf16[1024,128]{1,0:T(8,128)(2,1)S(1)}, bf16[1024,128]{1,0:T(8,128)(2,1)S(1)}, u32[]{:S(2)}, u32[]{:S(2)}) collective-permute-start(bf16[1024,128]{1,0:T(8,128)(2,1)S(1)} %collective-permute-done.2.first), channel_id=1, source_target_pairs={{0,4},{4,0},{8,12},{12,8},{16,20},{20,16},{24,28},{28,24},{1,5},{5... | collective-permute-start | bytes 786440 | tf_op jit(solution)/shard_map/ppermute | solution.py:33
  14.7 1.5 %collective-permute-start.4 = (bf16[1024,128]{1,0:T(8,128)(2,1)S(1)}, bf16[1024,128]{1,0:T(8,128)(2,1)S(1)}, u32[]{:S(2)}, u32[]{:S(2)}) collective-permute-start(bf16[1024,128]{1,0:T(8,128)(2,1)S(1)} %collective-permute-done.3.second), channel_id=1, source_target_pairs={{0,4},{4,0},{8,12},{12,8},{16,20},{20,16},{24,28},{28,24},{1,5},{5... | collective-permute-start | bytes 786440 | tf_op jit(solution)/shard_map/ppermute | solution.py:33
  15.3 1.0 %copy-start = (bf16[64,16,128]{2,1,0:T(8,128)(2,1)S(1)}, bf16[64,16,128]{2,1,0:T(8,128)(2,1)}, u32[]{:S(2)}) copy-start(bf16[64,16,128]{2,1,0:T(8,128)(2,1)} %param.3) | copy-start | bytes 786436

commit v6 on v5

--- a/solution.py
+++ b/solution.py
@@ -33,44 +33,47 @@
     return Block(lax.ppermute(block.value, "gx", pairs), *offsets)
 
 
-def parity_lines(first, second, upper, planes, even, odd, start):
+def parity_lines(first, second, planes, even, odd):
     lines, depth = first.shape
     rows = lines // planes
-
-    def spread(low, high):
-        for j in range(0, rows, CHUNK):
-            evens, odds = [], []
-            for i in range(j, j + CHUNK):
-                a = low[pl.ds(i * planes, planes), :]
-                b = high[pl.ds((rows - 1 - i) * planes, planes), :]
-                evens.append(a + b)
-                odds.append(a - b)
-            for part, ref in ((evens, even), (odds, odd)):
-                part = jnp.swapaxes(jnp.stack(part), 0, 1)
-                for y in range(planes):
-                    ref[pl.ds(start + j, CHUNK), pl.ds(y * depth, depth)] = part[y]
-
-    @pl.when(upper == 0)
-    def _():
-        spread(first, second)
-
-    @pl.when(upper != 0)
-    def _():
-        spread(second, first)
-
-
-def prepare_kernel(place, planes, first, second, even, odd):
-    parity_lines(first, second, place()[0], planes, even, odd, 0)
-
-
-def prepare(pair, count, planes):
+    for j in range(0, rows, CHUNK):
+        evens, odds = [], []
+        for i in range(j, j + CHUNK):
+            a = first[pl.ds(i * planes, planes), :]
+            b = second[pl.ds((rows - 1 - i) * planes, planes), :]
+            evens.append(a + b)
+            odds.append(a - b)
+        for part, ref in ((evens, even), (odds, odd)):
+            part = jnp.swapaxes(jnp.stack(part), 0, 1)
+            for y in range(planes):
+                ref[pl.ds(j, CHUNK), pl.ds(y * depth, depth)] = part[y]
+
+
+def oriented(vectors, place):
+    upper, at = place()
+    modes, rows = vectors.shape[2:]
+    row = lax.broadcasted_iota(jnp.int32, (rows, rows), 0)
+    column = lax.broadcasted_iota(jnp.int32, (rows, rows), 1)
+    chosen = jnp.where(upper == 1, rows - 1 - column, column)
+    order = jnp.where(row == chosen, 1.0, 0.0).astype(vectors.dtype)
+    sign = jnp.where(upper == 1, -1.0, 1.0)
+    even, odd = (
+        jnp.dot(vectors[at, parity], order, preferred_element_type=jnp.float32)
+        for parity in (0, 1)
+    )
+    return even.astype(vectors.dtype), (odd * sign).astype(vectors.dtype)
+
+
+def prepare_kernel(planes, first, second, even, odd):
+    parity_lines(first, second, planes, even, odd)
+
+
+def prepare(pair, planes):
     lines, depth = pair[0].value.shape
     shape = jax.ShapeDtypeStruct((lines // planes, planes * depth), jnp.bfloat16)
     vmem = pl.BlockSpec(memory_space=pltpu.VMEM)
     return pl.pallas_call(
-        functools.partial(
-            prepare_kernel, functools.partial(pair[0].place, count), planes
-        ),
+        functools.partial(prepare_kernel, planes),
         out_shape=(shape, shape),
         in_specs=[vmem, vmem],
         out_specs=(vmem, vmem),
@@ -79,56 +82,77 @@
     )(pair[0].value, pair[1].value)
 
 
-def combine_kernel(places, planes, last, vectors, first, second, *refs):
-    ready = 2 * (len(places) - 1)
-    lines, sums, (*outs, even, odd) = refs[:ready], refs[ready], refs[ready + last :]
-    depth = first.shape[1]
-    modes = vectors.shape[2]
-    spots = [place() for place in places]
-    parity_lines(first, second, spots[-1][0], planes, even, odd, 0)
+def combine_kernel(places, planes, vectors, first, second, *refs):
+    *lines, sums, following, even, odd = refs
+    matrices = [oriented(vectors, place) for place in places]
+    for parity in (0, 1):
+        following[parity] = matrices[-1][parity]
+    parity_lines(first, second, planes, even, odd)
     for parity, fresh in enumerate((even, odd)):
-        matrix = jnp.concatenate([vectors[at, parity] for _, at in spots], axis=1)
+        matrix = jnp.concatenate([both[parity] for both in matrices[:-1]], axis=1)
         parts = jnp.concatenate(
             [ref[...] for ref in lines[parity::2]] + [fresh[...]], axis=0
         )
-        result = jnp.dot(matrix, parts, preferred_element_type=jnp.float32)
-        if not last:
-            outs[0][parity] = result
-            continue
-        result = result + sums[parity]
+        sums[parity] = jnp.dot(matrix, parts, preferred_element_type=jnp.float32)
+
+
+def combine(vectors, ready, pair, following, count, planes):
+    first, second = (block.value for block in pair)
+    lines, depth = first.shape
+    rows = lines // planes
+    modes = vectors.shape[2]
+    blocks = [block for block, _ in ready] + [pair[0], following]
+    operands = [vectors, first, second] + [part for _, both in ready for part in both]
+    vmem = pl.BlockSpec(memory_space=pltpu.VMEM)
+    return pl.pallas_call(
+        functools.partial(
+            combine_kernel,
+            [functools.partial(block.place, count) for block in blocks],
+            planes,
+        ),
+        out_shape=(
+            jax.ShapeDtypeStruct((2, modes, planes * depth), jnp.float32),
+            jax.ShapeDtypeStruct((2, modes, rows), vectors.dtype),
+        ),
+        in_specs=[vmem] * len(operands),
+        out_specs=(vmem, vmem),
+        scratch_shapes=[pltpu.VMEM((rows, planes * depth), jnp.bfloat16)] * 2,
+        compiler_params=PARAMS,
+        name="combine",
+    )(*operands)
+
+
+def finish_kernel(planes, matrices, first, second, sums, *refs):
+    *outs, even, odd = refs
+    depth = first.shape[1]
+    modes = matrices.shape[1]
+    parity_lines(first, second, planes, even, odd)
+    for parity, parts in enumerate((even, odd)):
+        result = sums[parity] + jnp.dot(
+            matrices[parity], parts[...], preferred_element_type=jnp.float32
+        )
         for y in range(planes):
             outs[parity][pl.ds(y, modes, stride=planes), :] = result[
                 :, y * depth : (y + 1) * depth
             ]
 
 
-def combine(vectors, pair, count, planes, ready=(), sums=None):
-    last = sums is not None
+def finish(matrices, pair, sums, planes):
     first, second = (block.value for block in pair)
     lines, depth = first.shape
-    rows = lines // planes
-    modes = vectors.shape[2]
-    if last:
-        shape = [jax.ShapeDtypeStruct((modes * planes, depth), jnp.float32)] * 2
-    else:
-        shape = [jax.ShapeDtypeStruct((2, modes, planes * depth), jnp.float32)]
-    operands = [vectors, first, second]
-    for _, parts in ready:
-        operands += parts
-    if last:
-        operands.append(sums)
-    places = [functools.partial(block.place, count) for block, _ in ready]
-    places.append(functools.partial(pair[0].place, count))
+    modes = matrices.shape[1]
+    shape = jax.ShapeDtypeStruct((modes * planes, depth), jnp.float32)
     vmem = pl.BlockSpec(memory_space=pltpu.VMEM)
     return pl.pallas_call(
-        functools.partial(combine_kernel, places, planes, last),
-        out_shape=shape,
-        in_specs=[vmem] * len(operands),
-        out_specs=[vmem] * len(shape),
-        scratch_shapes=[pltpu.VMEM((rows, planes * depth), jnp.bfloat16)] * 2,
+        functools.partial(finish_kernel, planes),
+        out_shape=(shape, shape),
+        in_specs=[vmem] * 4,
+        out_specs=(vmem, vmem),
+        scratch_shapes=[pltpu.VMEM((lines // planes, planes * depth), jnp.bfloat16)]
+        * 2,
         compiler_params=PARAMS,
-        name="finish" if last else "combine",
-    )(*operands)
+        name="finish",
+    )(matrices, first, second, sums)
 
 
 def local(field, even_vectors, odd_vectors):
@@ -181,9 +205,11 @@
         left.remove(j)
         pairs.append((j, i))
     pairs = [(both[i], both[j]) for j, i in sorted(pairs)]
-    ready = [(pair[0], prepare(pair, count, planes)) for pair in pairs[:-2]]
-    (sums,) = combine(vectors, pairs[-2], count, planes, ready)
-    even, odd = combine(vectors, pairs[-1], count, planes, sums=sums)
+    ready = [(pair[0], prepare(pair, planes)) for pair in pairs[:-2]]
+    sums, matrices = combine(
+        vectors, ready, pairs[-2], pairs[-1][0], count, planes
+    )
+    even, odd = finish(matrices, pairs[-1], sums, planes)
     return even.reshape(modes, planes, depth), odd.reshape(modes, planes, depth)
 
 

time: 17.7 us -> 17.7 us (level)
  no operation moved by 1% of the time
where the time goes in v6:
time: 17.7 us; the launch traced here: 17.4 us
  starting transfers between devices  10.6 us (60%)
  waiting for transfers between devices  3.12 us (18%)
  Pallas kernels  2.26 us (13%)
  other arithmetic  0.75 us (4%)
  between operations  0.68 us (4%)
    ppermute x7, starting transfers between devices, send(): return Block(lax.ppermute(block.value, 'gx', pairs), *offsets)  6.37 us
    ppermute x2, starting transfers between devices, widen(): return jnp.concatenate((vectors, lax.ppermute(vectors, 'gz', pairs)))  4.23 us
    ppermute x2, waiting for transfers between devices, widen(): return jnp.concatenate((vectors, lax.ppermute(vectors, 'gz', pairs)))  2.34 us
    pallas_call x1, Pallas kernels, finish(): pl.pallas_call(functools.partial(finish_kernel, planes), out_shape=(shape...  1.21 us
    ppermute x7, waiting for transfers between devices, send(): return Block(lax.ppermute(block.value, 'gx', pairs), *offsets)  0.78 us
    broadcast_in_dim x1, other arithmetic, local(): vectors = jnp.stack((even_vectors, odd_vectors))[None]  0.72 us
    pallas_call x1, Pallas kernels, combine(): pl.pallas_call(functools.partial(combine_kernel, [functools.partial(block...  0.63 us
    pallas_call x2, Pallas kernels, prepare(): pl.pallas_call(functools.partial(prepare_kernel, planes), out_shape=(shap...  0.42 us
  transfers between devices with their start and end apart: 9, of which 4 were waited for; matrix products, arithmetic and copies ran while one was open for 4% of the time, Pallas kernels for 6%

profile of v6, /device:TPU:0, one launch (start us, length us, event | category | flops | bytes accessed | tf_op | source)
XLA Modules:
  0.0 17.4 jit_solution(662403012744448614)
XLA Ops:
  0.6 2.4 %collective-permute-start.3 = (bf16[1024,128]{1,0:T(8,128)(2,1)}, bf16[1024,128]{1,0:T(8,128)(2,1)S(1)}, u32[]{:S(2)}, u32[]{:S(2)}) collective-permute-start(bf16[1024,128]{1,0:T(8,128)(2,1)} %bitcast.7), channel_id=1, source_target_pairs={{0,12},{4,16},{8,28},{12,0},{16,4},{20,24},{24,20},{28,8},{1,13},{... | collective-permute-start | bytes 786440 | tf_op jit(solution)/shard_map/ppermute | solution.py:33
  3.1 0.7 %maximum_bitcast_fusion = bf16[1,2,32,64]{3,2,1,0:T(8,128)(2,1)S(1)} fusion(bf16[1,32,64]{2,1,0:T(8,128)(2,1)} %bitcast.11, bf16[1,32,64]{2,1,0:T(8,128)(2,1)} %bitcast.12), kind=kLoop, calls=%fused_computation.2 | loop fusion | flops 4096 | bytes 16384 | tf_op jit(solution)/shard_map/broadcast_in_dim | solution.py:173
  3.8 1.6 %collective-permute-start = (bf16[1,2,32,64]{3,2,1,0:T(8,128)(2,1)S(1)}, bf16[1,2,32,64]{3,2,1,0:T(8,128)(2,1)S(1)}, u32[]{:S(2)}, u32[]{:S(2)}) collective-permute-start(bf16[1,2,32,64]{3,2,1,0:T(8,128)(2,1)S(1)} %maximum_bitcast_fusion), channel_id=1, source_target_pairs={{0,1},{1,0},{2,3},{3,2},{4,5},{5,4},{6,7},{7,6},{8,9},{9,8},{10,11... | collective-permute-start | bytes 24584 | tf_op jit(solution)/shard_map/ppermute | solution.py:167
  5.4 0.4 %collective-permute-start.2 = (bf16[1024,128]{1,0:T(8,128)(2,1)}, bf16[1024,128]{1,0:T(8,128)(2,1)S(1)}, u32[]{:S(2)}, u32[]{:S(2)}) collective-permute-start(bf16[1024,128]{1,0:T(8,128)(2,1)} %bitcast.8), channel_id=1, source_target_pairs={{0,4},{4,0},{8,12},{12,8},{16,20},{20,16},{24,28},{28,24},{1,5},{5... | collective-permute-start | bytes 786440 | tf_op jit(solution)/shard_map/ppermute | solution.py:33
  5.8 1.1 %collective-permute-start.6 = (bf16[1024,128]{1,0:T(8,128)(2,1)}, bf16[1024,128]{1,0:T(8,128)(2,1)S(1)}, u32[]{:S(2)}, u32[]{:S(2)}) collective-permute-start(bf16[1024,128]{1,0:T(8,128)(2,1)} %bitcast.9), channel_id=1, source_target_pairs={{0,20},{4,8},{8,4},{12,24},{16,28},{20,0},{24,12},{28,16},{1,21},{... | collective-permute-start | bytes 786440 | tf_op jit(solution)/shard_map/ppermute | solution.py:33
  6.9 0.6 %collective-permute-done = bf16[1,2,32,64]{3,2,1,0:T(8,128)(2,1)S(1)} collective-permute-done((bf16[1,2,32,64]{3,2,1,0:T(8,128)(2,1)S(1)}, bf16[1,2,32,64]{3,2,1,0:T(8,128)(2,1)S(1)}, u32[]{:S(2)}, u32[]{:S(2)}) %collective-permute-start) | collective-permute-done | bytes 8224 | tf_op jit(solution)/shard_map/ppermute | solution.py:167
  7.6 0.0 collective-permute-done.3.first
  7.6 1.8 %collective-permute-start.4 = (bf16[1024,128]{1,0:T(8,128)(2,1)S(1)}, bf16[1024,128]{1,0:T(8,128)(2,1)S(1)}, u32[]{:S(2)}, u32[]{:S(2)}) collective-permute-start(bf16[1024,128]{1,0:T(8,128)(2,1)S(1)} %collective-permute-done.3.first), channel_id=1, source_target_pairs={{0,20},{4,8},{8,4},{12,24},{16,28},{20,0},{24,12},{28,16},{1,21},{... | collective-permute-start | bytes 786440 | tf_op jit(solution)/shard_map/ppermute | solution.py:33
  9.4 2.6 %collective-permute-start.1 = (bf16[2,2,32,64]{3,2,1,0:T(8,128)(2,1)S(1)}, bf16[2,2,32,64]{3,2,1,0:T(8,128)(2,1)S(1)}, u32[]{:S(2)}, u32[]{:S(2)}) collective-permute-start(bf16[2,2,32,64]{3,2,1,0:T(8,128)(2,1)S(1)} %pad_maximum_fusion.1), channel_id=1, source_target_pairs={{0,2},{1,3},{2,0},{3,1},{4,6},{5,7},{6,4},{7,5},{8,10},{9,11},{10,... | collective-permute-start | bytes 49160 | tf_op jit(solution)/shard_map/ppermute | solution.py:167
  12.0 0.0 collective-permute-done.2.first
  12.0 0.0 collective-permute-done.6.first
  12.0 0.2 %collective-permute-start.7 = (bf16[1024,128]{1,0:T(8,128)(2,1)S(1)}, bf16[1024,128]{1,0:T(8,128)(2,1)S(1)}, u32[]{:S(2)}, u32[]{:S(2)}) collective-permute-start(bf16[1024,128]{1,0:T(8,128)(2,1)S(1)} %collective-permute-done.6.first), channel_id=1, source_target_pairs={{0,4},{4,0},{8,12},{12,8},{16,20},{20,16},{24,28},{28,24},{1,5},{5... | collective-permute-start | bytes 786440 | tf_op jit(solution)/shard_map/ppermute | solution.py:33
  12.2 0.3 %collective-permute-start.5 = (bf16[1024,128]{1,0:T(8,128)(2,1)S(1)}, bf16[1024,128]{1,0:T(8,128)(2,1)S(1)}, u32[]{:S(2)}, u32[]{:S(2)}) collective-permute-start(bf16[1024,128]{1,0:T(8,128)(2,1)S(1)} %collective-permute-done.3.first), channel_id=1, source_target_pairs={{0,4},{4,0},{8,12},{12,8},{16,20},{20,16},{24,28},{28,24},{1,5},{5... | collective-permute-start | bytes 786440 | tf_op jit(solution)/shard_map/ppermute | solution.py:33
  12.5 1.7 %collective-permute-done.1 = bf16[2,2,32,64]{3,2,1,0:T(8,128)(2,1)S(1)} collective-permute-done((bf16[2,2,32,64]{3,2,1,0:T(8,128)(2,1)S(1)}, bf16[2,2,32,64]{3,2,1,0:T(8,128)(2,1)S(1)}, u32[]{:S(2)}, u32[]{:S(2)}) %collective-permute-start.1) | collective-permute-done | bytes 16416 | tf_op jit(solution)/shard_map/ppermute | solution.py:167
  14.2 0.4 %collective-permute-done.4.second = bf16[1024,128]{1,0:T(8,128)(2,1)S(1)} collective-permute-done((bf16[1024,128]{1,0:T(8,128)(2,1)S(1)}, bf16[1024,128]{1,0:T(8,128)(2,1)S(1)}, u32[]{:S(2)}, u32[]{:S(2)}) %collective-permute-start.4) | collective-permute-done | bytes 262176 | tf_op jit(solution)/shard_map/ppermute | solution.py:33
  14.7 0.1 collective-permute-start.8
  14.8 0.0 collective-permute-done.7.second
  14.8 0.2 %prepare.3 = (bf16[64,2048]{1,0:T(8,128)(2,1)S(1)}, bf16[64,2048]{1,0:T(8,128)(2,1)S(1)}) custom-call(bf16[1024,128]{1,0:T(8,128)(2,1)S(1)} %collective-permute-done.6.first, bf16[1024,128]{1,0:T(8,128)(2,1)S(1)} %collective-permute-done.7.second), custom_call_target="tpu_custom_call" | custom-call | tf_op jit(solution)/shard_map/prepare/pallas_call | solution.py:75
  15.0 0.0 collective-permute-done.5.second
  15.0 0.2 %prepare.2 = (bf16[64,2048]{1,0:T(8,128)(2,1)S(1)}, bf16[64,2048]{1,0:T(8,128)(2,1)S(1)}) custom-call(bf16[1024,128]{1,0:T(8,128)(2,1)S(1)} %collective-permute-done.3.first, bf16[1024,128]{1,0:T(8,128)(2,1)S(1)} %collective-permute-done.5.second), custom_call_target="tpu_custom_call" | custom-call | tf_op jit(solution)/shard_map/prepare/pallas_call | solution.py:75
  15.2 0.0 copy-start
  15.2 0.6 %combine.1 = (f32[2,32,2048]{2,1,0:T(8,128)S(1)}, bf16[2,32,64]{2,1,0:T(8,128)(2,1)S(1)}) custom-call(bf16[4,2,32,64]{3,2,1,0:T(8,128)(2,1)S(1)} %pad_maximum_fusion.vectors, bf16[1024,128]{1,0:T(8,128)(2,1)S(1)} %collective-permute-done.2.first, bf16[1024,128]{1,0:T(8,128)(2,1)S(1)} %collective-permute-done.4.second, ...), custom_call_target="tpu_custom_call" | custom-call | tf_op jit(solution)/shard_map/combine/pallas_call | solution.py:107
  15.9 0.3 %collective-permute-done.8.second = bf16[1024,128]{1,0:T(8,128)(2,1)S(1)} collective-permute-done((bf16[1024,128]{1,0:T(8,128)(2,1)S(1)}, bf16[1024,128]{1,0:T(8,128)(2,1)S(1)}, u32[]{:S(2)}, u32[]{:S(2)}) %collective-permute-start.8) | collective-permute-done | bytes 262176 | tf_op jit(solution)/shard_map/ppermute | solution.py:33
  16.2 0.0 copy-done
  16.2 1.2 %finish.1 = (f32[512,128]{1,0:T(8,128)}, f32[512,128]{1,0:T(8,128)}) custom-call(bf16[2,32,64]{2,1,0:T(8,128)(2,1)S(1)} %get-tuple-element.21.matrices, bf16[1024,128]{1,0:T(8,128)(2,1)S(1)} %bitcast.10, bf16[1024,128]{1,0:T(8,128)(2,1)S(1)} %collective-permute-done.8.second, f32[2,32,2048]{2,1,0:T(8,128)S(1)} %get-tuple-element.23.sums), custom_call_target="tpu_custom_call" | custom-call | tf_op jit(solution)/shard_map/finish/pallas_call | solution.py:146
  (2 shorter events, 0.0 us)
Async XLA Ops:
  0.6 7.0 %collective-permute-start.3 = (bf16[1024,128]{1,0:T(8,128)(2,1)}, bf16[1024,128]{1,0:T(8,128)(2,1)S(1)}, u32[]{:S(2)}, u32[]{:S(2)}) collective-permute-start(bf16[1024,128]{1,0:T(8,128)(2,1)} %bitcast.7), channel_id=1, source_target_pairs={{0,12},{4,16},{8,28},{12,0},{16,4},{20,24},{24,20},{28,8},{1,13},{... | collective-permute-start | bytes 786440 | tf_op jit(solution)/shard_map/ppermute | solution.py:33
  3.8 3.8 %collective-permute-start = (bf16[1,2,32,64]{3,2,1,0:T(8,128)(2,1)S(1)}, bf16[1,2,32,64]{3,2,1,0:T(8,128)(2,1)S(1)}, u32[]{:S(2)}, u32[]{:S(2)}) collective-permute-start(bf16[1,2,32,64]{3,2,1,0:T(8,128)(2,1)S(1)} %maximum_bitcast_fusion), channel_id=1, source_target_pairs={{0,1},{1,0},{2,3},{3,2},{4,5},{5,4},{6,7},{7,6},{8,9},{9,8},{10,11... | collective-permute-start | bytes 24584 | tf_op jit(solution)/shard_map/ppermute | solution.py:167
  5.4 6.6 %collective-permute-start.2 = (bf16[1024,128]{1,0:T(8,128)(2,1)}, bf16[1024,128]{1,0:T(8,128)(2,1)S(1)}, u32[]{:S(2)}, u32[]{:S(2)}) collective-permute-start(bf16[1024,128]{1,0:T(8,128)(2,1)} %bitcast.8), channel_id=1, source_target_pairs={{0,4},{4,0},{8,12},{12,8},{16,20},{20,16},{24,28},{28,24},{1,5},{5... | collective-permute-start | bytes 786440 | tf_op jit(solution)/shard_map/ppermute | solution.py:33
  5.8 6.2 %collective-permute-start.6 = (bf16[1024,128]{1,0:T(8,128)(2,1)}, bf16[1024,128]{1,0:T(8,128)(2,1)S(1)}, u32[]{:S(2)}, u32[]{:S(2)}) collective-permute-start(bf16[1024,128]{1,0:T(8,128)(2,1)} %bitcast.9), channel_id=1, source_target_pairs={{0,20},{4,8},{8,4},{12,24},{16,28},{20,0},{24,12},{28,16},{1,21},{... | collective-permute-start | bytes 786440 | tf_op jit(solution)/shard_map/ppermute | solution.py:33
  7.6 7.1 %collective-permute-start.4 = (bf16[1024,128]{1,0:T(8,128)(2,1)S(1)}, bf16[1024,128]{1,0:T(8,128)(2,1)S(1)}, u32[]{:S(2)}, u32[]{:S(2)}) collective-permute-start(bf16[1024,128]{1,0:T(8,128)(2,1)S(1)} %collective-permute-done.3.first), channel_id=1, source_target_pairs={{0,20},{4,8},{8,4},{12,24},{16,28},{20,0},{24,12},{28,16},{1,21},{... | collective-permute-start | bytes 786440 | tf_op jit(solution)/shard_map/ppermute | solution.py:33
  9.4 4.8 %collective-permute-start.1 = (bf16[2,2,32,64]{3,2,1,0:T(8,128)(2,1)S(1)}, bf16[2,2,32,64]{3,2,1,0:T(8,128)(2,1)S(1)}, u32[]{:S(2)}, u32[]{:S(2)}) collective-permute-start(bf16[2,2,32,64]{3,2,1,0:T(8,128)(2,1)S(1)} %pad_maximum_fusion.1), channel_id=1, source_target_pairs={{0,2},{1,3},{2,0},{3,1},{4,6},{5,7},{6,4},{7,5},{8,10},{9,11},{10,... | collective-permute-start | bytes 49160 | tf_op jit(solution)/shard_map/ppermute | solution.py:167
  12.0 2.8 %collective-permute-start.7 = (bf16[1024,128]{1,0:T(8,128)(2,1)S(1)}, bf16[1024,128]{1,0:T(8,128)(2,1)S(1)}, u32[]{:S(2)}, u32[]{:S(2)}) collective-permute-start(bf16[1024,128]{1,0:T(8,128)(2,1)S(1)} %collective-permute-done.6.first), channel_id=1, source_target_pairs={{0,4},{4,0},{8,12},{12,8},{16,20},{20,16},{24,28},{28,24},{1,5},{5... | collective-permute-start | bytes 786440 | tf_op jit(solution)/shard_map/ppermute | solution.py:33
  12.2 2.8 %collective-permute-start.5 = (bf16[1024,128]{1,0:T(8,128)(2,1)S(1)}, bf16[1024,128]{1,0:T(8,128)(2,1)S(1)}, u32[]{:S(2)}, u32[]{:S(2)}) collective-permute-start(bf16[1024,128]{1,0:T(8,128)(2,1)S(1)} %collective-permute-done.3.first), channel_id=1, source_target_pairs={{0,4},{4,0},{8,12},{12,8},{16,20},{20,16},{24,28},{28,24},{1,5},{5... | collective-permute-start | bytes 786440 | tf_op jit(solution)/shard_map/ppermute | solution.py:33
  14.7 1.5 %collective-permute-start.8 = (bf16[1024,128]{1,0:T(8,128)(2,1)S(1)}, bf16[1024,128]{1,0:T(8,128)(2,1)S(1)}, u32[]{:S(2)}, u32[]{:S(2)}) collective-permute-start(bf16[1024,128]{1,0:T(8,128)(2,1)S(1)} %collective-permute-done.4.second), channel_id=1, source_target_pairs={{0,4},{4,0},{8,12},{12,8},{16,20},{20,16},{24,28},{28,24},{1,5},{5... | collective-permute-start | bytes 786440 | tf_op jit(solution)/shard_map/ppermute | solution.py:33
  15.2 1.0 %copy-start = (bf16[64,16,128]{2,1,0:T(8,128)(2,1)S(1)}, bf16[64,16,128]{2,1,0:T(8,128)(2,1)}, u32[]{:S(2)}) copy-start(bf16[64,16,128]{2,1,0:T(8,128)(2,1)} %param.3) | copy-start | bytes 786436

commit v7 on v6

--- a/solution.py
+++ b/solution.py
@@ -122,14 +122,14 @@
     )(*operands)
 
 
-def finish_kernel(planes, matrices, first, second, sums, *refs):
-    *outs, even, odd = refs
-    depth = first.shape[1]
+def finish_kernel(planes, matrices, lines, second, sums, *outs):
+    depth = second.shape[1]
     modes = matrices.shape[1]
-    parity_lines(first, second, planes, even, odd)
-    for parity, parts in enumerate((even, odd)):
+    here = lines[...]
+    there = lines_of(second, planes, True)
+    for parity, parts in enumerate((here + there, here - there)):
         result = sums[parity] + jnp.dot(
-            matrices[parity], parts[...], preferred_element_type=jnp.float32
+            matrices[parity], parts, preferred_element_type=jnp.float32
         )
         for y in range(planes):
             outs[parity][pl.ds(y, modes, stride=planes), :] = result[
@@ -137,9 +137,8 @@
             ]
 
 
-def finish(matrices, pair, sums, planes):
-    first, second = (block.value for block in pair)
-    lines, depth = first.shape
+def finish(matrices, lines, second, sums, planes):
+    depth = second.value.shape[1]
     modes = matrices.shape[1]
     shape = jax.ShapeDtypeStruct((modes * planes, depth), jnp.float32)
     vmem = pl.BlockSpec(memory_space=pltpu.VMEM)
@@ -148,11 +147,36 @@
         out_shape=(shape, shape),
         in_specs=[vmem] * 4,
         out_specs=(vmem, vmem),
-        scratch_shapes=[pltpu.VMEM((lines // planes, planes * depth), jnp.bfloat16)]
-        * 2,
         compiler_params=PARAMS,
         name="finish",
-    )(matrices, first, second, sums)
+    )(matrices, lines, second.value, sums)
+
+
+def lines_of(block, planes, backwards):
+    rows = block.shape[0] // planes
+    order = range(rows - 1, -1, -1) if backwards else range(rows)
+    lines = jnp.stack([block[pl.ds(i * planes, planes), :] for i in order])
+    lines = jnp.swapaxes(lines, 0, 1)
+    return jnp.concatenate([lines[y] for y in range(planes)], axis=1)
+
+
+def bring_kernel(planes, source, lines):
+    lines[...] = lines_of(source, planes, False)
+
+
+def bring(block, planes):
+    lines, depth = block.value.shape
+    vmem = pl.BlockSpec(memory_space=pltpu.VMEM)
+    return pl.pallas_call(
+        functools.partial(bring_kernel, planes),
+        out_shape=jax.ShapeDtypeStruct(
+            (lines // planes, planes * depth), block.value.dtype
+        ),
+        in_specs=[vmem],
+        out_specs=vmem,
+        compiler_params=PARAMS,
+        name="bring",
+    )(block.value)
 
 
 def local(field, even_vectors, odd_vectors):
@@ -186,9 +210,11 @@
         masks = masks[2:]
     for step in steps:
         vectors = widen(vectors, step)
+    own_lines = bring(held[0], planes)
     others = []
     for block in held[:-1]:
-        block = after(block, *(other.value for other in others[:1]))
+        if others:
+            block = after(block, others[0].value, own_lines)
         others.append(send(block, 1, 1, count))
     others.append(send(after(held[-1], vectors), 1, 1, count))
 
@@ -209,7 +235,7 @@
     sums, matrices = combine(
         vectors, ready, pairs[-2], pairs[-1][0], count, planes
     )
-    even, odd = finish(matrices, pairs[-1], sums, planes)
+    even, odd = finish(matrices, own_lines, pairs[-1][1], sums, planes)
     return even.reshape(modes, planes, depth), odd.reshape(modes, planes, depth)
 
 

time: 17.7 us -> 17.5 us (0.989)
  waiting for transfers between devices: 3.12 us -> 2.02 us
  local copies, waits for them, and re-layouts: 0.01 us -> 0.95 us
    ppermute x2, waiting for transfers between devices: 2.34 us -> 1.23 us  [widen(): return jnp.concatenate((vectors, lax.ppermute(vectors, 'gz', pairs)))]
    unnamed x2, local copies, waits for them, and re-layouts: 0.01 us -> 0.95 us
  transfers between devices with their start and end apart: 9 -> 9, of which waited for: 4 -> 4; matrix products, arithmetic and copies ran while one was open for 4% -> 4% of each run, Pallas kernels for 6% -> 7%
where the time goes in v7:
time: 17.5 us; the launch traced here: 17.3 us
  starting transfers between devices  10.7 us (61%)
  Pallas kernels  2.22 us (13%)
  waiting for transfers between devices  2.02 us (12%)
  local copies, waits for them, and re-layouts  0.95 us (5%)
  other arithmetic  0.75 us (4%)
  between operations  0.67 us (4%)
    ppermute x7, starting transfers between devices, send(): return Block(lax.ppermute(block.value, 'gx', pairs), *offsets)  6.44 us
    ppermute x2, starting transfers between devices, widen(): return jnp.concatenate((vectors, lax.ppermute(vectors, 'gz', pairs)))  4.23 us
    ppermute x2, waiting for transfers between devices, widen(): return jnp.concatenate((vectors, lax.ppermute(vectors, 'gz', pairs)))  1.23 us
    pallas_call x1, Pallas kernels, finish(): pl.pallas_call(functools.partial(finish_kernel, planes), out_shape=(shape...  1.08 us
    unnamed x2, local copies, waits for them, and re-layouts  0.95 us
    ppermute x7, waiting for transfers between devices, send(): return Block(lax.ppermute(block.value, 'gx', pairs), *offsets)  0.8 us
    broadcast_in_dim x1, other arithmetic, local(): vectors = jnp.stack((even_vectors, odd_vectors))[None]  0.72 us
    pallas_call x1, Pallas kernels, combine(): pl.pallas_call(functools.partial(combine_kernel, [functools.partial(block...  0.63 us
  transfers between devices with their start and end apart: 9, of which 4 were waited for; matrix products, arithmetic and copies ran while one was open for 4% of the time, Pallas kernels for 7%

profile of v7, /device:TPU:0, one launch (start us, length us, event | category | flops | bytes accessed | tf_op | source)
XLA Modules:
  0.0 17.3 jit_solution(16258911273821190924)
XLA Ops:
  0.6 2.4 %collective-permute-start.3 = (bf16[1024,128]{1,0:T(8,128)(2,1)}, bf16[1024,128]{1,0:T(8,128)(2,1)S(1)}, u32[]{:S(2)}, u32[]{:S(2)}) collective-permute-start(bf16[1024,128]{1,0:T(8,128)(2,1)} %bitcast.7), channel_id=1, source_target_pairs={{0,12},{4,16},{8,28},{12,0},{16,4},{20,24},{24,20},{28,8},{1,13},{... | collective-permute-start | bytes 786440 | tf_op jit(solution)/shard_map/ppermute | solution.py:33
  3.1 0.7 %maximum_bitcast_fusion = bf16[1,2,32,64]{3,2,1,0:T(8,128)(2,1)S(1)} fusion(bf16[1,32,64]{2,1,0:T(8,128)(2,1)} %bitcast.11, bf16[1,32,64]{2,1,0:T(8,128)(2,1)} %bitcast.12), kind=kLoop, calls=%fused_computation.2 | loop fusion | flops 4096 | bytes 16384 | tf_op jit(solution)/shard_map/broadcast_in_dim | solution.py:197
  3.8 1.6 %collective-permute-start = (bf16[1,2,32,64]{3,2,1,0:T(8,128)(2,1)S(1)}, bf16[1,2,32,64]{3,2,1,0:T(8,128)(2,1)S(1)}, u32[]{:S(2)}, u32[]{:S(2)}) collective-permute-start(bf16[1,2,32,64]{3,2,1,0:T(8,128)(2,1)S(1)} %maximum_bitcast_fusion), channel_id=1, source_target_pairs={{0,1},{1,0},{2,3},{3,2},{4,5},{5,4},{6,7},{7,6},{8,9},{9,8},{10,11... | collective-permute-start | bytes 24584 | tf_op jit(solution)/shard_map/ppermute | solution.py:191
  5.4 0.4 %collective-permute-start.2 = (bf16[1024,128]{1,0:T(8,128)(2,1)}, bf16[1024,128]{1,0:T(8,128)(2,1)S(1)}, u32[]{:S(2)}, u32[]{:S(2)}) collective-permute-start(bf16[1024,128]{1,0:T(8,128)(2,1)} %bitcast.8), channel_id=1, source_target_pairs={{0,4},{4,0},{8,12},{12,8},{16,20},{20,16},{24,28},{28,24},{1,5},{5... | collective-permute-start | bytes 786440 | tf_op jit(solution)/shard_map/ppermute | solution.py:33
  5.8 1.1 %collective-permute-start.6 = (bf16[1024,128]{1,0:T(8,128)(2,1)}, bf16[1024,128]{1,0:T(8,128)(2,1)S(1)}, u32[]{:S(2)}, u32[]{:S(2)}) collective-permute-start(bf16[1024,128]{1,0:T(8,128)(2,1)} %bitcast.9), channel_id=1, source_target_pairs={{0,20},{4,8},{8,4},{12,24},{16,28},{20,0},{24,12},{28,16},{1,21},{... | collective-permute-start | bytes 786440 | tf_op jit(solution)/shard_map/ppermute | solution.py:33
  6.9 0.6 %collective-permute-done = bf16[1,2,32,64]{3,2,1,0:T(8,128)(2,1)S(1)} collective-permute-done((bf16[1,2,32,64]{3,2,1,0:T(8,128)(2,1)S(1)}, bf16[1,2,32,64]{3,2,1,0:T(8,128)(2,1)S(1)}, u32[]{:S(2)}, u32[]{:S(2)}) %collective-permute-start) | collective-permute-done | bytes 8224 | tf_op jit(solution)/shard_map/ppermute | solution.py:191
  7.6 0.0 collective-permute-done.3.first
  7.6 1.8 %collective-permute-start.4 = (bf16[1024,128]{1,0:T(8,128)(2,1)S(1)}, bf16[1024,128]{1,0:T(8,128)(2,1)S(1)}, u32[]{:S(2)}, u32[]{:S(2)}) collective-permute-start(bf16[1024,128]{1,0:T(8,128)(2,1)S(1)} %collective-permute-done.3.first), channel_id=1, source_target_pairs={{0,20},{4,8},{8,4},{12,24},{16,28},{20,0},{24,12},{28,16},{1,21},{... | collective-permute-start | bytes 786440 | tf_op jit(solution)/shard_map/ppermute | solution.py:33
  9.4 2.6 %collective-permute-start.1 = (bf16[2,2,32,64]{3,2,1,0:T(8,128)(2,1)S(1)}, bf16[2,2,32,64]{3,2,1,0:T(8,128)(2,1)S(1)}, u32[]{:S(2)}, u32[]{:S(2)}) collective-permute-start(bf16[2,2,32,64]{3,2,1,0:T(8,128)(2,1)S(1)} %pad_maximum_fusion.1), channel_id=1, source_target_pairs={{0,2},{1,3},{2,0},{3,1},{4,6},{5,7},{6,4},{7,5},{8,10},{9,11},{10,... | collective-permute-start | bytes 49160 | tf_op jit(solution)/shard_map/ppermute | solution.py:191
  12.0 0.0 copy-start
  12.0 0.9 %copy-done = bf16[64,16,128]{2,1,0:T(8,128)(2,1)S(1)} copy-done((bf16[64,16,128]{2,1,0:T(8,128)(2,1)S(1)}, bf16[64,16,128]{2,1,0:T(8,128)(2,1)}, u32[]{:S(2)}) %copy-start) | copy-done | bytes 262168
  12.9 0.1 bring.1.lines
  13.0 0.0 collective-permute-done.2.first
  13.1 0.1 collective-permute-start.5
  13.2 0.0 collective-permute-done.6.first
  13.2 0.4 %collective-permute-start.7 = (bf16[1024,128]{1,0:T(8,128)(2,1)S(1)}, bf16[1024,128]{1,0:T(8,128)(2,1)S(1)}, u32[]{:S(2)}, u32[]{:S(2)}) collective-permute-start(bf16[1024,128]{1,0:T(8,128)(2,1)S(1)} %collective-permute-done.6.first), channel_id=1, source_target_pairs={{0,4},{4,0},{8,12},{12,8},{16,20},{20,16},{24,28},{28,24},{1,5},{5... | collective-permute-start | bytes 786440 | tf_op jit(solution)/shard_map/ppermute | solution.py:33
  13.6 0.6 %collective-permute-done.1 = bf16[2,2,32,64]{3,2,1,0:T(8,128)(2,1)S(1)} collective-permute-done((bf16[2,2,32,64]{3,2,1,0:T(8,128)(2,1)S(1)}, bf16[2,2,32,64]{3,2,1,0:T(8,128)(2,1)S(1)}, u32[]{:S(2)}, u32[]{:S(2)}) %collective-permute-start.1) | collective-permute-done | bytes 16416 | tf_op jit(solution)/shard_map/ppermute | solution.py:191
  14.2 0.4 %collective-permute-done.4.second = bf16[1024,128]{1,0:T(8,128)(2,1)S(1)} collective-permute-done((bf16[1024,128]{1,0:T(8,128)(2,1)S(1)}, bf16[1024,128]{1,0:T(8,128)(2,1)S(1)}, u32[]{:S(2)}, u32[]{:S(2)}) %collective-permute-start.4) | collective-permute-done | bytes 262176 | tf_op jit(solution)/shard_map/ppermute | solution.py:33
  14.7 0.1 collective-permute-start.8
  14.8 0.0 collective-permute-done.5.second
  14.8 0.2 %prepare.2 = (bf16[64,2048]{1,0:T(8,128)(2,1)S(1)}, bf16[64,2048]{1,0:T(8,128)(2,1)S(1)}) custom-call(bf16[1024,128]{1,0:T(8,128)(2,1)S(1)} %collective-permute-done.3.first, bf16[1024,128]{1,0:T(8,128)(2,1)S(1)} %collective-permute-done.5.second), custom_call_target="tpu_custom_call" | custom-call | tf_op jit(solution)/shard_map/prepare/pallas_call | solution.py:75
  15.0 0.0 collective-permute-done.7.second
  15.0 0.2 %prepare.3 = (bf16[64,2048]{1,0:T(8,128)(2,1)S(1)}, bf16[64,2048]{1,0:T(8,128)(2,1)S(1)}) custom-call(bf16[1024,128]{1,0:T(8,128)(2,1)S(1)} %collective-permute-done.6.first, bf16[1024,128]{1,0:T(8,128)(2,1)S(1)} %collective-permute-done.7.second), custom_call_target="tpu_custom_call" | custom-call | tf_op jit(solution)/shard_map/prepare/pallas_call | solution.py:75
  15.2 0.6 %combine.1 = (f32[2,32,2048]{2,1,0:T(8,128)S(1)}, bf16[2,32,64]{2,1,0:T(8,128)(2,1)S(1)}) custom-call(bf16[4,2,32,64]{3,2,1,0:T(8,128)(2,1)S(1)} %pad_maximum_fusion.vectors, bf16[1024,128]{1,0:T(8,128)(2,1)S(1)} %collective-permute-done.2.first, bf16[1024,128]{1,0:T(8,128)(2,1)S(1)} %collective-permute-done.4.second, ...), custom_call_target="tpu_custom_call" | custom-call | tf_op jit(solution)/shard_map/combine/pallas_call | solution.py:107
  15.9 0.3 %collective-permute-done.8.second = bf16[1024,128]{1,0:T(8,128)(2,1)S(1)} collective-permute-done((bf16[1024,128]{1,0:T(8,128)(2,1)S(1)}, bf16[1024,128]{1,0:T(8,128)(2,1)S(1)}, u32[]{:S(2)}, u32[]{:S(2)}) %collective-permute-start.8) | collective-permute-done | bytes 262176 | tf_op jit(solution)/shard_map/ppermute | solution.py:33
  16.2 1.1 %finish.1 = (f32[512,128]{1,0:T(8,128)}, f32[512,128]{1,0:T(8,128)}) custom-call(bf16[2,32,64]{2,1,0:T(8,128)(2,1)S(1)} %get-tuple-element.21.matrices, bf16[64,2048]{1,0:T(8,128)(2,1)S(1)} %bring.1.lines, bf16[1024,128]{1,0:T(8,128)(2,1)S(1)} %collective-permute-done.8.second, f32[2,32,2048]{2,1,0:T(8,128)S(1)} %get-tuple-element.23.sums), custom_call_target="tpu_custom_call" | custom-call | tf_op jit(solution)/shard_map/finish/pallas_call | solution.py:145
  (2 shorter events, 0.0 us)
Async XLA Ops:
  0.6 7.0 %collective-permute-start.3 = (bf16[1024,128]{1,0:T(8,128)(2,1)}, bf16[1024,128]{1,0:T(8,128)(2,1)S(1)}, u32[]{:S(2)}, u32[]{:S(2)}) collective-permute-start(bf16[1024,128]{1,0:T(8,128)(2,1)} %bitcast.7), channel_id=1, source_target_pairs={{0,12},{4,16},{8,28},{12,0},{16,4},{20,24},{24,20},{28,8},{1,13},{... | collective-permute-start | bytes 786440 | tf_op jit(solution)/shard_map/ppermute | solution.py:33
  3.8 3.8 %collective-permute-start = (bf16[1,2,32,64]{3,2,1,0:T(8,128)(2,1)S(1)}, bf16[1,2,32,64]{3,2,1,0:T(8,128)(2,1)S(1)}, u32[]{:S(2)}, u32[]{:S(2)}) collective-permute-start(bf16[1,2,32,64]{3,2,1,0:T(8,128)(2,1)S(1)} %maximum_bitcast_fusion), channel_id=1, source_target_pairs={{0,1},{1,0},{2,3},{3,2},{4,5},{5,4},{6,7},{7,6},{8,9},{9,8},{10,11... | collective-permute-start | bytes 24584 | tf_op jit(solution)/shard_map/ppermute | solution.py:191
  5.4 7.6 %collective-permute-start.2 = (bf16[1024,128]{1,0:T(8,128)(2,1)}, bf16[1024,128]{1,0:T(8,128)(2,1)S(1)}, u32[]{:S(2)}, u32[]{:S(2)}) collective-permute-start(bf16[1024,128]{1,0:T(8,128)(2,1)} %bitcast.8), channel_id=1, source_target_pairs={{0,4},{4,0},{8,12},{12,8},{16,20},{20,16},{24,28},{28,24},{1,5},{5... | collective-permute-start | bytes 786440 | tf_op jit(solution)/shard_map/ppermute | solution.py:33
  5.8 7.3 %collective-permute-start.6 = (bf16[1024,128]{1,0:T(8,128)(2,1)}, bf16[1024,128]{1,0:T(8,128)(2,1)S(1)}, u32[]{:S(2)}, u32[]{:S(2)}) collective-permute-start(bf16[1024,128]{1,0:T(8,128)(2,1)} %bitcast.9), channel_id=1, source_target_pairs={{0,20},{4,8},{8,4},{12,24},{16,28},{20,0},{24,12},{28,16},{1,21},{... | collective-permute-start | bytes 786440 | tf_op jit(solution)/shard_map/ppermute | solution.py:33
  7.6 7.1 %collective-permute-start.4 = (bf16[1024,128]{1,0:T(8,128)(2,1)S(1)}, bf16[1024,128]{1,0:T(8,128)(2,1)S(1)}, u32[]{:S(2)}, u32[]{:S(2)}) collective-permute-start(bf16[1024,128]{1,0:T(8,128)(2,1)S(1)} %collective-permute-done.3.first), channel_id=1, source_target_pairs={{0,20},{4,8},{8,4},{12,24},{16,28},{20,0},{24,12},{28,16},{1,21},{... | collective-permute-start | bytes 786440 | tf_op jit(solution)/shard_map/ppermute | solution.py:33
  9.4 4.8 %collective-permute-start.1 = (bf16[2,2,32,64]{3,2,1,0:T(8,128)(2,1)S(1)}, bf16[2,2,32,64]{3,2,1,0:T(8,128)(2,1)S(1)}, u32[]{:S(2)}, u32[]{:S(2)}) collective-permute-start(bf16[2,2,32,64]{3,2,1,0:T(8,128)(2,1)S(1)} %pad_maximum_fusion.1), channel_id=1, source_target_pairs={{0,2},{1,3},{2,0},{3,1},{4,6},{5,7},{6,4},{7,5},{8,10},{9,11},{10,... | collective-permute-start | bytes 49160 | tf_op jit(solution)/shard_map/ppermute | solution.py:191
  12.0 0.9 %copy-start = (bf16[64,16,128]{2,1,0:T(8,128)(2,1)S(1)}, bf16[64,16,128]{2,1,0:T(8,128)(2,1)}, u32[]{:S(2)}) copy-start(bf16[64,16,128]{2,1,0:T(8,128)(2,1)} %param.3) | copy-start | bytes 786436
  13.1 1.7 %collective-permute-start.5 = (bf16[1024,128]{1,0:T(8,128)(2,1)S(1)}, bf16[1024,128]{1,0:T(8,128)(2,1)S(1)}, u32[]{:S(2)}, u32[]{:S(2)}) collective-permute-start(bf16[1024,128]{1,0:T(8,128)(2,1)S(1)} %collective-permute-done.3.first), channel_id=1, source_target_pairs={{0,4},{4,0},{8,12},{12,8},{16,20},{20,16},{24,28},{28,24},{1,5},{5... | collective-permute-start | bytes 786440 | tf_op jit(solution)/shard_map/ppermute | solution.py:33
  13.2 1.8 %collective-permute-start.7 = (bf16[1024,128]{1,0:T(8,128)(2,1)S(1)}, bf16[1024,128]{1,0:T(8,128)(2,1)S(1)}, u32[]{:S(2)}, u32[]{:S(2)}) collective-permute-start(bf16[1024,128]{1,0:T(8,128)(2,1)S(1)} %collective-permute-done.6.first), channel_id=1, source_target_pairs={{0,4},{4,0},{8,12},{12,8},{16,20},{20,16},{24,28},{28,24},{1,5},{5... | collective-permute-start | bytes 786440 | tf_op jit(solution)/shard_map/ppermute | solution.py:33
  14.7 1.5 %collective-permute-start.8 = (bf16[1024,128]{1,0:T(8,128)(2,1)S(1)}, bf16[1024,128]{1,0:T(8,128)(2,1)S(1)}, u32[]{:S(2)}, u32[]{:S(2)}) collective-permute-start(bf16[1024,128]{1,0:T(8,128)(2,1)S(1)} %collective-permute-done.4.second), channel_id=1, source_target_pairs={{0,4},{4,0},{8,12},{12,8},{16,20},{20,16},{24,28},{28,24},{1,5},{5... | collective-permute-start | bytes 786440 | tf_op jit(solution)/shard_map/ppermute | solution.py:33

commit v8 on v7

--- a/solution.py
+++ b/solution.py
@@ -200,8 +200,8 @@
     while masks:
         a, b = (masks + masks)[:2]
         crossed = len(masks) > 1
+        far = [send(block, b, a, count) for block in held] if crossed else []
         near = [send(block, a, b, count) for block in held]
-        far = [send(block, b, a, count) for block in held] if crossed else []
         if steps:
             vectors = widen(vectors, steps.pop(0))
             near[0] = after(near[0], vectors)

time: 17.5 us -> 17.5 us (level)
  no operation moved by 1% of the time
where the time goes in v8:
time: 17.5 us; the launch traced here: 17.3 us
  starting transfers between devices  10.7 us (61%)
  Pallas kernels  2.22 us (13%)
  waiting for transfers between devices  2.02 us (12%)
  local copies, waits for them, and re-layouts  0.95 us (5%)
  other arithmetic  0.75 us (4%)
  between operations  0.67 us (4%)
    ppermute x7, starting transfers between devices, send(): return Block(lax.ppermute(block.value, 'gx', pairs), *offsets)  6.44 us
    ppermute x2, starting transfers between devices, widen(): return jnp.concatenate((vectors, lax.ppermute(vectors, 'gz', pairs)))  4.23 us
    ppermute x2, waiting for transfers between devices, widen(): return jnp.concatenate((vectors, lax.ppermute(vectors, 'gz', pairs)))  1.23 us
    pallas_call x1, Pallas kernels, finish(): pl.pallas_call(functools.partial(finish_kernel, planes), out_shape=(shape...  1.08 us
    unnamed x2, local copies, waits for them, and re-layouts  0.95 us
    ppermute x7, waiting for transfers between devices, send(): return Block(lax.ppermute(block.value, 'gx', pairs), *offsets)  0.8 us
    broadcast_in_dim x1, other arithmetic, local(): vectors = jnp.stack((even_vectors, odd_vectors))[None]  0.72 us
    pallas_call x1, Pallas kernels, combine(): pl.pallas_call(functools.partial(combine_kernel, [functools.partial(block...  0.63 us
  transfers between devices with their start and end apart: 9, of which 4 were waited for; matrix products, arithmetic and copies ran while one was open for 4% of the time, Pallas kernels for 7%

profile of v8, /device:TPU:0, one launch (start us, length us, event | category | flops | bytes accessed | tf_op | source)
XLA Modules:
  0.0 17.3 jit_solution(16258911273821190924)
XLA Ops:
  0.6 2.4 %collective-permute-start.3 = (bf16[1024,128]{1,0:T(8,128)(2,1)}, bf16[1024,128]{1,0:T(8,128)(2,1)S(1)}, u32[]{:S(2)}, u32[]{:S(2)}) collective-permute-start(bf16[1024,128]{1,0:T(8,128)(2,1)} %bitcast.7), channel_id=1, source_target_pairs={{0,12},{4,16},{8,28},{12,0},{16,4},{20,24},{24,20},{28,8},{1,13},{... | collective-permute-start | bytes 786440 | tf_op jit(solution)/shard_map/ppermute | solution.py:33
  3.1 0.7 %maximum_bitcast_fusion = bf16[1,2,32,64]{3,2,1,0:T(8,128)(2,1)S(1)} fusion(bf16[1,32,64]{2,1,0:T(8,128)(2,1)} %bitcast.11, bf16[1,32,64]{2,1,0:T(8,128)(2,1)} %bitcast.12), kind=kLoop, calls=%fused_computation.2 | loop fusion | flops 4096 | bytes 16384 | tf_op jit(solution)/shard_map/broadcast_in_dim | solution.py:197
  3.8 1.6 %collective-permute-start = (bf16[1,2,32,64]{3,2,1,0:T(8,128)(2,1)S(1)}, bf16[1,2,32,64]{3,2,1,0:T(8,128)(2,1)S(1)}, u32[]{:S(2)}, u32[]{:S(2)}) collective-permute-start(bf16[1,2,32,64]{3,2,1,0:T(8,128)(2,1)S(1)} %maximum_bitcast_fusion), channel_id=1, source_target_pairs={{0,1},{1,0},{2,3},{3,2},{4,5},{5,4},{6,7},{7,6},{8,9},{9,8},{10,11... | collective-permute-start | bytes 24584 | tf_op jit(solution)/shard_map/ppermute | solution.py:191
  5.4 0.4 %collective-permute-start.2 = (bf16[1024,128]{1,0:T(8,128)(2,1)}, bf16[1024,128]{1,0:T(8,128)(2,1)S(1)}, u32[]{:S(2)}, u32[]{:S(2)}) collective-permute-start(bf16[1024,128]{1,0:T(8,128)(2,1)} %bitcast.8), channel_id=1, source_target_pairs={{0,4},{4,0},{8,12},{12,8},{16,20},{20,16},{24,28},{28,24},{1,5},{5... | collective-permute-start | bytes 786440 | tf_op jit(solution)/shard_map/ppermute | solution.py:33
  5.8 1.1 %collective-permute-start.6 = (bf16[1024,128]{1,0:T(8,128)(2,1)}, bf16[1024,128]{1,0:T(8,128)(2,1)S(1)}, u32[]{:S(2)}, u32[]{:S(2)}) collective-permute-start(bf16[1024,128]{1,0:T(8,128)(2,1)} %bitcast.9), channel_id=1, source_target_pairs={{0,20},{4,8},{8,4},{12,24},{16,28},{20,0},{24,12},{28,16},{1,21},{... | collective-permute-start | bytes 786440 | tf_op jit(solution)/shard_map/ppermute | solution.py:33
  6.9 0.6 %collective-permute-done = bf16[1,2,32,64]{3,2,1,0:T(8,128)(2,1)S(1)} collective-permute-done((bf16[1,2,32,64]{3,2,1,0:T(8,128)(2,1)S(1)}, bf16[1,2,32,64]{3,2,1,0:T(8,128)(2,1)S(1)}, u32[]{:S(2)}, u32[]{:S(2)}) %collective-permute-start) | collective-permute-done | bytes 8224 | tf_op jit(solution)/shard_map/ppermute | solution.py:191
  7.6 0.0 collective-permute-done.3.first
  7.6 1.8 %collective-permute-start.4 = (bf16[1024,128]{1,0:T(8,128)(2,1)S(1)}, bf16[1024,128]{1,0:T(8,128)(2,1)S(1)}, u32[]{:S(2)}, u32[]{:S(2)}) collective-permute-start(bf16[1024,128]{1,0:T(8,128)(2,1)S(1)} %collective-permute-done.3.first), channel_id=1, source_target_pairs={{0,20},{4,8},{8,4},{12,24},{16,28},{20,0},{24,12},{28,16},{1,21},{... | collective-permute-start | bytes 786440 | tf_op jit(solution)/shard_map/ppermute | solution.py:33
  9.4 2.6 %collective-permute-start.1 = (bf16[2,2,32,64]{3,2,1,0:T(8,128)(2,1)S(1)}, bf16[2,2,32,64]{3,2,1,0:T(8,128)(2,1)S(1)}, u32[]{:S(2)}, u32[]{:S(2)}) collective-permute-start(bf16[2,2,32,64]{3,2,1,0:T(8,128)(2,1)S(1)} %pad_maximum_fusion.1), channel_id=1, source_target_pairs={{0,2},{1,3},{2,0},{3,1},{4,6},{5,7},{6,4},{7,5},{8,10},{9,11},{10,... | collective-permute-start | bytes 49160 | tf_op jit(solution)/shard_map/ppermute | solution.py:191
  12.0 0.0 copy-start
  12.0 0.9 %copy-done = bf16[64,16,128]{2,1,0:T(8,128)(2,1)S(1)} copy-done((bf16[64,16,128]{2,1,0:T(8,128)(2,1)S(1)}, bf16[64,16,128]{2,1,0:T(8,128)(2,1)}, u32[]{:S(2)}) %copy-start) | copy-done | bytes 262168
  12.9 0.1 bring.1.lines
  13.0 0.0 collective-permute-done.2.first
  13.1 0.1 collective-permute-start.5
  13.2 0.0 collective-permute-done.6.first
  13.2 0.4 %collective-permute-start.7 = (bf16[1024,128]{1,0:T(8,128)(2,1)S(1)}, bf16[1024,128]{1,0:T(8,128)(2,1)S(1)}, u32[]{:S(2)}, u32[]{:S(2)}) collective-permute-start(bf16[1024,128]{1,0:T(8,128)(2,1)S(1)} %collective-permute-done.6.first), channel_id=1, source_target_pairs={{0,4},{4,0},{8,12},{12,8},{16,20},{20,16},{24,28},{28,24},{1,5},{5... | collective-permute-start | bytes 786440 | tf_op jit(solution)/shard_map/ppermute | solution.py:33
  13.6 0.6 %collective-permute-done.1 = bf16[2,2,32,64]{3,2,1,0:T(8,128)(2,1)S(1)} collective-permute-done((bf16[2,2,32,64]{3,2,1,0:T(8,128)(2,1)S(1)}, bf16[2,2,32,64]{3,2,1,0:T(8,128)(2,1)S(1)}, u32[]{:S(2)}, u32[]{:S(2)}) %collective-permute-start.1) | collective-permute-done | bytes 16416 | tf_op jit(solution)/shard_map/ppermute | solution.py:191
  14.2 0.4 %collective-permute-done.4.second = bf16[1024,128]{1,0:T(8,128)(2,1)S(1)} collective-permute-done((bf16[1024,128]{1,0:T(8,128)(2,1)S(1)}, bf16[1024,128]{1,0:T(8,128)(2,1)S(1)}, u32[]{:S(2)}, u32[]{:S(2)}) %collective-permute-start.4) | collective-permute-done | bytes 262176 | tf_op jit(solution)/shard_map/ppermute | solution.py:33
  14.7 0.1 collective-permute-start.8
  14.8 0.0 collective-permute-done.5.second
  14.8 0.2 %prepare.2 = (bf16[64,2048]{1,0:T(8,128)(2,1)S(1)}, bf16[64,2048]{1,0:T(8,128)(2,1)S(1)}) custom-call(bf16[1024,128]{1,0:T(8,128)(2,1)S(1)} %collective-permute-done.3.first, bf16[1024,128]{1,0:T(8,128)(2,1)S(1)} %collective-permute-done.5.second), custom_call_target="tpu_custom_call" | custom-call | tf_op jit(solution)/shard_map/prepare/pallas_call | solution.py:75
  15.0 0.0 collective-permute-done.7.second
  15.0 0.2 %prepare.3 = (bf16[64,2048]{1,0:T(8,128)(2,1)S(1)}, bf16[64,2048]{1,0:T(8,128)(2,1)S(1)}) custom-call(bf16[1024,128]{1,0:T(8,128)(2,1)S(1)} %collective-permute-done.6.first, bf16[1024,128]{1,0:T(8,128)(2,1)S(1)} %collective-permute-done.7.second), custom_call_target="tpu_custom_call" | custom-call | tf_op jit(solution)/shard_map/prepare/pallas_call | solution.py:75
  15.2 0.6 %combine.1 = (f32[2,32,2048]{2,1,0:T(8,128)S(1)}, bf16[2,32,64]{2,1,0:T(8,128)(2,1)S(1)}) custom-call(bf16[4,2,32,64]{3,2,1,0:T(8,128)(2,1)S(1)} %pad_maximum_fusion.vectors, bf16[1024,128]{1,0:T(8,128)(2,1)S(1)} %collective-permute-done.2.first, bf16[1024,128]{1,0:T(8,128)(2,1)S(1)} %collective-permute-done.4.second, ...), custom_call_target="tpu_custom_call" | custom-call | tf_op jit(solution)/shard_map/combine/pallas_call | solution.py:107
  15.9 0.3 %collective-permute-done.8.second = bf16[1024,128]{1,0:T(8,128)(2,1)S(1)} collective-permute-done((bf16[1024,128]{1,0:T(8,128)(2,1)S(1)}, bf16[1024,128]{1,0:T(8,128)(2,1)S(1)}, u32[]{:S(2)}, u32[]{:S(2)}) %collective-permute-start.8) | collective-permute-done | bytes 262176 | tf_op jit(solution)/shard_map/ppermute | solution.py:33
  16.2 1.1 %finish.1 = (f32[512,128]{1,0:T(8,128)}, f32[512,128]{1,0:T(8,128)}) custom-call(bf16[2,32,64]{2,1,0:T(8,128)(2,1)S(1)} %get-tuple-element.21.matrices, bf16[64,2048]{1,0:T(8,128)(2,1)S(1)} %bring.1.lines, bf16[1024,128]{1,0:T(8,128)(2,1)S(1)} %collective-permute-done.8.second, f32[2,32,2048]{2,1,0:T(8,128)S(1)} %get-tuple-element.23.sums), custom_call_target="tpu_custom_call" | custom-call | tf_op jit(solution)/shard_map/finish/pallas_call | solution.py:145
  (2 shorter events, 0.0 us)
Async XLA Ops:
  0.6 7.0 %collective-permute-start.3 = (bf16[1024,128]{1,0:T(8,128)(2,1)}, bf16[1024,128]{1,0:T(8,128)(2,1)S(1)}, u32[]{:S(2)}, u32[]{:S(2)}) collective-permute-start(bf16[1024,128]{1,0:T(8,128)(2,1)} %bitcast.7), channel_id=1, source_target_pairs={{0,12},{4,16},{8,28},{12,0},{16,4},{20,24},{24,20},{28,8},{1,13},{... | collective-permute-start | bytes 786440 | tf_op jit(solution)/shard_map/ppermute | solution.py:33
  3.8 3.8 %collective-permute-start = (bf16[1,2,32,64]{3,2,1,0:T(8,128)(2,1)S(1)}, bf16[1,2,32,64]{3,2,1,0:T(8,128)(2,1)S(1)}, u32[]{:S(2)}, u32[]{:S(2)}) collective-permute-start(bf16[1,2,32,64]{3,2,1,0:T(8,128)(2,1)S(1)} %maximum_bitcast_fusion), channel_id=1, source_target_pairs={{0,1},{1,0},{2,3},{3,2},{4,5},{5,4},{6,7},{7,6},{8,9},{9,8},{10,11... | collective-permute-start | bytes 24584 | tf_op jit(solution)/shard_map/ppermute | solution.py:191
  5.4 7.6 %collective-permute-start.2 = (bf16[1024,128]{1,0:T(8,128)(2,1)}, bf16[1024,128]{1,0:T(8,128)(2,1)S(1)}, u32[]{:S(2)}, u32[]{:S(2)}) collective-permute-start(bf16[1024,128]{1,0:T(8,128)(2,1)} %bitcast.8), channel_id=1, source_target_pairs={{0,4},{4,0},{8,12},{12,8},{16,20},{20,16},{24,28},{28,24},{1,5},{5... | collective-permute-start | bytes 786440 | tf_op jit(solution)/shard_map/ppermute | solution.py:33
  5.8 7.3 %collective-permute-start.6 = (bf16[1024,128]{1,0:T(8,128)(2,1)}, bf16[1024,128]{1,0:T(8,128)(2,1)S(1)}, u32[]{:S(2)}, u32[]{:S(2)}) collective-permute-start(bf16[1024,128]{1,0:T(8,128)(2,1)} %bitcast.9), channel_id=1, source_target_pairs={{0,20},{4,8},{8,4},{12,24},{16,28},{20,0},{24,12},{28,16},{1,21},{... | collective-permute-start | bytes 786440 | tf_op jit(solution)/shard_map/ppermute | solution.py:33
  7.6 7.1 %collective-permute-start.4 = (bf16[1024,128]{1,0:T(8,128)(2,1)S(1)}, bf16[1024,128]{1,0:T(8,128)(2,1)S(1)}, u32[]{:S(2)}, u32[]{:S(2)}) collective-permute-start(bf16[1024,128]{1,0:T(8,128)(2,1)S(1)} %collective-permute-done.3.first), channel_id=1, source_target_pairs={{0,20},{4,8},{8,4},{12,24},{16,28},{20,0},{24,12},{28,16},{1,21},{... | collective-permute-start | bytes 786440 | tf_op jit(solution)/shard_map/ppermute | solution.py:33
  9.4 4.8 %collective-permute-start.1 = (bf16[2,2,32,64]{3,2,1,0:T(8,128)(2,1)S(1)}, bf16[2,2,32,64]{3,2,1,0:T(8,128)(2,1)S(1)}, u32[]{:S(2)}, u32[]{:S(2)}) collective-permute-start(bf16[2,2,32,64]{3,2,1,0:T(8,128)(2,1)S(1)} %pad_maximum_fusion.1), channel_id=1, source_target_pairs={{0,2},{1,3},{2,0},{3,1},{4,6},{5,7},{6,4},{7,5},{8,10},{9,11},{10,... | collective-permute-start | bytes 49160 | tf_op jit(solution)/shard_map/ppermute | solution.py:191
  12.0 0.9 %copy-start = (bf16[64,16,128]{2,1,0:T(8,128)(2,1)S(1)}, bf16[64,16,128]{2,1,0:T(8,128)(2,1)}, u32[]{:S(2)}) copy-start(bf16[64,16,128]{2,1,0:T(8,128)(2,1)} %param.3) | copy-start | bytes 786436
  13.1 1.7 %collective-permute-start.5 = (bf16[1024,128]{1,0:T(8,128)(2,1)S(1)}, bf16[1024,128]{1,0:T(8,128)(2,1)S(1)}, u32[]{:S(2)}, u32[]{:S(2)}) collective-permute-start(bf16[1024,128]{1,0:T(8,128)(2,1)S(1)} %collective-permute-done.3.first), channel_id=1, source_target_pairs={{0,4},{4,0},{8,12},{12,8},{16,20},{20,16},{24,28},{28,24},{1,5},{5... | collective-permute-start | bytes 786440 | tf_op jit(solution)/shard_map/ppermute | solution.py:33
  13.2 1.8 %collective-permute-start.7 = (bf16[1024,128]{1,0:T(8,128)(2,1)S(1)}, bf16[1024,128]{1,0:T(8,128)(2,1)S(1)}, u32[]{:S(2)}, u32[]{:S(2)}) collective-permute-start(bf16[1024,128]{1,0:T(8,128)(2,1)S(1)} %collective-permute-done.6.first), channel_id=1, source_target_pairs={{0,4},{4,0},{8,12},{12,8},{16,20},{20,16},{24,28},{28,24},{1,5},{5... | collective-permute-start | bytes 786440 | tf_op jit(solution)/shard_map/ppermute | solution.py:33
  14.7 1.5 %collective-permute-start.8 = (bf16[1024,128]{1,0:T(8,128)(2,1)S(1)}, bf16[1024,128]{1,0:T(8,128)(2,1)S(1)}, u32[]{:S(2)}, u32[]{:S(2)}) collective-permute-start(bf16[1024,128]{1,0:T(8,128)(2,1)S(1)} %collective-permute-done.4.second), channel_id=1, source_target_pairs={{0,4},{4,0},{8,12},{12,8},{16,20},{20,16},{24,28},{28,24},{1,5},{5... | collective-permute-start | bytes 786440 | tf_op jit(solution)/shard_map/ppermute | solution.py:33

commit v9 on v8

--- a/solution.py
+++ b/solution.py
@@ -9,6 +9,7 @@
 
 PARAMS = pltpu.CompilerParams(vmem_limit_bytes=48 * 1024 * 1024)
 CHUNK = 16
+GROUP = 8
 
 
 class Block:
@@ -125,16 +126,26 @@
 def finish_kernel(planes, matrices, lines, second, sums, *outs):
     depth = second.shape[1]
     modes = matrices.shape[1]
-    here = lines[...]
-    there = lines_of(second, planes, True)
-    for parity, parts in enumerate((here + there, here - there)):
-        result = sums[parity] + jnp.dot(
-            matrices[parity], parts, preferred_element_type=jnp.float32
-        )
-        for y in range(planes):
-            outs[parity][pl.ds(y, modes, stride=planes), :] = result[
-                :, y * depth : (y + 1) * depth
-            ]
+    rows = second.shape[0] // planes
+    there = jnp.swapaxes(
+        jnp.stack(
+            [second[pl.ds(i * planes, planes), :] for i in reversed(range(rows))]
+        ),
+        0,
+        1,
+    )
+    for start in range(0, planes, GROUP):
+        columns = pl.ds(start * depth, GROUP * depth)
+        here = lines[:, columns]
+        other = jnp.concatenate([there[y] for y in range(start, start + GROUP)], axis=1)
+        for parity, parts in enumerate((here + other, here - other)):
+            result = sums[parity, :, columns] + jnp.dot(
+                matrices[parity], parts, preferred_element_type=jnp.float32
+            )
+            for y in range(GROUP):
+                outs[parity][pl.ds(start + y, modes, stride=planes), :] = result[
+                    :, y * depth : (y + 1) * depth
+                ]
 
 
 def finish(matrices, lines, second, sums, planes):

time: 17.5 us -> 17.6 us (level)
  no operation moved by 1% of the time
where the time goes in v9:
time: 17.6 us; the launch traced here: 17.3 us
  starting transfers between devices  10.7 us (61%)
  Pallas kernels  2.23 us (13%)
  waiting for transfers between devices  2.02 us (11%)
  local copies, waits for them, and re-layouts  0.95 us (5%)
  other arithmetic  0.75 us (4%)
  between operations  0.67 us (4%)
    ppermute x7, starting transfers between devices, send(): return Block(lax.ppermute(block.value, 'gx', pairs), *offsets)  6.44 us
    ppermute x2, starting transfers between devices, widen(): return jnp.concatenate((vectors, lax.ppermute(vectors, 'gz', pairs)))  4.23 us
    ppermute x2, waiting for transfers between devices, widen(): return jnp.concatenate((vectors, lax.ppermute(vectors, 'gz', pairs)))  1.23 us
    pallas_call x1, Pallas kernels, finish(): pl.pallas_call(functools.partial(finish_kernel, planes), out_shape=(shape...  1.09 us
    unnamed x2, local copies, waits for them, and re-layouts  0.95 us
    ppermute x7, waiting for transfers between devices, send(): return Block(lax.ppermute(block.value, 'gx', pairs), *offsets)  0.8 us
    broadcast_in_dim x1, other arithmetic, local(): vectors = jnp.stack((even_vectors, odd_vectors))[None]  0.72 us
    pallas_call x1, Pallas kernels, combine(): pl.pallas_call(functools.partial(combine_kernel, [functools.partial(block...  0.63 us
  transfers between devices with their start and end apart: 9, of which 4 were waited for; matrix products, arithmetic and copies ran while one was open for 4% of the time, Pallas kernels for 7%

profile of v9, /device:TPU:0, one launch (start us, length us, event | category | flops | bytes accessed | tf_op | source)
XLA Modules:
  0.0 17.3 jit_solution(3947368611995589920)
XLA Ops:
  0.6 2.4 %collective-permute-start.3 = (bf16[1024,128]{1,0:T(8,128)(2,1)}, bf16[1024,128]{1,0:T(8,128)(2,1)S(1)}, u32[]{:S(2)}, u32[]{:S(2)}) collective-permute-start(bf16[1024,128]{1,0:T(8,128)(2,1)} %bitcast.7), channel_id=1, source_target_pairs={{0,12},{4,16},{8,28},{12,0},{16,4},{20,24},{24,20},{28,8},{1,13},{... | collective-permute-start | bytes 786440 | tf_op jit(solution)/shard_map/ppermute | solution.py:34
  3.1 0.7 %maximum_bitcast_fusion = bf16[1,2,32,64]{3,2,1,0:T(8,128)(2,1)S(1)} fusion(bf16[1,32,64]{2,1,0:T(8,128)(2,1)} %bitcast.11, bf16[1,32,64]{2,1,0:T(8,128)(2,1)} %bitcast.12), kind=kLoop, calls=%fused_computation.2 | loop fusion | flops 4096 | bytes 16384 | tf_op jit(solution)/shard_map/broadcast_in_dim | solution.py:208
  3.8 1.6 %collective-permute-start = (bf16[1,2,32,64]{3,2,1,0:T(8,128)(2,1)S(1)}, bf16[1,2,32,64]{3,2,1,0:T(8,128)(2,1)S(1)}, u32[]{:S(2)}, u32[]{:S(2)}) collective-permute-start(bf16[1,2,32,64]{3,2,1,0:T(8,128)(2,1)S(1)} %maximum_bitcast_fusion), channel_id=1, source_target_pairs={{0,1},{1,0},{2,3},{3,2},{4,5},{5,4},{6,7},{7,6},{8,9},{9,8},{10,11... | collective-permute-start | bytes 24584 | tf_op jit(solution)/shard_map/ppermute | solution.py:202
  5.4 0.4 %collective-permute-start.2 = (bf16[1024,128]{1,0:T(8,128)(2,1)}, bf16[1024,128]{1,0:T(8,128)(2,1)S(1)}, u32[]{:S(2)}, u32[]{:S(2)}) collective-permute-start(bf16[1024,128]{1,0:T(8,128)(2,1)} %bitcast.8), channel_id=1, source_target_pairs={{0,4},{4,0},{8,12},{12,8},{16,20},{20,16},{24,28},{28,24},{1,5},{5... | collective-permute-start | bytes 786440 | tf_op jit(solution)/shard_map/ppermute | solution.py:34
  5.8 1.1 %collective-permute-start.6 = (bf16[1024,128]{1,0:T(8,128)(2,1)}, bf16[1024,128]{1,0:T(8,128)(2,1)S(1)}, u32[]{:S(2)}, u32[]{:S(2)}) collective-permute-start(bf16[1024,128]{1,0:T(8,128)(2,1)} %bitcast.9), channel_id=1, source_target_pairs={{0,20},{4,8},{8,4},{12,24},{16,28},{20,0},{24,12},{28,16},{1,21},{... | collective-permute-start | bytes 786440 | tf_op jit(solution)/shard_map/ppermute | solution.py:34
  6.9 0.6 %collective-permute-done = bf16[1,2,32,64]{3,2,1,0:T(8,128)(2,1)S(1)} collective-permute-done((bf16[1,2,32,64]{3,2,1,0:T(8,128)(2,1)S(1)}, bf16[1,2,32,64]{3,2,1,0:T(8,128)(2,1)S(1)}, u32[]{:S(2)}, u32[]{:S(2)}) %collective-permute-start) | collective-permute-done | bytes 8224 | tf_op jit(solution)/shard_map/ppermute | solution.py:202
  7.6 0.0 collective-permute-done.3.first
  7.6 1.8 %collective-permute-start.4 = (bf16[1024,128]{1,0:T(8,128)(2,1)S(1)}, bf16[1024,128]{1,0:T(8,128)(2,1)S(1)}, u32[]{:S(2)}, u32[]{:S(2)}) collective-permute-start(bf16[1024,128]{1,0:T(8,128)(2,1)S(1)} %collective-permute-done.3.first), channel_id=1, source_target_pairs={{0,20},{4,8},{8,4},{12,24},{16,28},{20,0},{24,12},{28,16},{1,21},{... | collective-permute-start | bytes 786440 | tf_op jit(solution)/shard_map/ppermute | solution.py:34
  9.4 2.6 %collective-permute-start.1 = (bf16[2,2,32,64]{3,2,1,0:T(8,128)(2,1)S(1)}, bf16[2,2,32,64]{3,2,1,0:T(8,128)(2,1)S(1)}, u32[]{:S(2)}, u32[]{:S(2)}) collective-permute-start(bf16[2,2,32,64]{3,2,1,0:T(8,128)(2,1)S(1)} %pad_maximum_fusion.1), channel_id=1, source_target_pairs={{0,2},{1,3},{2,0},{3,1},{4,6},{5,7},{6,4},{7,5},{8,10},{9,11},{10,... | collective-permute-start | bytes 49160 | tf_op jit(solution)/shard_map/ppermute | solution.py:202
  12.0 0.0 copy-start
  12.0 0.9 %copy-done = bf16[64,16,128]{2,1,0:T(8,128)(2,1)S(1)} copy-done((bf16[64,16,128]{2,1,0:T(8,128)(2,1)S(1)}, bf16[64,16,128]{2,1,0:T(8,128)(2,1)}, u32[]{:S(2)}) %copy-start) | copy-done | bytes 262168
  12.9 0.1 bring.1.lines
  13.0 0.0 collective-permute-done.2.first
  13.1 0.1 collective-permute-start.5
  13.2 0.0 collective-permute-done.6.first
  13.2 0.4 %collective-permute-start.7 = (bf16[1024,128]{1,0:T(8,128)(2,1)S(1)}, bf16[1024,128]{1,0:T(8,128)(2,1)S(1)}, u32[]{:S(2)}, u32[]{:S(2)}) collective-permute-start(bf16[1024,128]{1,0:T(8,128)(2,1)S(1)} %collective-permute-done.6.first), channel_id=1, source_target_pairs={{0,4},{4,0},{8,12},{12,8},{16,20},{20,16},{24,28},{28,24},{1,5},{5... | collective-permute-start | bytes 786440 | tf_op jit(solution)/shard_map/ppermute | solution.py:34
  13.6 0.6 %collective-permute-done.1 = bf16[2,2,32,64]{3,2,1,0:T(8,128)(2,1)S(1)} collective-permute-done((bf16[2,2,32,64]{3,2,1,0:T(8,128)(2,1)S(1)}, bf16[2,2,32,64]{3,2,1,0:T(8,128)(2,1)S(1)}, u32[]{:S(2)}, u32[]{:S(2)}) %collective-permute-start.1) | collective-permute-done | bytes 16416 | tf_op jit(solution)/shard_map/ppermute | solution.py:202
  14.2 0.4 %collective-permute-done.4.second = bf16[1024,128]{1,0:T(8,128)(2,1)S(1)} collective-permute-done((bf16[1024,128]{1,0:T(8,128)(2,1)S(1)}, bf16[1024,128]{1,0:T(8,128)(2,1)S(1)}, u32[]{:S(2)}, u32[]{:S(2)}) %collective-permute-start.4) | collective-permute-done | bytes 262176 | tf_op jit(solution)/shard_map/ppermute | solution.py:34
  14.7 0.1 collective-permute-start.8
  14.8 0.0 collective-permute-done.5.second
  14.8 0.2 %prepare.2 = (bf16[64,2048]{1,0:T(8,128)(2,1)S(1)}, bf16[64,2048]{1,0:T(8,128)(2,1)S(1)}) custom-call(bf16[1024,128]{1,0:T(8,128)(2,1)S(1)} %collective-permute-done.3.first, bf16[1024,128]{1,0:T(8,128)(2,1)S(1)} %collective-permute-done.5.second), custom_call_target="tpu_custom_call" | custom-call | tf_op jit(solution)/shard_map/prepare/pallas_call | solution.py:76
  15.0 0.0 collective-permute-done.7.second
  15.0 0.2 %prepare.3 = (bf16[64,2048]{1,0:T(8,128)(2,1)S(1)}, bf16[64,2048]{1,0:T(8,128)(2,1)S(1)}) custom-call(bf16[1024,128]{1,0:T(8,128)(2,1)S(1)} %collective-permute-done.6.first, bf16[1024,128]{1,0:T(8,128)(2,1)S(1)} %collective-permute-done.7.second), custom_call_target="tpu_custom_call" | custom-call | tf_op jit(solution)/shard_map/prepare/pallas_call | solution.py:76
  15.2 0.6 %combine.1 = (f32[2,32,2048]{2,1,0:T(8,128)S(1)}, bf16[2,32,64]{2,1,0:T(8,128)(2,1)S(1)}) custom-call(bf16[4,2,32,64]{3,2,1,0:T(8,128)(2,1)S(1)} %pad_maximum_fusion.vectors, bf16[1024,128]{1,0:T(8,128)(2,1)S(1)} %collective-permute-done.2.first, bf16[1024,128]{1,0:T(8,128)(2,1)S(1)} %collective-permute-done.4.second, ...), custom_call_target="tpu_custom_call" | custom-call | tf_op jit(solution)/shard_map/combine/pallas_call | solution.py:108
  15.9 0.3 %collective-permute-done.8.second = bf16[1024,128]{1,0:T(8,128)(2,1)S(1)} collective-permute-done((bf16[1024,128]{1,0:T(8,128)(2,1)S(1)}, bf16[1024,128]{1,0:T(8,128)(2,1)S(1)}, u32[]{:S(2)}, u32[]{:S(2)}) %collective-permute-start.8) | collective-permute-done | bytes 262176 | tf_op jit(solution)/shard_map/ppermute | solution.py:34
  16.2 1.1 %finish.1 = (f32[512,128]{1,0:T(8,128)}, f32[512,128]{1,0:T(8,128)}) custom-call(bf16[2,32,64]{2,1,0:T(8,128)(2,1)S(1)} %get-tuple-element.21.matrices, bf16[64,2048]{1,0:T(8,128)(2,1)S(1)} %bring.1.lines, bf16[1024,128]{1,0:T(8,128)(2,1)S(1)} %collective-permute-done.8.second, f32[2,32,2048]{2,1,0:T(8,128)S(1)} %get-tuple-element.23.sums), custom_call_target="tpu_custom_call" | custom-call | tf_op jit(solution)/shard_map/finish/pallas_call | solution.py:156
  (2 shorter events, 0.0 us)
Async XLA Ops:
  0.6 7.0 %collective-permute-start.3 = (bf16[1024,128]{1,0:T(8,128)(2,1)}, bf16[1024,128]{1,0:T(8,128)(2,1)S(1)}, u32[]{:S(2)}, u32[]{:S(2)}) collective-permute-start(bf16[1024,128]{1,0:T(8,128)(2,1)} %bitcast.7), channel_id=1, source_target_pairs={{0,12},{4,16},{8,28},{12,0},{16,4},{20,24},{24,20},{28,8},{1,13},{... | collective-permute-start | bytes 786440 | tf_op jit(solution)/shard_map/ppermute | solution.py:34
  3.8 3.8 %collective-permute-start = (bf16[1,2,32,64]{3,2,1,0:T(8,128)(2,1)S(1)}, bf16[1,2,32,64]{3,2,1,0:T(8,128)(2,1)S(1)}, u32[]{:S(2)}, u32[]{:S(2)}) collective-permute-start(bf16[1,2,32,64]{3,2,1,0:T(8,128)(2,1)S(1)} %maximum_bitcast_fusion), channel_id=1, source_target_pairs={{0,1},{1,0},{2,3},{3,2},{4,5},{5,4},{6,7},{7,6},{8,9},{9,8},{10,11... | collective-permute-start | bytes 24584 | tf_op jit(solution)/shard_map/ppermute | solution.py:202
  5.4 7.6 %collective-permute-start.2 = (bf16[1024,128]{1,0:T(8,128)(2,1)}, bf16[1024,128]{1,0:T(8,128)(2,1)S(1)}, u32[]{:S(2)}, u32[]{:S(2)}) collective-permute-start(bf16[1024,128]{1,0:T(8,128)(2,1)} %bitcast.8), channel_id=1, source_target_pairs={{0,4},{4,0},{8,12},{12,8},{16,20},{20,16},{24,28},{28,24},{1,5},{5... | collective-permute-start | bytes 786440 | tf_op jit(solution)/shard_map/ppermute | solution.py:34
  5.8 7.3 %collective-permute-start.6 = (bf16[1024,128]{1,0:T(8,128)(2,1)}, bf16[1024,128]{1,0:T(8,128)(2,1)S(1)}, u32[]{:S(2)}, u32[]{:S(2)}) collective-permute-start(bf16[1024,128]{1,0:T(8,128)(2,1)} %bitcast.9), channel_id=1, source_target_pairs={{0,20},{4,8},{8,4},{12,24},{16,28},{20,0},{24,12},{28,16},{1,21},{... | collective-permute-start | bytes 786440 | tf_op jit(solution)/shard_map/ppermute | solution.py:34
  7.6 7.1 %collective-permute-start.4 = (bf16[1024,128]{1,0:T(8,128)(2,1)S(1)}, bf16[1024,128]{1,0:T(8,128)(2,1)S(1)}, u32[]{:S(2)}, u32[]{:S(2)}) collective-permute-start(bf16[1024,128]{1,0:T(8,128)(2,1)S(1)} %collective-permute-done.3.first), channel_id=1, source_target_pairs={{0,20},{4,8},{8,4},{12,24},{16,28},{20,0},{24,12},{28,16},{1,21},{... | collective-permute-start | bytes 786440 | tf_op jit(solution)/shard_map/ppermute | solution.py:34
  9.4 4.8 %collective-permute-start.1 = (bf16[2,2,32,64]{3,2,1,0:T(8,128)(2,1)S(1)}, bf16[2,2,32,64]{3,2,1,0:T(8,128)(2,1)S(1)}, u32[]{:S(2)}, u32[]{:S(2)}) collective-permute-start(bf16[2,2,32,64]{3,2,1,0:T(8,128)(2,1)S(1)} %pad_maximum_fusion.1), channel_id=1, source_target_pairs={{0,2},{1,3},{2,0},{3,1},{4,6},{5,7},{6,4},{7,5},{8,10},{9,11},{10,... | collective-permute-start | bytes 49160 | tf_op jit(solution)/shard_map/ppermute | solution.py:202
  12.0 0.9 %copy-start = (bf16[64,16,128]{2,1,0:T(8,128)(2,1)S(1)}, bf16[64,16,128]{2,1,0:T(8,128)(2,1)}, u32[]{:S(2)}) copy-start(bf16[64,16,128]{2,1,0:T(8,128)(2,1)} %param.3) | copy-start | bytes 786436
  13.1 1.7 %collective-permute-start.5 = (bf16[1024,128]{1,0:T(8,128)(2,1)S(1)}, bf16[1024,128]{1,0:T(8,128)(2,1)S(1)}, u32[]{:S(2)}, u32[]{:S(2)}) collective-permute-start(bf16[1024,128]{1,0:T(8,128)(2,1)S(1)} %collective-permute-done.3.first), channel_id=1, source_target_pairs={{0,4},{4,0},{8,12},{12,8},{16,20},{20,16},{24,28},{28,24},{1,5},{5... | collective-permute-start | bytes 786440 | tf_op jit(solution)/shard_map/ppermute | solution.py:34
  13.2 1.8 %collective-permute-start.7 = (bf16[1024,128]{1,0:T(8,128)(2,1)S(1)}, bf16[1024,128]{1,0:T(8,128)(2,1)S(1)}, u32[]{:S(2)}, u32[]{:S(2)}) collective-permute-start(bf16[1024,128]{1,0:T(8,128)(2,1)S(1)} %collective-permute-done.6.first), channel_id=1, source_target_pairs={{0,4},{4,0},{8,12},{12,8},{16,20},{20,16},{24,28},{28,24},{1,5},{5... | collective-permute-start | bytes 786440 | tf_op jit(solution)/shard_map/ppermute | solution.py:34
  14.7 1.5 %collective-permute-start.8 = (bf16[1024,128]{1,0:T(8,128)(2,1)S(1)}, bf16[1024,128]{1,0:T(8,128)(2,1)S(1)}, u32[]{:S(2)}, u32[]{:S(2)}) collective-permute-start(bf16[1024,128]{1,0:T(8,128)(2,1)S(1)} %collective-permute-done.4.second), channel_id=1, source_target_pairs={{0,4},{4,0},{8,12},{12,8},{16,20},{20,16},{24,28},{28,24},{1,5},{5... | collective-permute-start | bytes 786440 | tf_op jit(solution)/shard_map/ppermute | solution.py:34

commit v10 on v8

--- a/solution.py
+++ b/solution.py
@@ -8,7 +8,7 @@
 from jax.sharding import PartitionSpec as P
 
 PARAMS = pltpu.CompilerParams(vmem_limit_bytes=48 * 1024 * 1024)
-CHUNK = 16
+CHUNK = 32
 
 
 class Block:

time: 17.5 us -> 17.5 us (level)
  no operation moved by 1% of the time
where the time goes in v10:
time: 17.5 us; the launch traced here: 17.3 us
  starting transfers between devices  10.7 us (61%)
  Pallas kernels  2.22 us (13%)
  waiting for transfers between devices  2.02 us (12%)
  local copies, waits for them, and re-layouts  0.95 us (5%)
  other arithmetic  0.75 us (4%)
  between operations  0.67 us (4%)
    ppermute x7, starting transfers between devices, send(): return Block(lax.ppermute(block.value, 'gx', pairs), *offsets)  6.44 us
    ppermute x2, starting transfers between devices, widen(): return jnp.concatenate((vectors, lax.ppermute(vectors, 'gz', pairs)))  4.23 us
    ppermute x2, waiting for transfers between devices, widen(): return jnp.concatenate((vectors, lax.ppermute(vectors, 'gz', pairs)))  1.23 us
    pallas_call x1, Pallas kernels, finish(): pl.pallas_call(functools.partial(finish_kernel, planes), out_shape=(shape...  1.08 us
    unnamed x2, local copies, waits for them, and re-layouts  0.95 us
    ppermute x7, waiting for transfers between devices, send(): return Block(lax.ppermute(block.value, 'gx', pairs), *offsets)  0.79 us
    broadcast_in_dim x1, other arithmetic, local(): vectors = jnp.stack((even_vectors, odd_vectors))[None]  0.72 us
    pallas_call x1, Pallas kernels, combine(): pl.pallas_call(functools.partial(combine_kernel, [functools.partial(block...  0.63 us
  transfers between devices with their start and end apart: 9, of which 4 were waited for; matrix products, arithmetic and copies ran while one was open for 4% of the time, Pallas kernels for 7%

profile of v10, /device:TPU:0, one launch (start us, length us, event | category | flops | bytes accessed | tf_op | source)
XLA Modules:
  0.0 17.3 jit_solution(962971770876081721)
XLA Ops:
  0.6 2.4 %collective-permute-start.3 = (bf16[1024,128]{1,0:T(8,128)(2,1)}, bf16[1024,128]{1,0:T(8,128)(2,1)S(1)}, u32[]{:S(2)}, u32[]{:S(2)}) collective-permute-start(bf16[1024,128]{1,0:T(8,128)(2,1)} %bitcast.7), channel_id=1, source_target_pairs={{0,12},{4,16},{8,28},{12,0},{16,4},{20,24},{24,20},{28,8},{1,13},{... | collective-permute-start | bytes 786440 | tf_op jit(solution)/shard_map/ppermute | solution.py:33
  3.1 0.7 %maximum_bitcast_fusion = bf16[1,2,32,64]{3,2,1,0:T(8,128)(2,1)S(1)} fusion(bf16[1,32,64]{2,1,0:T(8,128)(2,1)} %bitcast.11, bf16[1,32,64]{2,1,0:T(8,128)(2,1)} %bitcast.12), kind=kLoop, calls=%fused_computation.2 | loop fusion | flops 4096 | bytes 16384 | tf_op jit(solution)/shard_map/broadcast_in_dim | solution.py:197
  3.8 1.6 %collective-permute-start = (bf16[1,2,32,64]{3,2,1,0:T(8,128)(2,1)S(1)}, bf16[1,2,32,64]{3,2,1,0:T(8,128)(2,1)S(1)}, u32[]{:S(2)}, u32[]{:S(2)}) collective-permute-start(bf16[1,2,32,64]{3,2,1,0:T(8,128)(2,1)S(1)} %maximum_bitcast_fusion), channel_id=1, source_target_pairs={{0,1},{1,0},{2,3},{3,2},{4,5},{5,4},{6,7},{7,6},{8,9},{9,8},{10,11... | collective-permute-start | bytes 24584 | tf_op jit(solution)/shard_map/ppermute | solution.py:191
  5.4 0.4 %collective-permute-start.2 = (bf16[1024,128]{1,0:T(8,128)(2,1)}, bf16[1024,128]{1,0:T(8,128)(2,1)S(1)}, u32[]{:S(2)}, u32[]{:S(2)}) collective-permute-start(bf16[1024,128]{1,0:T(8,128)(2,1)} %bitcast.8), channel_id=1, source_target_pairs={{0,4},{4,0},{8,12},{12,8},{16,20},{20,16},{24,28},{28,24},{1,5},{5... | collective-permute-start | bytes 786440 | tf_op jit(solution)/shard_map/ppermute | solution.py:33
  5.8 1.1 %collective-permute-start.6 = (bf16[1024,128]{1,0:T(8,128)(2,1)}, bf16[1024,128]{1,0:T(8,128)(2,1)S(1)}, u32[]{:S(2)}, u32[]{:S(2)}) collective-permute-start(bf16[1024,128]{1,0:T(8,128)(2,1)} %bitcast.9), channel_id=1, source_target_pairs={{0,20},{4,8},{8,4},{12,24},{16,28},{20,0},{24,12},{28,16},{1,21},{... | collective-permute-start | bytes 786440 | tf_op jit(solution)/shard_map/ppermute | solution.py:33
  6.9 0.6 %collective-permute-done = bf16[1,2,32,64]{3,2,1,0:T(8,128)(2,1)S(1)} collective-permute-done((bf16[1,2,32,64]{3,2,1,0:T(8,128)(2,1)S(1)}, bf16[1,2,32,64]{3,2,1,0:T(8,128)(2,1)S(1)}, u32[]{:S(2)}, u32[]{:S(2)}) %collective-permute-start) | collective-permute-done | bytes 8224 | tf_op jit(solution)/shard_map/ppermute | solution.py:191
  7.6 0.0 collective-permute-done.3.first
  7.6 1.8 %collective-permute-start.4 = (bf16[1024,128]{1,0:T(8,128)(2,1)S(1)}, bf16[1024,128]{1,0:T(8,128)(2,1)S(1)}, u32[]{:S(2)}, u32[]{:S(2)}) collective-permute-start(bf16[1024,128]{1,0:T(8,128)(2,1)S(1)} %collective-permute-done.3.first), channel_id=1, source_target_pairs={{0,20},{4,8},{8,4},{12,24},{16,28},{20,0},{24,12},{28,16},{1,21},{... | collective-permute-start | bytes 786440 | tf_op jit(solution)/shard_map/ppermute | solution.py:33
  9.4 2.6 %collective-permute-start.1 = (bf16[2,2,32,64]{3,2,1,0:T(8,128)(2,1)S(1)}, bf16[2,2,32,64]{3,2,1,0:T(8,128)(2,1)S(1)}, u32[]{:S(2)}, u32[]{:S(2)}) collective-permute-start(bf16[2,2,32,64]{3,2,1,0:T(8,128)(2,1)S(1)} %pad_maximum_fusion.1), channel_id=1, source_target_pairs={{0,2},{1,3},{2,0},{3,1},{4,6},{5,7},{6,4},{7,5},{8,10},{9,11},{10,... | collective-permute-start | bytes 49160 | tf_op jit(solution)/shard_map/ppermute | solution.py:191
  12.0 0.0 copy-start
  12.0 0.9 %copy-done = bf16[64,16,128]{2,1,0:T(8,128)(2,1)S(1)} copy-done((bf16[64,16,128]{2,1,0:T(8,128)(2,1)S(1)}, bf16[64,16,128]{2,1,0:T(8,128)(2,1)}, u32[]{:S(2)}) %copy-start) | copy-done | bytes 262168
  12.9 0.1 bring.1.lines
  13.0 0.0 collective-permute-done.2.first
  13.1 0.1 collective-permute-start.5
  13.2 0.0 collective-permute-done.6.first
  13.2 0.4 %collective-permute-start.7 = (bf16[1024,128]{1,0:T(8,128)(2,1)S(1)}, bf16[1024,128]{1,0:T(8,128)(2,1)S(1)}, u32[]{:S(2)}, u32[]{:S(2)}) collective-permute-start(bf16[1024,128]{1,0:T(8,128)(2,1)S(1)} %collective-permute-done.6.first), channel_id=1, source_target_pairs={{0,4},{4,0},{8,12},{12,8},{16,20},{20,16},{24,28},{28,24},{1,5},{5... | collective-permute-start | bytes 786440 | tf_op jit(solution)/shard_map/ppermute | solution.py:33
  13.6 0.6 %collective-permute-done.1 = bf16[2,2,32,64]{3,2,1,0:T(8,128)(2,1)S(1)} collective-permute-done((bf16[2,2,32,64]{3,2,1,0:T(8,128)(2,1)S(1)}, bf16[2,2,32,64]{3,2,1,0:T(8,128)(2,1)S(1)}, u32[]{:S(2)}, u32[]{:S(2)}) %collective-permute-start.1) | collective-permute-done | bytes 16416 | tf_op jit(solution)/shard_map/ppermute | solution.py:191
  14.2 0.4 %collective-permute-done.4.second = bf16[1024,128]{1,0:T(8,128)(2,1)S(1)} collective-permute-done((bf16[1024,128]{1,0:T(8,128)(2,1)S(1)}, bf16[1024,128]{1,0:T(8,128)(2,1)S(1)}, u32[]{:S(2)}, u32[]{:S(2)}) %collective-permute-start.4) | collective-permute-done | bytes 262176 | tf_op jit(solution)/shard_map/ppermute | solution.py:33
  14.7 0.1 collective-permute-start.8
  14.8 0.0 collective-permute-done.5.second
  14.8 0.2 %prepare.2 = (bf16[64,2048]{1,0:T(8,128)(2,1)S(1)}, bf16[64,2048]{1,0:T(8,128)(2,1)S(1)}) custom-call(bf16[1024,128]{1,0:T(8,128)(2,1)S(1)} %collective-permute-done.3.first, bf16[1024,128]{1,0:T(8,128)(2,1)S(1)} %collective-permute-done.5.second), custom_call_target="tpu_custom_call" | custom-call | tf_op jit(solution)/shard_map/prepare/pallas_call | solution.py:75
  15.0 0.0 collective-permute-done.7.second
  15.0 0.2 %prepare.3 = (bf16[64,2048]{1,0:T(8,128)(2,1)S(1)}, bf16[64,2048]{1,0:T(8,128)(2,1)S(1)}) custom-call(bf16[1024,128]{1,0:T(8,128)(2,1)S(1)} %collective-permute-done.6.first, bf16[1024,128]{1,0:T(8,128)(2,1)S(1)} %collective-permute-done.7.second), custom_call_target="tpu_custom_call" | custom-call | tf_op jit(solution)/shard_map/prepare/pallas_call | solution.py:75
  15.2 0.6 %combine.1 = (f32[2,32,2048]{2,1,0:T(8,128)S(1)}, bf16[2,32,64]{2,1,0:T(8,128)(2,1)S(1)}) custom-call(bf16[4,2,32,64]{3,2,1,0:T(8,128)(2,1)S(1)} %pad_maximum_fusion.vectors, bf16[1024,128]{1,0:T(8,128)(2,1)S(1)} %collective-permute-done.2.first, bf16[1024,128]{1,0:T(8,128)(2,1)S(1)} %collective-permute-done.4.second, ...), custom_call_target="tpu_custom_call" | custom-call | tf_op jit(solution)/shard_map/combine/pallas_call | solution.py:107
  15.9 0.3 %collective-permute-done.8.second = bf16[1024,128]{1,0:T(8,128)(2,1)S(1)} collective-permute-done((bf16[1024,128]{1,0:T(8,128)(2,1)S(1)}, bf16[1024,128]{1,0:T(8,128)(2,1)S(1)}, u32[]{:S(2)}, u32[]{:S(2)}) %collective-permute-start.8) | collective-permute-done | bytes 262176 | tf_op jit(solution)/shard_map/ppermute | solution.py:33
  16.2 1.1 %finish.1 = (f32[512,128]{1,0:T(8,128)}, f32[512,128]{1,0:T(8,128)}) custom-call(bf16[2,32,64]{2,1,0:T(8,128)(2,1)S(1)} %get-tuple-element.21.matrices, bf16[64,2048]{1,0:T(8,128)(2,1)S(1)} %bring.1.lines, bf16[1024,128]{1,0:T(8,128)(2,1)S(1)} %collective-permute-done.8.second, f32[2,32,2048]{2,1,0:T(8,128)S(1)} %get-tuple-element.23.sums), custom_call_target="tpu_custom_call" | custom-call | tf_op jit(solution)/shard_map/finish/pallas_call | solution.py:145
  (2 shorter events, 0.0 us)
Async XLA Ops:
  0.6 7.0 %collective-permute-start.3 = (bf16[1024,128]{1,0:T(8,128)(2,1)}, bf16[1024,128]{1,0:T(8,128)(2,1)S(1)}, u32[]{:S(2)}, u32[]{:S(2)}) collective-permute-start(bf16[1024,128]{1,0:T(8,128)(2,1)} %bitcast.7), channel_id=1, source_target_pairs={{0,12},{4,16},{8,28},{12,0},{16,4},{20,24},{24,20},{28,8},{1,13},{... | collective-permute-start | bytes 786440 | tf_op jit(solution)/shard_map/ppermute | solution.py:33
  3.8 3.8 %collective-permute-start = (bf16[1,2,32,64]{3,2,1,0:T(8,128)(2,1)S(1)}, bf16[1,2,32,64]{3,2,1,0:T(8,128)(2,1)S(1)}, u32[]{:S(2)}, u32[]{:S(2)}) collective-permute-start(bf16[1,2,32,64]{3,2,1,0:T(8,128)(2,1)S(1)} %maximum_bitcast_fusion), channel_id=1, source_target_pairs={{0,1},{1,0},{2,3},{3,2},{4,5},{5,4},{6,7},{7,6},{8,9},{9,8},{10,11... | collective-permute-start | bytes 24584 | tf_op jit(solution)/shard_map/ppermute | solution.py:191
  5.4 7.6 %collective-permute-start.2 = (bf16[1024,128]{1,0:T(8,128)(2,1)}, bf16[1024,128]{1,0:T(8,128)(2,1)S(1)}, u32[]{:S(2)}, u32[]{:S(2)}) collective-permute-start(bf16[1024,128]{1,0:T(8,128)(2,1)} %bitcast.8), channel_id=1, source_target_pairs={{0,4},{4,0},{8,12},{12,8},{16,20},{20,16},{24,28},{28,24},{1,5},{5... | collective-permute-start | bytes 786440 | tf_op jit(solution)/shard_map/ppermute | solution.py:33
  5.8 7.3 %collective-permute-start.6 = (bf16[1024,128]{1,0:T(8,128)(2,1)}, bf16[1024,128]{1,0:T(8,128)(2,1)S(1)}, u32[]{:S(2)}, u32[]{:S(2)}) collective-permute-start(bf16[1024,128]{1,0:T(8,128)(2,1)} %bitcast.9), channel_id=1, source_target_pairs={{0,20},{4,8},{8,4},{12,24},{16,28},{20,0},{24,12},{28,16},{1,21},{... | collective-permute-start | bytes 786440 | tf_op jit(solution)/shard_map/ppermute | solution.py:33
  7.6 7.1 %collective-permute-start.4 = (bf16[1024,128]{1,0:T(8,128)(2,1)S(1)}, bf16[1024,128]{1,0:T(8,128)(2,1)S(1)}, u32[]{:S(2)}, u32[]{:S(2)}) collective-permute-start(bf16[1024,128]{1,0:T(8,128)(2,1)S(1)} %collective-permute-done.3.first), channel_id=1, source_target_pairs={{0,20},{4,8},{8,4},{12,24},{16,28},{20,0},{24,12},{28,16},{1,21},{... | collective-permute-start | bytes 786440 | tf_op jit(solution)/shard_map/ppermute | solution.py:33
  9.4 4.8 %collective-permute-start.1 = (bf16[2,2,32,64]{3,2,1,0:T(8,128)(2,1)S(1)}, bf16[2,2,32,64]{3,2,1,0:T(8,128)(2,1)S(1)}, u32[]{:S(2)}, u32[]{:S(2)}) collective-permute-start(bf16[2,2,32,64]{3,2,1,0:T(8,128)(2,1)S(1)} %pad_maximum_fusion.1), channel_id=1, source_target_pairs={{0,2},{1,3},{2,0},{3,1},{4,6},{5,7},{6,4},{7,5},{8,10},{9,11},{10,... | collective-permute-start | bytes 49160 | tf_op jit(solution)/shard_map/ppermute | solution.py:191
  12.0 0.9 %copy-start = (bf16[64,16,128]{2,1,0:T(8,128)(2,1)S(1)}, bf16[64,16,128]{2,1,0:T(8,128)(2,1)}, u32[]{:S(2)}) copy-start(bf16[64,16,128]{2,1,0:T(8,128)(2,1)} %param.3) | copy-start | bytes 786436
  13.1 1.7 %collective-permute-start.5 = (bf16[1024,128]{1,0:T(8,128)(2,1)S(1)}, bf16[1024,128]{1,0:T(8,128)(2,1)S(1)}, u32[]{:S(2)}, u32[]{:S(2)}) collective-permute-start(bf16[1024,128]{1,0:T(8,128)(2,1)S(1)} %collective-permute-done.3.first), channel_id=1, source_target_pairs={{0,4},{4,0},{8,12},{12,8},{16,20},{20,16},{24,28},{28,24},{1,5},{5... | collective-permute-start | bytes 786440 | tf_op jit(solution)/shard_map/ppermute | solution.py:33
  13.2 1.8 %collective-permute-start.7 = (bf16[1024,128]{1,0:T(8,128)(2,1)S(1)}, bf16[1024,128]{1,0:T(8,128)(2,1)S(1)}, u32[]{:S(2)}, u32[]{:S(2)}) collective-permute-start(bf16[1024,128]{1,0:T(8,128)(2,1)S(1)} %collective-permute-done.6.first), channel_id=1, source_target_pairs={{0,4},{4,0},{8,12},{12,8},{16,20},{20,16},{24,28},{28,24},{1,5},{5... | collective-permute-start | bytes 786440 | tf_op jit(solution)/shard_map/ppermute | solution.py:33
  14.7 1.5 %collective-permute-start.8 = (bf16[1024,128]{1,0:T(8,128)(2,1)S(1)}, bf16[1024,128]{1,0:T(8,128)(2,1)S(1)}, u32[]{:S(2)}, u32[]{:S(2)}) collective-permute-start(bf16[1024,128]{1,0:T(8,128)(2,1)S(1)} %collective-permute-done.4.second), channel_id=1, source_target_pairs={{0,4},{4,0},{8,12},{12,8},{16,20},{20,16},{24,28},{28,24},{1,5},{5... | collective-permute-start | bytes 786440 | tf_op jit(solution)/shard_map/ppermute | solution.py:33
